TPU v7x, 256 devices: a whole 4x4x8 slice. The times are simulated.
256 devices in a mesh: sec: 2 (over z_lo), gx: 8 (over x, core), row: 16 (over y, z_hi).
Axes of the slice: x: 4, y: 4, z: 8 (z_hi: 4, z_lo: 2; z = z_hi * 2 + z_lo), core: 2. Of those that a mesh axis runs over, the one named last changes fastest.
Arguments:
- les_density: float32 [128, 512, 256], P('gx', 'row', 'sec'), may hold values from 0.5 to 1.5
- les_rest: float32 [4, 128, 512, 256], P(None, 'gx', 'row', 'sec'), may hold values from -4 to 4
- acoustic: float32 [4, 64, 256, 256], P(None, 'gx', 'row', 'sec'), may hold values from -6 to 6
- block_owner: int32 [131072, 1], P(('sec', 'gx', 'row')), may hold values from 0 to 127; in each aligned block of 512 rows (0 to 511, 512 to 1023, ...) at most 10 rows name the same one
- block_weights: bfloat16 [131072, 64, 128], P(('sec', 'gx', 'row')), may hold values from -0.5 to 0.5
- block_counts: int32 [131072], P(('sec', 'gx', 'row')), may hold values from 32 to 128
- block_patch: int32 [131072], P(('sec', 'gx', 'row')), may hold values from 0 to 255
- tile_class: int32 [2, 8, 16], P('sec', 'gx', 'row'), may hold values from 0 to 3
- sample_index: int32 [32768], P(('sec', 'gx', 'row')), may hold values from 0 to 16383
- far_kernel: float32 [128, 32768], P(None, ('sec', 'gx', 'row')), may hold values from -0.03125 to 0.03125
Outputs:
- les_next: float32 [5, 128, 512, 256], P(None, 'gx', 'row', 'sec')
- acoustic_next: float32 [4, 64, 256, 256], P(None, 'gx', 'row', 'sec')
- far_field: float32 [128], replicated
Inputs may be any that keep to these rules, and one draw needn't show every extreme that they name: `block_owner`: the rows of one device name no owner more than 10 times; some device's rows name some owner exactly 10 times.
All inputs are finite; a program needn't handle non-finite values.
Results may differ from a plain program's by a relative error of at most 0.0015.
Values sent between devices are 32-bit elements; how exact they have to be, the bound alone decides.
No kernel may reach another device: no remote copies, remote signals or barrier semaphores. Data moves between devices by JAX's collectives and lax.ppermute only.
A program may use at most 64 MiB of HBM per device.

v0:
```python
import jax
import jax.numpy as jnp
from jax import lax
from jax.sharding import PartitionSpec as P

LES_STEP = 0.2
WAVE_STEP = 0.25


def padded_2(block, sides, width):
    for axis, dim in sides:
        count = lax.axis_size(axis)
        forward = [(i, i + 1) for i in range(count - 1)]
        backward = [(target, source) for source, target in forward]
        low = lax.ppermute(
            lax.slice_in_dim(block, block.shape[dim] - width, None, axis=dim), axis, forward
        )
        high = lax.ppermute(lax.slice_in_dim(block, 0, width, axis=dim), axis, backward)
        block = jnp.concatenate([low, block, high], axis=dim)
    return block


def shifted(padded, direction, offset):
    selector = [slice(None), slice(1, -1), slice(1, -1), slice(1, -1)]
    selector[direction] = slice(offset, offset + padded.shape[direction] - 2)
    return padded[tuple(selector)]


def derive(padded, direction):
    return 0.5 * (shifted(padded, direction, 2) - shifted(padded, direction, 0))


def les_update(padded):
    les_state = padded[:5]
    flux_sum = derive(les_state * padded[5:6], 1)
    flux_sum = flux_sum + derive(les_state * padded[6:7], 2)
    flux_sum = flux_sum + derive(les_state * padded[7:8], 3)
    return shifted(les_state, 1, 1) - LES_STEP * flux_sum


def lamb_vector(velocity_pad):
    gradients = [
        [derive(velocity_pad[component : component + 1], spatial)[0] for spatial in (1, 2, 3)]
        for component in range(3)
    ]
    speed = shifted(velocity_pad, 1, 1)
    swirl_x = gradients[2][1] - gradients[1][2]
    swirl_y = gradients[0][2] - gradients[2][0]
    swirl_z = gradients[1][0] - gradients[0][1]
    lamb_x = swirl_y * speed[2] - swirl_z * speed[1]
    lamb_y = swirl_z * speed[0] - swirl_x * speed[2]
    lamb_z = swirl_x * speed[1] - swirl_y * speed[0]
    return jnp.stack([lamb_x, lamb_y, lamb_z])


def wave_update(padded, mean_flow, stiffness, source):
    current = shifted(padded, 1, 1)
    along = [derive(padded[part : part + 1], 1)[0] for part in range(4)]
    pressure_grad = [along[0], derive(padded[0:1], 2)[0], derive(padded[0:1], 3)[0]]
    divergence = along[1] + derive(padded[2:3], 2)[0] + derive(padded[3:4], 3)[0]
    pressure = current[0] - WAVE_STEP * (mean_flow * along[0] + stiffness * divergence)
    layers = [pressure]
    for spatial in range(3):
        layers.append(
            current[1 + spatial]
            - WAVE_STEP
            * (mean_flow * along[1 + spatial] + pressure_grad[spatial] + source[spatial])
        )
    return jnp.stack(layers)


def per_device(
    les_density,
    les_rest,
    acoustic,
    block_owner,
    block_weights,
    block_counts,
    block_patch,
    tile_class,
    sample_index,
    far_kernel,
):
    velocity = les_rest[0:3] / les_density[None]
    stacked = jnp.concatenate([les_density[None], les_rest, velocity], axis=0)
    padded = padded_2(stacked, (("gx", 1), ("row", 2), ("sec", 3)), 1)
    lamb = lamb_vector(padded[5:8]).astype(jnp.bfloat16)
    block_count = block_weights.shape[0]
    patch_cells = block_weights.shape[1]
    cell_block = block_weights.shape[2]
    lamb_blocks = lamb.reshape(3, block_count, cell_block)
    valid_mask = (
        jnp.arange(cell_block, dtype=jnp.int32)[None, None, :] < block_counts[:, None, None]
    )
    masked = jnp.where(valid_mask, block_weights, jnp.zeros_like(block_weights))
    payload = jnp.einsum("ckb,kpb->kcp", lamb_blocks, masked, preferred_element_type=jnp.float32)
    payload = payload.reshape(block_count, 3 * patch_cells)
    tiles_x = lax.axis_size("gx")
    tiles_r = lax.axis_size("row")
    owners = tiles_x * tiles_r
    capacity = max(2, 5 * block_count // (2 * owners))
    owner_ids = block_owner[:, 0]
    onehot = (owner_ids[:, None] == jnp.arange(owners, dtype=jnp.int32)[None, :]).astype(jnp.int32)
    earlier = jnp.cumsum(onehot, axis=0) - onehot
    slot_index = jnp.sum(earlier * onehot, axis=1)
    position = owner_ids * capacity + slot_index
    send_values = (
        jnp.zeros((owners * capacity, 3 * patch_cells), jnp.float32).at[position].set(payload)
    )
    send_patch = (
        jnp.zeros((owners * capacity,), jnp.float32)
        .at[position]
        .set(block_patch.astype(jnp.float32))
    )
    arrived_values, arrived_patch = (
        lax.all_to_all(
            send_values.reshape(owners, capacity, 3 * patch_cells),
            ("gx", "row"),
            split_axis=0,
            concat_axis=0,
            tiled=True,
        ),
        lax.all_to_all(
            send_patch.reshape(owners, capacity),
            ("gx", "row"),
            split_axis=0,
            concat_axis=0,
            tiled=True,
        ),
    )
    les_next = les_update(padded)
    wave_pad = padded_2(acoustic, (("gx", 1), ("row", 2), ("sec", 3)), 1)
    arrived_values = arrived_values.reshape(owners * capacity, 3 * patch_cells)
    arrived_patch = arrived_patch.reshape(owners * capacity)
    wave_cells = acoustic.shape[1] * acoustic.shape[2] * acoustic.shape[3]
    patch_count = wave_cells // patch_cells
    selector = (
        jnp.arange(patch_count, dtype=jnp.float32)[:, None] == arrived_patch[None, :]
    ).astype(jnp.float32)
    collected = jnp.dot(selector, arrived_values, precision=lax.Precision.HIGHEST)
    source = collected.reshape(patch_count, 3, patch_cells).transpose(1, 0, 2)
    source = source.reshape(3, acoustic.shape[1], acoustic.shape[2], acoustic.shape[3])
    class_value = tile_class.reshape(()).astype(jnp.float32)
    mean_flow = 0.1 + 0.3 * class_value
    stiffness = 1.0 + 0.25 * class_value
    acoustic_next = wave_update(wave_pad, mean_flow, stiffness, source)
    pressure_flat = acoustic_next[0].reshape(wave_cells)
    samples = jnp.take(pressure_flat, sample_index)
    partial_far = jnp.dot(far_kernel, samples, precision=lax.Precision.HIGHEST)
    far_field = lax.psum(partial_far, ("sec", "gx", "row"))
    return (les_next, acoustic_next, far_field)


def solution(mesh):
    in_specs = (
        P("gx", "row", "sec"),
        P(None, "gx", "row", "sec"),
        P(None, "gx", "row", "sec"),
        P(("sec", "gx", "row"), None),
        P(("sec", "gx", "row"), None, None),
        P(("sec", "gx", "row")),
        P(("sec", "gx", "row")),
        P("sec", "gx", "row"),
        P(("sec", "gx", "row")),
        P(None, ("sec", "gx", "row")),
    )
    out_specs = (P(None, "gx", "row", "sec"), P(None, "gx", "row", "sec"), P())
    return jax.shard_map(
        per_device, mesh=mesh, in_specs=in_specs, out_specs=out_specs, check_vma=False
    )
```

profile of v0, /device:TPU:1, one launch (start us, length us, event | category | flops | bytes accessed | tf_op | source)
XLA Modules:
  0.0 241.5 jit_solution(17950973690188842155)
XLA Ops:
  3.1 4.5 %collective-permute-start = (f32[8,1,32,128]{3,2,1,0:T(8,128)S(1)}, f32[8,1,32,128]{3,2,1,0:T(8,128)S(1)}, u32[]{:S(2)}, u32[]{:S(2)}) collective-permute-start(f32[8,1,32,128]{3,2,1,0:T(8,128)S(1)} %get-tuple-element.20), channel_id=1, source_target_pairs={{0,16},{16,32},{32,48},{48,64},{64,80},{80,96},{96,112},{1,17},{17... | collective-permute-start | bytes 393224 | tf_op jit(solution)/shard_map/ppermute | solution.py:15
  10.3 2.5 %scatter_custom_fusion = f32[1280]{0:T(1024)S(1)} fusion(s32[512]{0:T(512)S(1)} %bitcast.69, f32[512]{0:T(512)S(1)} %convert_element_type.20, f32[]{:T(128)} %constant.47.clone.1), kind=kCustom, calls=%fused_computation.136 | custom fusion | bytes 5124 | tf_op jit(solution)/shard_map/scatter | solution.py:113
  13.5 15.5 %all-to-all-start = ((f32[128,1,10]{2,1,0:T(1,128)}), f32[128,1,10]{2,1,0:T(1,128)S(1)}, u32[]{:S(2)}, u32[]{:S(2)}) async-start(f32[128,1,10]{2,1,0:T(1,128)} %bitcast.13), calls=%async_computation | async-start | bytes 131072 | tf_op jit(solution)/shard_map/all_to_all | solution.py:123
  29.0 3.6 %collective-permute-start.7 = (f32[4,1,16,128]{3,2,1,0:T(8,128)S(1)}, f32[4,1,16,128]{3,2,1,0:T(8,128)S(1)}, u32[]{:S(2)}, u32[]{:S(2)}) collective-permute-start(f32[4,1,16,128]{3,2,1,0:T(8,128)S(1)} %get-tuple-element.32), channel_id=1, source_target_pairs={{0,16},{16,32},{32,48},{48,64},{64,80},{80,96},{96,112},{1,17},{17... | collective-permute-start | bytes 98312 | tf_op jit(solution)/shard_map/ppermute | solution.py:15
  35.5 2.7 %collective-permute-done.6 = f32[4,1,16,128]{3,2,1,0:T(8,128)S(1)} collective-permute-done((f32[4,1,16,128]{3,2,1,0:T(8,128)S(1)}, f32[4,1,16,128]{3,2,1,0:T(8,128)S(1)}, u32[]{:S(2)}, u32[]{:S(2)}) %collective-permute-start.6) | collective-permute-done | bytes 32800 | tf_op jit(solution)/shard_map/ppermute | solution.py:18
  40.3 4.9 %collective-permute-start.9 = (f32[4,10,1,128]{3,2,1,0:T(1,128)S(1)}, f32[4,10,1,128]{3,2,1,0:T(1,128)S(1)}, u32[]{:S(2)}, u32[]{:S(2)}) collective-permute-start(f32[4,10,1,128]{3,2,1,0:T(1,128)S(1)} %get-tuple-element.26), channel_id=1, source_target_pairs={{0,1},{1,2},{2,3},{3,4},{4,5},{5,6},{6,7},{7,8},{8,9},{9,10},{10,1... | collective-permute-start | bytes 61448 | tf_op jit(solution)/shard_map/ppermute | solution.py:15
  47.6 5.2 %collective-permute-start.2 = (f32[8,18,1,128]{3,2,1,0:T(1,128)S(1)}, f32[8,18,1,128]{3,2,1,0:T(1,128)S(1)}, u32[]{:S(2)}, u32[]{:S(2)}) collective-permute-start(f32[8,18,1,128]{3,2,1,0:T(1,128)S(1)} %get-tuple-element.18), channel_id=1, source_target_pairs={{0,1},{1,2},{2,3},{3,4},{4,5},{5,6},{6,7},{7,8},{8,9},{9,10},{10,1... | collective-permute-start | bytes 221192 | tf_op jit(solution)/shard_map/ppermute | solution.py:15
  56.5 4.8 %collective-permute-start.11 = (f32[4,10,18,1]{3,2,1,0:T(8,128)}, f32[4,10,18,1]{3,2,1,0:T(8,128)}, u32[]{:S(2)}, u32[]{:S(2)}) collective-permute-start(f32[4,10,18,1]{3,2,1,0:T(8,128)} %get-tuple-element.25), channel_id=1, source_target_pairs={{0,128},{1,129},{2,130},{3,131},{4,132},{5,133},{6,134},{7,135},{8... | collective-permute-start | bytes 8648 | tf_op jit(solution)/shard_map/ppermute | solution.py:15
  61.7 3.4 %fusion.72 = (f32[8,18,34,1]{3,2,1,0:T(8,128)}, f32[8,18,34,1]{3,2,1,0:T(8,128)}) fusion(f32[8,18,34,128]{3,2,1,0:T(8,128)S(1)} %pad_maximum_fusion.2), kind=kLoop, calls=%fused_computation.150 | loop fusion | bytes 78336 | tf_op jit(solution)/shard_map/slice | solution.py:16
  65.1 3.6 %copy.25 = f32[8,18,34,1]{2,0,3,1:T(8,128)} copy(f32[8,18,34,1]{3,2,1,0:T(8,128)} %get-tuple-element.14) | data formatting | bytes 39168 | tf_op jit(solution)/shard_map/slice | solution.py:16
  70.6 3.6 %copy.26 = f32[8,18,34,1]{2,0,3,1:T(8,128)} copy(f32[8,18,34,1]{3,2,1,0:T(8,128)} %get-tuple-element.15) | data formatting | bytes 39168 | tf_op jit(solution)/shard_map/slice | solution.py:18
  78.2 3.6 %copy.27 = f32[8,18,34,1]{3,2,1,0:T(8,128)} copy(f32[8,18,34,1]{2,0,3,1:T(8,128)} %collective-permute-done.4) | data formatting | bytes 39168 | tf_op jit(solution)/shard_map/ppermute | solution.py:15
  81.8 3.6 %copy.28 = f32[8,18,34,1]{3,2,1,0:T(8,128)} copy(f32[8,18,34,1]{2,0,3,1:T(8,128)} %collective-permute-done.5) | data formatting | bytes 39168 | tf_op jit(solution)/shard_map/ppermute | solution.py:18
  85.4 8.2 %pad_maximum_fusion.1 = (f32[8,18,34,129]{3,2,1,0:T(8,128)S(1)}, f32[8,18,34,129]{3,2,1,0:T(8,128)S(1)}) fusion(f32[8,18,34,1]{3,2,1,0:T(8,128)} %copy.28, f32[8,18,1,128]{3,2,1,0:T(1,128)S(1)} %collective-permute-done.3, f32[8,1,32,128]{3,2,1,0:T(8,128)S(1)} %collective-permute-done.1, f32[3,16,32,128]{3,2,1,0:T(8,128)S(1)} %slice_divide_fusion, ...), kind=kLoop, calls=%fused_computation.7 | loop fusion | flops 8842176 | bytes 7598592 | tf_op jit(solution)/shard_map/concatenate | solution.py:19
  94.9 8.8 %fusion = f32[512,3,64]{2,1,0:T(4,128)} fusion(bf16[512,64,128]{2,1,0:T(8,128)(2,1)} %param.14, pred[512,128]{1,0:T(8,128)(4,1)S(1)} %copy-done.15, bf16[1,512,128]{2,0,1:T(2,128)(2,1)S(1)} %copy.36, bf16[1,512,128]{2,0,1:T(2,128)(2,1)S(1)} %copy.35, bf16[1,512,128]{2,0,1:T(2,128)(2,1)S(1)} %copy.34), kind=kOutput, calls=%fused_computation.3 | convolution fusion | flops 30539776 | bytes 9240576 | tf_op jit(solution)/shard_map/ckb,kpb->kcp/dot_general | solution.py:96
  106.2 3.8 %scatter_custom_fusion.1 = f32[1280,192]{1,0:T(8,128)} fusion(s32[512]{0:T(512)S(1)} %bitcast.70, f32[512,192]{1,0:T(8,128)} %copy.38, f32[]{:T(128)} %constant.47.clone.1), kind=kCustom, calls=%fused_computation.30 | custom fusion | bytes 983552 | tf_op jit(solution)/shard_map/scatter | solution.py:108
  110.0 2.6 %reshape.112 = f32[128,10,192]{2,1,0:T(8,128)} reshape(f32[1280,192]{1,0:T(8,128)} %scatter_custom_fusion.1) | data formatting | bytes 1966080 | tf_op jit(solution)/shard_map/reshape | solution.py:117
  112.6 3.5 %reshape.160 = f32[128,1,1920]{2,1,0:T(1,128)} reshape(f32[128,10,192]{2,1,0:T(8,128)} %reshape.112) | data formatting | bytes 1966080
  116.2 17.5 %all-to-all-start.1 = ((f32[128,1,1920]{2,1,0:T(1,128)}), f32[128,1,1920]{2,1,0:T(1,128)}, u32[]{:S(2)}, u32[]{:S(2)}) async-start(f32[128,1,1920]{2,1,0:T(1,128)} %reshape.160), calls=%async_computation.1 | async-start | bytes 1966080 | tf_op jit(solution)/shard_map/all_to_all | solution.py:116
  133.9 81.2 %psum.7 = f32[128]{0:T(128)} all-reduce(f32[128]{0:T(128)S(1)} %convolution_bitcast_fusion), channel_id=1, replica_groups=mesh['sec'=2,'gx'=8,'row'=16] {'sec','gx','row'}, use_global_device_ids=true, to_apply=%region_5.6 | all-reduce | flops 128 | bytes 1024 | tf_op jit(solution)/shard_map/psum | solution.py:150
  215.2 8.2 %pad_maximum_fusion = f32[8,18,34,130]{3,2,1,0:T(8,128)S(1)} fusion(f32[8,18,34,1]{3,2,1,0:T(8,128)} %copy.28, f32[8,18,1,128]{3,2,1,0:T(1,128)S(1)} %collective-permute-done.3, f32[8,1,32,128]{3,2,1,0:T(8,128)S(1)} %collective-permute-done.1, f32[3,16,32,128]{3,2,1,0:T(8,128)S(1)} %slice_divide_fusion, f32[4,16,32,128]{3,2,1,0:T(8,128)S(1)} %copy-done.1, ...), kind=kLoop, calls=%fused_computation.6 | loop fusion | flops 5091840 | bytes 5091840 | tf_op jit(solution)/shard_map/concatenate | solution.py:19
  224.5 2.2 slice_multiply_fusion.2
  226.7 2.9 %fusion.6 = f32[5,16,32,128]{3,2,1,0:T(8,128)} fusion(f32[5,18,34,130]{3,2,1,0:T(8,128)S(1)} %get-tuple-element.10, f32[5,18,34,130]{3,2,1,0:T(8,128)S(1)} %get-tuple-element.9, f32[5,18,34,130]{3,2,1,0:T(8,128)S(1)} %get-tuple-element.8, f32[4,16,32,128]{3,2,1,0:T(8,128)S(1)} %copy-done.1, f32[1,16,32,128]{3,2,1,0:T(8,128)S(1)} %bitcast.55), kind=kLoop, calls=%fused_computation.17 | loop fusion | flops 2621440 | bytes 10485760 | tf_op jit(solution)/shard_map/sub | solution.py:38
  230.1 4.2 %reduce.4 = f32[128,1920]{1,0:T(8,128)S(1)} reduce(f32[128,1,1920]{2,1,0:T(1,128)} %all-to-all-done.1, f32[]{:T(128)} %broadcast.111), dimensions={1}, to_apply=%all_to_all.11.reduce_sub_computation | reduce | bytes 1966084 | tf_op jit(solution)/shard_map/all_to_all | solution.py:116
  (118 shorter events, 34.7 us)
Async XLA Ops:
  0.6 133.1 %copy-start = (f32[128,128]{1,0:T(8,128)S(1)}, f32[128,128]{1,0:T(8,128)}, u32[]{:S(2)}) copy-start(f32[128,128]{1,0:T(8,128)} %param.19) | copy-start | bytes 196612
  0.7 28.4 %copy-start.7 = (f32[4,8,16,128]{3,2,1,0:T(8,128)S(1)}, f32[4,8,16,128]{3,2,1,0:T(8,128)}, u32[]{:S(2)}) copy-start(f32[4,8,16,128]{3,2,1,0:T(8,128)} %param.12) | copy-start | bytes 786436
  0.7 33.9 %copy-start.17 = (s32[512]{0:T(512)S(1)}, s32[512]{0:T(512)}, u32[]{:S(2)}) copy-start(s32[512]{0:T(512)} %param.15) | copy-start | bytes 6148
  0.7 34.7 %copy-start.19 = (s32[128]{0:T(128)S(1)}, s32[128]{0:T(128)}, u32[]{:S(2)}) copy-start(s32[128]{0:T(128)} %param.18) | copy-start | bytes 1540
  2.1 45.4 %copy-start.1 = (f32[4,16,32,128]{3,2,1,0:T(8,128)S(1)}, f32[4,16,32,128]{3,2,1,0:T(8,128)}, u32[]{:S(2)}) copy-start(f32[4,16,32,128]{3,2,1,0:T(8,128)} %param.11) | copy-start | bytes 3145732
  2.1 45.4 %copy-start.2 = (f32[16,32,128]{2,1,0:T(8,128)S(1)}, f32[16,32,128]{2,1,0:T(8,128)}, u32[]{:S(2)}) copy-start(f32[16,32,128]{2,1,0:T(8,128)} %param.10) | copy-start | bytes 786436
  3.1 44.3 %collective-permute-start = (f32[8,1,32,128]{3,2,1,0:T(8,128)S(1)}, f32[8,1,32,128]{3,2,1,0:T(8,128)S(1)}, u32[]{:S(2)}, u32[]{:S(2)}) collective-permute-start(f32[8,1,32,128]{3,2,1,0:T(8,128)S(1)} %get-tuple-element.20), channel_id=1, source_target_pairs={{0,16},{16,32},{32,48},{48,64},{64,80},{80,96},{96,112},{1,17},{17... | collective-permute-start | bytes 393224 | tf_op jit(solution)/shard_map/ppermute | solution.py:15
  7.6 39.8 %collective-permute-start.1 = (f32[8,1,32,128]{3,2,1,0:T(8,128)S(1)}, f32[8,1,32,128]{3,2,1,0:T(8,128)S(1)}, u32[]{:S(2)}, u32[]{:S(2)}) collective-permute-start(f32[8,1,32,128]{3,2,1,0:T(8,128)S(1)} %get-tuple-element.21), channel_id=1, source_target_pairs={{16,0},{32,16},{48,32},{64,48},{80,64},{96,80},{112,96},{17,1},{33... | collective-permute-start | bytes 393224 | tf_op jit(solution)/shard_map/ppermute | solution.py:18
  13.5 32.3 %all-to-all-start = ((f32[128,1,10]{2,1,0:T(1,128)}), f32[128,1,10]{2,1,0:T(1,128)S(1)}, u32[]{:S(2)}, u32[]{:S(2)}) async-start(f32[128,1,10]{2,1,0:T(1,128)} %bitcast.13), calls=%async_computation | async-start | bytes 131072 | tf_op jit(solution)/shard_map/all_to_all | solution.py:123
  29.0 6.4 %collective-permute-start.7 = (f32[4,1,16,128]{3,2,1,0:T(8,128)S(1)}, f32[4,1,16,128]{3,2,1,0:T(8,128)S(1)}, u32[]{:S(2)}, u32[]{:S(2)}) collective-permute-start(f32[4,1,16,128]{3,2,1,0:T(8,128)S(1)} %get-tuple-element.32), channel_id=1, source_target_pairs={{0,16},{16,32},{32,48},{48,64},{64,80},{80,96},{96,112},{1,17},{17... | collective-permute-start | bytes 98312 | tf_op jit(solution)/shard_map/ppermute | solution.py:15
  32.7 5.5 %collective-permute-start.6 = (f32[4,1,16,128]{3,2,1,0:T(8,128)S(1)}, f32[4,1,16,128]{3,2,1,0:T(8,128)S(1)}, u32[]{:S(2)}, u32[]{:S(2)}) collective-permute-start(f32[4,1,16,128]{3,2,1,0:T(8,128)S(1)} %get-tuple-element.31), channel_id=1, source_target_pairs={{16,0},{32,16},{48,32},{64,48},{80,64},{96,80},{112,96},{17,1},{33... | collective-permute-start | bytes 98312 | tf_op jit(solution)/shard_map/ppermute | solution.py:18
  39.0 8.3 %collective-permute-start.8 = (f32[4,10,1,128]{3,2,1,0:T(1,128)S(1)}, f32[4,10,1,128]{3,2,1,0:T(1,128)S(1)}, u32[]{:S(2)}, u32[]{:S(2)}) collective-permute-start(f32[4,10,1,128]{3,2,1,0:T(1,128)S(1)} %get-tuple-element.27), channel_id=1, source_target_pairs={{1,0},{2,1},{3,2},{4,3},{5,4},{6,5},{7,6},{8,7},{9,8},{10,9},{11,1... | collective-permute-start | bytes 61448 | tf_op jit(solution)/shard_map/ppermute | solution.py:18
  40.3 7.1 %collective-permute-start.9 = (f32[4,10,1,128]{3,2,1,0:T(1,128)S(1)}, f32[4,10,1,128]{3,2,1,0:T(1,128)S(1)}, u32[]{:S(2)}, u32[]{:S(2)}) collective-permute-start(f32[4,10,1,128]{3,2,1,0:T(1,128)S(1)} %get-tuple-element.26), channel_id=1, source_target_pairs={{0,1},{1,2},{2,3},{3,4},{4,5},{5,6},{6,7},{7,8},{8,9},{9,10},{10,1... | collective-permute-start | bytes 61448 | tf_op jit(solution)/shard_map/ppermute | solution.py:15
  47.3 28.4 %copy-start.11 = (f32[4,10,1,128]{3,2,1,0:T(1,128)}, f32[4,10,1,128]{3,2,1,0:T(1,128)S(1)}, u32[]{:S(2)}) copy-start(f32[4,10,1,128]{3,2,1,0:T(1,128)S(1)} %collective-permute-done.8) | copy-start | bytes 61444
  47.3 28.3 %copy-start.13 = (f32[4,10,1,128]{3,2,1,0:T(1,128)}, f32[4,10,1,128]{3,2,1,0:T(1,128)S(1)}, u32[]{:S(2)}) copy-start(f32[4,10,1,128]{3,2,1,0:T(1,128)S(1)} %collective-permute-done.9) | copy-start | bytes 61444
  47.6 13.7 %collective-permute-start.2 = (f32[8,18,1,128]{3,2,1,0:T(1,128)S(1)}, f32[8,18,1,128]{3,2,1,0:T(1,128)S(1)}, u32[]{:S(2)}, u32[]{:S(2)}) collective-permute-start(f32[8,18,1,128]{3,2,1,0:T(1,128)S(1)} %get-tuple-element.18), channel_id=1, source_target_pairs={{0,1},{1,2},{2,3},{3,4},{4,5},{5,6},{6,7},{7,8},{8,9},{9,10},{10,1... | collective-permute-start | bytes 221192 | tf_op jit(solution)/shard_map/ppermute | solution.py:15
  52.8 8.5 %collective-permute-start.3 = (f32[8,18,1,128]{3,2,1,0:T(1,128)S(1)}, f32[8,18,1,128]{3,2,1,0:T(1,128)S(1)}, u32[]{:S(2)}, u32[]{:S(2)}) collective-permute-start(f32[8,18,1,128]{3,2,1,0:T(1,128)S(1)} %get-tuple-element.19), channel_id=1, source_target_pairs={{1,0},{2,1},{3,2},{4,3},{5,4},{6,5},{7,6},{8,7},{9,8},{10,9},{11,1... | collective-permute-start | bytes 221192 | tf_op jit(solution)/shard_map/ppermute | solution.py:18
  55.2 20.5 %collective-permute-start.10 = (f32[4,10,18,1]{3,2,1,0:T(8,128)}, f32[4,10,18,1]{3,2,1,0:T(8,128)S(1)}, u32[]{:S(2)}, u32[]{:S(2)}) collective-permute-start(f32[4,10,18,1]{3,2,1,0:T(8,128)} %get-tuple-element.24), channel_id=1, source_target_pairs={{128,0},{129,1},{130,2},{131,3},{132,4},{133,5},{134,6},{135,7},{1... | collective-permute-start | bytes 8648 | tf_op jit(solution)/shard_map/ppermute | solution.py:18
  56.5 19.2 %collective-permute-start.11 = (f32[4,10,18,1]{3,2,1,0:T(8,128)}, f32[4,10,18,1]{3,2,1,0:T(8,128)}, u32[]{:S(2)}, u32[]{:S(2)}) collective-permute-start(f32[4,10,18,1]{3,2,1,0:T(8,128)} %get-tuple-element.25), channel_id=1, source_target_pairs={{0,128},{1,129},{2,130},{3,131},{4,132},{5,133},{6,134},{7,135},{8... | collective-permute-start | bytes 8648 | tf_op jit(solution)/shard_map/ppermute | solution.py:15
  68.7 9.5 %collective-permute-start.4 = (f32[8,18,34,1]{2,0,3,1:T(8,128)}, f32[8,18,34,1]{2,0,3,1:T(8,128)}, u32[]{:S(2)}, u32[]{:S(2)}) collective-permute-start(f32[8,18,34,1]{2,0,3,1:T(8,128)} %copy.25), channel_id=1, source_target_pairs={{0,128},{1,129},{2,130},{3,131},{4,132},{5,133},{6,134},{7,135},{8... | collective-permute-start | bytes 58760 | tf_op jit(solution)/shard_map/ppermute | solution.py:15
  74.2 7.6 %collective-permute-start.5 = (f32[8,18,34,1]{2,0,3,1:T(8,128)}, f32[8,18,34,1]{2,0,3,1:T(8,128)}, u32[]{:S(2)}, u32[]{:S(2)}) collective-permute-start(f32[8,18,34,1]{2,0,3,1:T(8,128)} %copy.26), channel_id=1, source_target_pairs={{128,0},{129,1},{130,2},{131,3},{132,4},{133,5},{134,6},{135,7},{1... | collective-permute-start | bytes 58760 | tf_op jit(solution)/shard_map/ppermute | solution.py:18
  75.6 9.7 %copy-start.3 = (f32[4,10,18,1]{3,2,1,0:T(8,128)}, f32[4,10,18,1]{3,2,1,0:T(8,128)S(1)}, u32[]{:S(2)}) copy-start(f32[4,10,18,1]{3,2,1,0:T(8,128)S(1)} %collective-permute-done.10) | copy-start | bytes 8644
  110.0 23.7 %copy-start.20 = (s32[128]{0:T(128)S(1)}, s32[128]{0:T(128)}, u32[]{:S(2)}) copy-start(s32[128]{0:T(128)} %param.18) | copy-start | bytes 1540
  116.2 113.4 %all-to-all-start.1 = ((f32[128,1,1920]{2,1,0:T(1,128)}), f32[128,1,1920]{2,1,0:T(1,128)}, u32[]{:S(2)}, u32[]{:S(2)}) async-start(f32[128,1,1920]{2,1,0:T(1,128)} %reshape.160), calls=%async_computation.1 | async-start | bytes 1966080 | tf_op jit(solution)/shard_map/all_to_all | solution.py:116
  (11 other events, 50.2 us)
where the time goes:
time: 243 us; the launch traced here: 242 us
  blocking collectives  81.2 us (33%)
  starting transfers between devices  67.2 us (28%)
  local copies, waits for them, and re-layouts  43.8 us (18%)
  other arithmetic  34.6 us (14%)
  matrix products  9.91 us (4%)
  waiting for transfers between devices  2.76 us (1%)
    psum x1, blocking collectives, per_device(): far_field = lax.psum(partial_far, ('sec', 'gx', 'row'))  81.2 us
    ppermute x6, starting transfers between devices, padded_2(): lax.ppermute(lax.slice_in_dim(block, block.shape[dim] - width, None, axis...  24.9 us
    all_to_all x1, starting transfers between devices, per_device(): lax.all_to_all(send_values.reshape(owners, capacity, 3 * patch_cells), ('...  17.5 us
    concatenate x4, other arithmetic, padded_2(): block = jnp.concatenate([low, block, high], axis=dim)  17 us
    all_to_all x1, starting transfers between devices, per_device(): lax.all_to_all(send_patch.reshape(owners, capacity), ('gx', 'row'), split...  15.5 us
    ppermute x6, starting transfers between devices, padded_2(): lax.ppermute(lax.slice_in_dim(block, 0, width, axis=dim), axis, backward)  9.18 us
    dot_general x1, matrix products, per_device(): jnp.einsum('ckb,kpb->kcp', lamb_blocks, masked, preferred_element_type=jn...  8.81 us
    slice x3, local copies, waits for them, and re-layouts, padded_2(): lax.slice_in_dim(block, block.shape[dim] - width, None, axis=dim)  6.97 us
  transfers between devices with their start and end apart: 14, of which 1 were waited for; matrix products, arithmetic and copies ran while one was open for 16% of the time, Pallas kernels for 0%

commit v1 on v0

v1 whole, which is shorter than its diff:
```python
import jax
import jax.numpy as jnp
from jax import lax
from jax.experimental import pallas as pl
from jax.experimental.pallas import tpu as pltpu
from jax.sharding import PartitionSpec as P

LES_STEP = 0.2
WAVE_STEP = 0.25
CAP = 10
ROWS = 16
F32 = jnp.float32
BF16 = jnp.bfloat16
ALL = ("sec", "gx", "row")
MIB = 1 << 20


def iota(shape, dim):
    return lax.broadcasted_iota(jnp.int32, shape, dim)


def as_column(line):
    return jnp.transpose(jnp.broadcast_to(line, (128, 128)))


def edge_line(block, high, eye):
    column = jnp.where(high, block[:, 127:128], block[:, 0:1])
    return jnp.sum(jnp.where(eye, column, 0.0), axis=0, keepdims=True)


def safe(density):
    return jnp.where(density == 0.0, 1.0, density)


def down(plane, halo):
    return jnp.where(iota(plane.shape, 0) == 0, halo, pltpu.roll(plane, 1, 0))


def up(plane, halo):
    last = plane.shape[0] - 1
    return jnp.where(iota(plane.shape, 0) == last, halo, pltpu.roll(plane, last, 0))


def derive_z(plane, halo, sec):
    lane = iota(plane.shape, 1)
    before = jnp.where(lane == 0, jnp.where(sec == 1, halo, 0.0), pltpu.roll(plane, 1, 1))
    after = jnp.where(lane == 127, jnp.where(sec == 0, halo, 0.0), pltpu.roll(plane, 127, 1))
    return 0.5 * (after - before)


def pack_kernel(rho, rest, wave, x_low, x_high, y_low, y_high, z_face):
    high = lax.axis_index("sec") == 0
    for target, plane, wave_plane in ((x_low, 0, 0), (x_high, 15, 7)):
        target[0:32] = rho[plane * 32 : plane * 32 + 32]
        for part in range(4):
            at = part * 512 + plane * 32
            target[32 * part + 32 : 32 * part + 64] = rest[at : at + 32]
            at = part * 128 + wave_plane * 16
            target[160 + 16 * part : 176 + 16 * part] = wave[at : at + 16]
    for target, line, wave_line in ((y_low, 0, 0), (y_high, 31, 15)):
        target[0:16] = rho[pl.ds(line, 16, stride=32)]
        for part in range(4):
            target[16 * part + 16 : 16 * part + 32] = rest[pl.ds(part * 512 + line, 16, stride=32)]
        target[80:88] = wave[pl.ds(wave_line, 8, stride=16)]
        target[88:96] = wave[pl.ds(256 + wave_line, 8, stride=16)]
    eye = iota((128, 128), 0) == iota((128, 128), 1)
    for piece in range(4):
        z_face[piece : piece + 1] = edge_line(rho[piece * 128 : piece * 128 + 128], high, eye)
    for piece in range(16):
        z_face[piece + 4 : piece + 5] = edge_line(rest[piece * 128 : piece * 128 + 128], high, eye)
    z_face[20:21] = edge_line(wave[0:128], high, eye)
    z_face[21:22] = edge_line(wave[384:512], high, eye)
    z_face[22:24] = jnp.zeros((2, 128), F32)


def slot_kernel(owner, counts, patch, slots, valid, patches):
    below = iota((128, 128), 0) < iota((128, 128), 1)
    target = iota((128, 128), 0) * 16
    lane = iota((128, 128), 1)
    lines = [owner[piece : piece + 1].astype(F32) for piece in range(4)]
    columns = [as_column(line) for line in lines]
    for piece in range(4):
        rank = jnp.zeros((1, 128), F32)
        for other in range(piece + 1):
            same = columns[other] == lines[piece]
            if other == piece:
                same = same & below
            rank = rank + jnp.sum(same.astype(F32), axis=0, keepdims=True)
        code = (lines[piece] * 16.0 + rank).astype(jnp.int32)
        here = slice(piece * 128, piece * 128 + 128)
        for slot in range(CAP):
            hit = (target + slot) == code
            slots[slot * 128 : slot * 128 + 128, here] = hit.astype(F32).astype(BF16)
        limit = as_column(counts[piece : piece + 1].astype(F32))
        valid[here] = (lane.astype(F32) < limit).astype(F32)
        patches[here] = as_column(patch[piece : piece + 1].astype(F32)).astype(BF16)


def send_kernel(
    rho, momentum, x_low, x_high, y_low, y_high, z_face, slots, valid, patches, weights,
    send, speed, z_speed, payload,
):
    step = pl.program_id(0)
    steps = pl.num_programs(0)
    lines = 512 // steps
    sec = lax.axis_index("sec")

    @pl.when(step == 0)
    def _():
        for part in range(3):
            speed[part, 32:544] = momentum[part * 512 : part * 512 + 512] / rho[...]
            for at, face in ((0, x_low), (544, x_high)):
                speed[part, at : at + 32] = (
                    face[32 * part + 32 : 32 * part + 64] / safe(face[0:32])
                )
        for part in range(2):
            edge = z_face[4 * part + 4 : 4 * part + 8] / safe(z_face[0:4])
            for piece in range(4):
                z_speed[part, piece * 128 : piece * 128 + 128] = as_column(
                    edge[piece : piece + 1]
                )
        payload[:, 384:512] = patches[...]

    group = iota((16, 128), 0)
    half = iota((16, 128), 1) < 64
    keep = [(group // 4 == part).astype(F32).astype(BF16) for part in range(4)]
    wide = iota((16, 256), 1) // 64 == iota((16, 256), 0) % 4

    for plane in range(lines // 32):
        x = step * (lines // 32) + plane
        at = pl.multiple_of(x * 32, 32)
        v = [speed[part, pl.ds(at + 32, 32)] for part in range(3)]
        v_before = [speed[part, pl.ds(at, 32)] for part in range(3)]
        v_after = [speed[part, pl.ds(at + 64, 32)] for part in range(3)]
        y_before, y_after = {}, {}
        for part in (0, 2):
            here = 16 * part + 16
            y_before[part] = y_low[pl.ds(here + x, 1)] / safe(y_low[pl.ds(x, 1)])
            y_after[part] = y_high[pl.ds(here + x, 1)] / safe(y_high[pl.ds(x, 1)])
        along = {part: 0.5 * (v_after[part] - v_before[part]) for part in (1, 2)}
        across = {
            part: 0.5 * (up(v[part], y_after[part]) - down(v[part], y_before[part]))
            for part in (0, 2)
        }
        deep = {part: derive_z(v[part], z_speed[part, pl.ds(at, 32)], sec) for part in (0, 1)}
        swirl_x = across[2] - deep[1]
        swirl_y = deep[0] - along[2]
        swirl_z = along[1] - across[0]
        mask = valid[pl.ds(at, 32)]
        lamb = [
            ((swirl_y * v[2] - swirl_z * v[1]) * mask).astype(BF16),
            ((swirl_z * v[0] - swirl_x * v[2]) * mask).astype(BF16),
            ((swirl_x * v[1] - swirl_y * v[0]) * mask).astype(BF16),
        ]
        for part in range(2):
            rows = slice(part * 16, part * 16 + 16)
            left = jnp.concatenate(
                [
                    jnp.concatenate([lamb[c][rows] * keep[k] for k in range(4)], axis=1)
                    for c in range(3)
                ],
                axis=0,
            )
            first = plane * 32 + part * 16
            right = jnp.concatenate(
                [
                    weights[(first + 4 * k) * 64 : (first + 4 * k + 4) * 64]
                    for k in range(4)
                ],
                axis=1,
            )
            product = lax.dot_general(
                left, right, (((1,), (1,)), ((), ())), preferred_element_type=F32
            )
            folded = []
            for c in range(3):
                picked = jnp.where(wide, product[c * 16 : c * 16 + 16], 0.0)
                both = picked[:, 0:128] + picked[:, 128:256]
                folded.append(both + pltpu.roll(both, 64, 1))
            pair = jnp.where(half, folded[0], folded[1])
            pair_top = pair.astype(BF16)
            pair_rest = (pair - pair_top.astype(F32)).astype(BF16)
            single_top = folded[2].astype(BF16).astype(F32)
            single = jnp.where(half, single_top, folded[2] - single_top).astype(BF16)
            here = pl.ds(pl.multiple_of(at + part * 16, 16), 16)
            payload[here, 0:128] = pair_top
            payload[here, 128:256] = pair_rest
            payload[here, 256:384] = single

    @pl.when(step == steps - 1)
    def _():
        lane = iota((128, 128), 1)
        numbers = jnp.zeros((128, 128), F32)
        kept = None
        for slot in range(CAP):
            placed = jnp.dot(
                slots[slot * 128 : slot * 128 + 128], payload[...], preferred_element_type=F32
            )
            send[pl.ds(slot, 128, stride=ROWS)] = placed[:, 0:128] + placed[:, 128:256]
            third = placed[:, 256:384]
            third = third + pltpu.roll(third, 64, 1)
            if slot % 2 == 0:
                kept = third
            else:
                send[pl.ds(CAP + slot // 2, 128, stride=ROWS)] = jnp.where(
                    lane < 64, kept, third
                )
            numbers = jnp.where(lane == slot, placed[:, 384:512], numbers)
        send[pl.ds(ROWS - 1, 128, stride=ROWS)] = numbers


def wave_kernel(
    tile_class, wave, x_low, x_high, y_low, y_high, z_face, samples, far, base, share
):
    sec = lax.axis_index("sec")
    level = tile_class[0, 0].astype(F32)
    mean_flow = 0.1 + 0.3 * level
    stiffness = 1.0 + 0.25 * level
    z_pressure = as_column(z_face[20:21])
    z_speed = as_column(z_face[21:22])
    for x in range(8):
        def row(part, at):
            start = part * 128 + at * 16
            if at < 0:
                return x_low[160 + 16 * part : 176 + 16 * part]
            if at > 7:
                return x_high[160 + 16 * part : 176 + 16 * part]
            return wave[start : start + 16]

        now = [row(part, x) for part in range(4)]
        along = [0.5 * (row(part, x + 1) - row(part, x - 1)) for part in range(4)]
        across = [
            0.5
            * (
                up(now[part], y_high[80 + 8 * k + x : 81 + 8 * k + x])
                - down(now[part], y_low[80 + 8 * k + x : 81 + 8 * k + x])
            )
            for k, part in enumerate((0, 2))
        ]
        here = slice(x * 16, x * 16 + 16)
        deep = [derive_z(now[0], z_pressure[here], sec), derive_z(now[3], z_speed[here], sec)]
        divergence = along[1] + across[1] + deep[1]
        base[here] = now[0] - WAVE_STEP * (mean_flow * along[0] + stiffness * divergence)
        for part, gradient in ((1, along[0]), (2, across[0]), (3, deep[0])):
            base[part * 128 + x * 16 : part * 128 + x * 16 + 16] = now[part] - WAVE_STEP * (
                mean_flow * along[part] + gradient
            )
    index = samples[...]
    line, cell = index // 128, index % 128
    picks = (iota((128, 128), 0) == line).astype(F32)
    columns = lax.dot_general(
        base[0:128], picks, (((0,), (0,)), ((), ())),
        precision=lax.Precision.HIGHEST, preferred_element_type=F32,
    )
    values = jnp.sum(
        jnp.where(iota((128, 128), 0) == cell, columns, 0.0), axis=0, keepdims=True
    )
    total = lax.dot_general(
        jnp.broadcast_to(values, (8, 128)), far[...], (((1,), (1,)), ((), ())),
        precision=lax.Precision.HIGHEST, preferred_element_type=F32,
    )
    for block in range(share.shape[0] // 8):
        share[block * 8 : block * 8 + 8] = total


def les_kernel(rho, rest, x_low, x_high, y_low, y_high, z_face, out):
    sec = lax.axis_index("sec")
    lane = iota((32, 128), 1)
    z_rho = safe(z_face[0:4])
    z_v = z_face[12:16] / z_rho
    y_low_v = y_low[32:48] / safe(y_low[0:16])
    y_high_v = y_high[32:48] / safe(y_high[0:16])
    x_low_v = x_low[32:64] / safe(x_low[0:32])
    x_high_v = x_high[32:64] / safe(x_high[0:32])
    for part in range(5):
        def state(x):
            if part == 0:
                return rho[x * 32 : x * 32 + 32]
            return rest[part * 512 - 512 + x * 32 : part * 512 - 512 + x * 32 + 32]

        z_flux = z_face[4 * part : 4 * part + 4] * z_v
        y_low_flux = y_low[16 * part : 16 * part + 16] * y_low_v
        y_high_flux = y_high[16 * part : 16 * part + 16] * y_high_v
        for x in range(16):
            density = rho[x * 32 : x * 32 + 32]
            now = state(x)

            def stream(at):
                if at < 0:
                    return x_low[32 * part : 32 * part + 32] * x_low_v
                if at > 15:
                    return x_high[32 * part : 32 * part + 32] * x_high_v
                return state(at) * (rest[at * 32 : at * 32 + 32] / rho[at * 32 : at * 32 + 32])

            along = 0.5 * (stream(x + 1) - stream(x - 1))
            side = now * (rest[512 + x * 32 : 512 + x * 32 + 32] / density)
            across = 0.5 * (
                up(side, y_high_flux[x : x + 1]) - down(side, y_low_flux[x : x + 1])
            )
            depth = now * (rest[1024 + x * 32 : 1024 + x * 32 + 32] / density)
            if x % 4 == 0:
                z_column = as_column(z_flux[x // 4 : x // 4 + 1])
            deep = derive_z(depth, z_column[x % 4 * 32 : x % 4 * 32 + 32], sec)
            start = part * 512 + x * 32
            out[start : start + 32] = now - LES_STEP * (along + across + deep)


def finish_kernel(arrived, base, shares, out, far):
    names = jnp.transpose(arrived[pl.ds(ROWS - 1, 128, stride=ROWS)])
    place = iota((256, 128), 0)
    patch = (place % 128 * 2 + place // 128).astype(F32)
    half = iota((128, 128), 1) < 64
    total = jnp.zeros((256, 512), F32)
    for pair in range(CAP // 2):
        third = arrived[pl.ds(CAP + pair, 128, stride=ROWS)]
        left, right = [], []
        for slot in (2 * pair, 2 * pair + 1):
            left.append((patch == names[slot : slot + 1]).astype(F32).astype(BF16))
            both = arrived[pl.ds(slot, 128, stride=ROWS)]
            one = jnp.where(half == (slot % 2 == 0), third, 0.0)
            row = []
            for value in (both, one):
                top = value.astype(BF16)
                row += [top, (value - top.astype(F32)).astype(BF16)]
            right.append(jnp.concatenate(row, axis=1))
        total = total + jnp.dot(
            jnp.concatenate(left, axis=1),
            jnp.concatenate(right, axis=0),
            preferred_element_type=F32,
        )
    both = total[:, 0:128] + total[:, 128:256]
    third = total[:, 256:384] + total[:, 384:512]
    third = third + pltpu.roll(third, 64, 1)
    even, odd = both[0:128], both[128:256]
    source = [
        jnp.where(half, even, pltpu.roll(odd, 64, 1)),
        jnp.where(half, pltpu.roll(even, 64, 1), odd),
        jnp.where(half, third[0:128], third[128:256]),
    ]
    out[0:128] = base[0:128]
    for part in range(3):
        here = slice(part * 128 + 128, part * 128 + 256)
        out[here] = base[here] - WAVE_STEP * source[part]
    far[...] = jnp.sum(shares[...], axis=0, keepdims=True)


def call(kernel, outs, flops, moved, limit=16, **more):
    return pl.pallas_call(
        kernel,
        out_shape=[jax.ShapeDtypeStruct(shape, kind) for shape, kind in outs],
        compiler_params=pltpu.CompilerParams(vmem_limit_bytes=limit * MIB),
        cost_estimate=pl.CostEstimate(flops=flops, bytes_accessed=moved, transcendentals=0),
        **more,
    )


def shift(face, axis, offset):
    count = lax.axis_size(axis)
    pairs = [(i, i + offset) for i in range(count) if 0 <= i + offset < count]
    return lax.ppermute(face, axis, pairs)


def per_device(
    les_density,
    les_rest,
    acoustic,
    block_owner,
    block_weights,
    block_counts,
    block_patch,
    tile_class,
    sample_index,
    far_kernel,
):
    rho = les_density.reshape(512, 128)
    rest = les_rest.reshape(2048, 128)
    wave = acoustic.reshape(512, 128)
    with jax.named_scope("pack"):
        faces = call(
            pack_kernel,
            [((224, 128), F32)] * 2 + [((96, 128), F32)] * 2 + [((24, 128), F32)],
            1 << 20, 2 << 20,
        )(rho, rest, wave)
    halos = [
        shift(faces[1], "gx", 1),
        shift(faces[0], "gx", -1),
        shift(faces[3], "row", 1),
        shift(faces[2], "row", -1),
        lax.ppermute(faces[4], "sec", [(0, 1), (1, 0)]),
    ]
    with jax.named_scope("slots"):
        slots, valid, patches = call(
            slot_kernel,
            [((CAP * 128, 512), BF16), ((512, 128), F32), ((512, 128), BF16)],
            1 << 22, 2 << 20,
        )(
            block_owner.reshape(4, 128),
            block_counts.reshape(4, 128),
            block_patch.reshape(4, 128),
        )
    steps = 4
    with jax.named_scope("send"):
        whole = lambda shape: pl.BlockSpec(shape, lambda i: (0, 0))
        (send,) = call(
            send_kernel,
            [((128 * ROWS, 128), F32)],
            1 << 28, 16 << 20, 32,
            grid=(steps,),
            in_specs=[
                whole((512, 128)), whole((1536, 128)),
                whole((224, 128)), whole((224, 128)), whole((96, 128)), whole((96, 128)),
                whole((24, 128)), whole((CAP * 128, 512)), whole((512, 128)),
                whole((512, 128)),
                pl.BlockSpec((512 * 64 // steps, 128), lambda i: (i, 0)),
            ],
            out_specs=[whole((128 * ROWS, 128))],
            scratch_shapes=[
                pltpu.VMEM((3, 576, 128), F32),
                pltpu.VMEM((2, 512, 128), F32),
                pltpu.VMEM((512, 512), BF16),
            ],
        )(rho, rest, *halos, slots, valid, patches, block_weights.reshape(512 * 64, 128))
    arrived = lax.all_to_all(
        send.reshape(128, ROWS, 128), ("gx", "row"), split_axis=0, concat_axis=0, tiled=True
    )
    with jax.named_scope("wave"):
        smem = pl.BlockSpec(memory_space=pltpu.SMEM)
        vmem = pl.BlockSpec(memory_space=pltpu.VMEM)
        base, share = call(
            wave_kernel,
            [((512, 128), F32), ((256, 128), F32)],
            1 << 24, 2 << 20,
            in_specs=[smem] + [vmem] * 8,
        )(
            tile_class.reshape(1, 1), wave, *halos, sample_index.reshape(1, 128), far_kernel
        )
    shares = lax.all_to_all(
        share.reshape(256, 1, 128), ALL, split_axis=0, concat_axis=0, tiled=True
    )
    with jax.named_scope("les"):
        (les_next,) = call(les_kernel, [((2560, 128), F32)], 1 << 23, 4 << 20)(rho, rest, *halos)
    with jax.named_scope("finish"):
        wave_next, far_field = call(
            finish_kernel, [((512, 128), F32), ((1, 128), F32)], 1 << 28, 3 << 20,
        )(arrived.reshape(128 * ROWS, 128), base, shares.reshape(256, 128))
    return (
        les_next.reshape(5, 16, 32, 128),
        wave_next.reshape(4, 8, 16, 128),
        far_field.reshape(128),
    )


def solution(mesh):
    in_specs = (
        P("gx", "row", "sec"),
        P(None, "gx", "row", "sec"),
        P(None, "gx", "row", "sec"),
        P(("sec", "gx", "row"), None),
        P(("sec", "gx", "row"), None, None),
        P(("sec", "gx", "row")),
        P(("sec", "gx", "row")),
        P("sec", "gx", "row"),
        P(("sec", "gx", "row")),
        P(None, ("sec", "gx", "row")),
    )
    out_specs = (P(None, "gx", "row", "sec"), P(None, "gx", "row", "sec"), P())
    return jax.shard_map(
        per_device, mesh=mesh, in_specs=in_specs, out_specs=out_specs, check_vma=False
    )
```

time: 243 us -> 97.2 us (0.40)
  blocking collectives: 81.2 us -> 0 us
  local copies, waits for them, and re-layouts: 43.8 us -> 6.54 us
  other arithmetic: 34.6 us -> 0 us
  waiting for transfers between devices: 2.76 us -> 35.6 us
  starting transfers between devices: 67.2 us -> 39.7 us
  Pallas kernels: 0 us -> 13.5 us
  matrix products: 9.91 us -> 0 us
    psum x1 -> x0, blocking collectives: 81.2 us -> none  [per_device(): far_field = lax.psum(partial_far, ('sec', 'gx', 'row'))]
    all_to_all x2, waiting for transfers between devices: 0.01 us -> 31.6 us  [the longest x1 28.5 us: per_device(): lax.all_to_all(send.reshape(128, ROWS, 128), ('gx', 'row'), split_axis=0,...]
    ppermute x12 -> x5, starting transfers between devices: 34.1 us -> 14.3 us  [the longest x4 12.6 us: shift(): return lax.ppermute(face, axis, pairs)]
    concatenate x4 -> x0, other arithmetic: 17 us -> none  [padded_2(): block = jnp.concatenate([low, block, high], axis=dim)]
    pallas_call x0 -> x6, Pallas kernels: none -> 13.5 us  [the longest x1 5.68 us: per_device(): call(send_kernel, [((128 * ROWS, 128), F32)], 1 << 28, 16 << 20, 32, grid...]
    slice x10 -> x0, local copies, waits for them, and re-layouts: 11.9 us -> none  [the longest x3 6.97 us: padded_2(): lax.slice_in_dim(block, block.shape[dim] - width, None, axis=dim)]
    dot_general x3 -> x0, matrix products: 9.91 us -> none  [the longest x1 8.81 us: per_device(): jnp.einsum('ckb,kpb->kcp', lamb_blocks, masked, preferred_element_type=jn...]
    all_to_all x2, starting transfers between devices: 33.1 us -> 25.4 us  [the longest x1 14.1 us: per_device(): lax.all_to_all(share.reshape(256, 1, 128), ALL, split_axis=0, concat_axis...]
  transfers between devices with their start and end apart: 14 -> 7, of which waited for: 1 -> 4; matrix products, arithmetic and copies ran while one was open for 16% -> 0% of each run, Pallas kernels for 0% -> 3%
where the time goes in v1:
time: 97.2 us; the launch traced here: 96.8 us
  starting transfers between devices  39.7 us (41%)
  waiting for transfers between devices  35.6 us (37%)
  Pallas kernels  13.5 us (14%)
  local copies, waits for them, and re-layouts  6.54 us (7%)
  between operations  1.45 us (1%)
    all_to_all x1, waiting for transfers between devices, per_device(): lax.all_to_all(send.reshape(128, ROWS, 128), ('gx', 'row'), split_axis=0,...  28.5 us
    all_to_all x1, starting transfers between devices, per_device(): lax.all_to_all(share.reshape(256, 1, 128), ALL, split_axis=0, concat_axis...  14.1 us
    ppermute x4, starting transfers between devices, shift(): return lax.ppermute(face, axis, pairs)  12.6 us
    all_to_all x1, starting transfers between devices, per_device(): lax.all_to_all(send.reshape(128, ROWS, 128), ('gx', 'row'), split_axis=0,...  11.3 us
    unnamed x22, local copies, waits for them, and re-layouts  6.54 us
    pallas_call x1, Pallas kernels, per_device(): call(send_kernel, [((128 * ROWS, 128), F32)], 1 << 28, 16 << 20, 32, grid...  5.68 us
    ppermute x4, waiting for transfers between devices, shift(): return lax.ppermute(face, axis, pairs)  3.49 us
    all_to_all x1, waiting for transfers between devices, per_device(): lax.all_to_all(share.reshape(256, 1, 128), ALL, split_axis=0, concat_axis...  3.13 us
  transfers between devices with their start and end apart: 7, of which 4 were waited for; matrix products, arithmetic and copies ran while one was open for 0% of the time, Pallas kernels for 3%

profile of v1, /device:TPU:1, one launch (start us, length us, event | category | flops | bytes accessed | tf_op | source)
XLA Modules:
  0.0 96.8 jit_solution(8574599309340338875)
XLA Ops:
  0.7 1.2 %copy-done = f32[4,16,32,128]{3,2,1,0:T(8,128)S(1)} copy-done((f32[4,16,32,128]{3,2,1,0:T(8,128)S(1)}, f32[4,16,32,128]{3,2,1,0:T(8,128)}, u32[]{:S(2)}) %copy-start) | copy-done | bytes 1048600
  1.9 0.9 copy-done.3
  2.9 0.9 copy-done.5
  3.8 1.8 %pack.1 = (f32[224,128]{1,0:T(8,128)S(1)}, f32[224,128]{1,0:T(8,128)S(1)}, f32[96,128]{1,0:T(8,128)S(1)}, f32[96,128]{1,0:T(8,128)S(1)}, f32[24,128]{1,0:T(8,128)S(1)}) custom-call(f32[512,128]{1,0:T(8,128)S(1)} %bitcast.24, f32[2048,128]{1,0:T(8,128)S(1)} %bitcast.19, f32[512,128]{1,0:T(8,128)S(1)} %bitcast.27), custom_call_target="tpu_custom_call" | custom-call | flops 1048576 | bytes 2097152 | tf_op jit(solution)/shard_map/pack/pallas_call | solution.py:379
  5.6 4.5 %collective-permute-start = (f32[224,128]{1,0:T(8,128)S(1)}, f32[224,128]{1,0:T(8,128)S(1)}, u32[]{:S(2)}, u32[]{:S(2)}) collective-permute-start(f32[224,128]{1,0:T(8,128)S(1)} %get-tuple-element.15), channel_id=1, source_target_pairs={{0,16},{16,32},{32,48},{48,64},{64,80},{80,96},{96,112},{1,17},{17... | collective-permute-start | bytes 344072 | tf_op jit(solution)/shard_map/ppermute | solution.py:360
  10.1 1.9 %collective-permute-start.1 = (f32[224,128]{1,0:T(8,128)S(1)}, f32[224,128]{1,0:T(8,128)S(1)}, u32[]{:S(2)}, u32[]{:S(2)}) collective-permute-start(f32[224,128]{1,0:T(8,128)S(1)} %get-tuple-element.16), channel_id=1, source_target_pairs={{16,0},{32,16},{48,32},{64,48},{80,64},{96,80},{112,96},{17,1},{33... | collective-permute-start | bytes 344072 | tf_op jit(solution)/shard_map/ppermute | solution.py:360
  12.1 4.9 %collective-permute-start.2 = (f32[96,128]{1,0:T(8,128)S(1)}, f32[96,128]{1,0:T(8,128)S(1)}, u32[]{:S(2)}, u32[]{:S(2)}) collective-permute-start(f32[96,128]{1,0:T(8,128)S(1)} %get-tuple-element.17), channel_id=1, source_target_pairs={{0,1},{1,2},{2,3},{3,4},{4,5},{5,6},{6,7},{7,8},{8,9},{9,10},{10,1... | collective-permute-start | bytes 147464 | tf_op jit(solution)/shard_map/ppermute | solution.py:360
  17.0 1.3 %collective-permute-start.3 = (f32[96,128]{1,0:T(8,128)S(1)}, f32[96,128]{1,0:T(8,128)S(1)}, u32[]{:S(2)}, u32[]{:S(2)}) collective-permute-start(f32[96,128]{1,0:T(8,128)S(1)} %get-tuple-element.18), channel_id=1, source_target_pairs={{1,0},{2,1},{3,2},{4,3},{5,4},{6,5},{7,6},{8,7},{9,8},{10,9},{11,1... | collective-permute-start | bytes 147464 | tf_op jit(solution)/shard_map/ppermute | solution.py:360
  18.3 1.7 %collective-permute-start.4 = (f32[24,128]{1,0:T(8,128)S(1)}, f32[24,128]{1,0:T(8,128)S(1)}, u32[]{:S(2)}, u32[]{:S(2)}) collective-permute-start(f32[24,128]{1,0:T(8,128)S(1)} %get-tuple-element.19), channel_id=1, source_target_pairs={{0,128},{128,0},{1,129},{129,1},{2,130},{130,2},{3,131},{131,3},{4... | collective-permute-start | bytes 36872 | tf_op jit(solution)/shard_map/ppermute | solution.py:389
  20.7 0.4 collective-permute-done.4.z_face
  21.1 0.0 collective-permute-done.2.y_low
  21.1 3.5 %collective-permute-done.3.y_high = f32[96,128]{1,0:T(8,128)S(1)} collective-permute-done((f32[96,128]{1,0:T(8,128)S(1)}, f32[96,128]{1,0:T(8,128)S(1)}, u32[]{:S(2)}, u32[]{:S(2)}) %collective-permute-start.3) | collective-permute-done | bytes 49184 | tf_op jit(solution)/shard_map/ppermute | solution.py:360
  24.6 0.0 collective-permute-done.x_low
  24.6 1.4 %wave.1 = (f32[512,128]{1,0:T(8,128)S(1)}, f32[256,128]{1,0:T(8,128)}) custom-call(s32[1,1]{1,0:T(1,128)} %bitcast.18.tile_class, f32[512,128]{1,0:T(8,128)S(1)} %bitcast.28, f32[224,128]{1,0:T(8,128)S(1)} %collective-permute-done.x_low, f32[224,128]{1,0:T(8,128)S(1)} %collective-permute-done.1.x_high, f32[96,128]{1,0:T(8,128)S(1)} %collective-permute-done.2.y_low, ...), custom_call_target="tpu_custom_call" | custom-call | flops 16777216 | bytes 2097152 | tf_op jit(solution)/shard_map/wave/pallas_call | solution.py:429
  25.9 14.1 %all-to-all-start.1 = ((f32[256,1,128]{2,1,0:T(1,128)}), f32[256,1,128]{2,1,0:T(1,128)S(1)}, u32[]{:S(2)}, u32[]{:S(2)}) async-start(f32[256,1,128]{2,1,0:T(1,128)} %bitcast.13), calls=%async_computation.1 | async-start | bytes 262144 | tf_op jit(solution)/shard_map/all_to_all | solution.py:437
  40.0 0.6 slots.1
  40.7 0.0 copy-start.2
  40.7 3.4 %copy-done.2 = bf16[512,64,128]{2,1,0:T(8,128)(2,1)S(1)} copy-done((bf16[512,64,128]{2,1,0:T(8,128)(2,1)S(1)}, bf16[512,64,128]{2,1,0:T(8,128)(2,1)}, u32[]{:S(2)}) %copy-start.2) | copy-done | bytes 8388632
  44.1 5.7 %send.1 = f32[2048,128]{1,0:T(8,128)} custom-call(f32[512,128]{1,0:T(8,128)S(1)} %bitcast.25, f32[2048,128]{1,0:T(8,128)S(1)} %bitcast.20, f32[224,128]{1,0:T(8,128)S(1)} %collective-permute-done.x_low, f32[224,128]{1,0:T(8,128)S(1)} %collective-permute-done.1.x_high, f32[96,128]{1,0:T(8,128)S(1)} %collective-permute-done.2.y_low, ...), custom_call_target="tpu_custom_call" | custom-call | flops 268435456 | bytes 16777216 | tf_op jit(solution)/shard_map/send/pallas_call | solution.py:404
  49.7 3.1 %all-to-all-done.1 = f32[256,1,128]{2,1,0:T(1,128)S(1)} async-done(((f32[256,1,128]{2,1,0:T(1,128)}), f32[256,1,128]{2,1,0:T(1,128)S(1)}, u32[]{:S(2)}, u32[]{:S(2)}) %all-to-all-start.1) | async-done | bytes 131104 | tf_op jit(solution)/shard_map/all_to_all | solution.py:437
  52.9 11.3 %all-to-all-start = ((f32[128,16,128]{2,1,0:T(8,128)}), f32[128,16,128]{2,1,0:T(8,128)S(1)}, u32[]{:S(2)}, u32[]{:S(2)}) async-start(f32[128,16,128]{2,1,0:T(8,128)} %bitcast.8), calls=%async_computation | async-start | bytes 2097152 | tf_op jit(solution)/shard_map/all_to_all | solution.py:423
  64.2 2.7 %les.1 = f32[2560,128]{1,0:T(8,128)} custom-call(f32[512,128]{1,0:T(8,128)S(1)} %bitcast.26, f32[2048,128]{1,0:T(8,128)S(1)} %bitcast.21, f32[224,128]{1,0:T(8,128)S(1)} %collective-permute-done.x_low, f32[224,128]{1,0:T(8,128)S(1)} %collective-permute-done.1.x_high, f32[96,128]{1,0:T(8,128)S(1)} %collective-permute-done.2.y_low, ...), custom_call_target="tpu_custom_call" | custom-call | flops 8388608 | bytes 4194304 | tf_op jit(solution)/shard_map/les/pallas_call | solution.py:441
  66.9 28.5 %all-to-all-done = f32[128,16,128]{2,1,0:T(8,128)S(1)} async-done(((f32[128,16,128]{2,1,0:T(8,128)}), f32[128,16,128]{2,1,0:T(8,128)S(1)}, u32[]{:S(2)}, u32[]{:S(2)}) %all-to-all-start) | async-done | bytes 1048608 | tf_op jit(solution)/shard_map/all_to_all | solution.py:423
  95.4 1.4 %finish.1 = (f32[512,128]{1,0:T(8,128)}, f32[1,128]{1,0:T(1,128)}) custom-call(f32[2048,128]{1,0:T(8,128)S(1)} %bitcast.23, f32[512,128]{1,0:T(8,128)S(1)} %get-tuple-element.23.base, f32[256,128]{1,0:T(8,128)S(1)} %bitcast.29), custom_call_target="tpu_custom_call" | custom-call | flops 268435456 | bytes 3145728 | tf_op jit(solution)/shard_map/finish/pallas_call | solution.py:443
  (18 shorter events, 0.0 us)
Async XLA Ops:
  0.6 23.9 %copy-start.7 = (s32[128]{0:T(128)S(1)}, s32[128]{0:T(128)}, u32[]{:S(2)}) copy-start(s32[128]{0:T(128)} %param.18) | copy-start | bytes 1540
  0.6 39.4 %copy-start.8 = (s32[512,1]{0,1:T(1,128)S(1)}, s32[512,1]{0,1:T(1,128)}, u32[]{:S(2)}) copy-start(s32[512,1]{0,1:T(1,128)} %param.13) | copy-start | bytes 6148
  0.7 39.4 %copy-start.9 = (s32[512]{0:T(512)S(1)}, s32[512]{0:T(512)}, u32[]{:S(2)}) copy-start(s32[512]{0:T(512)} %param.15) | copy-start | bytes 6148
  0.7 1.2 %copy-start = (f32[4,16,32,128]{3,2,1,0:T(8,128)S(1)}, f32[4,16,32,128]{3,2,1,0:T(8,128)}, u32[]{:S(2)}) copy-start(f32[4,16,32,128]{3,2,1,0:T(8,128)} %param.11) | copy-start | bytes 3145732
  1.9 0.9 copy-start.3
  2.9 0.9 copy-start.5
  3.8 20.8 %copy-start.6 = (f32[128,128]{1,0:T(8,128)S(1)}, f32[128,128]{1,0:T(8,128)}, u32[]{:S(2)}) copy-start(f32[128,128]{1,0:T(8,128)} %far.1) | copy-start | bytes 196612
  3.8 36.2 %copy-start.10 = (s32[512]{0:T(512)S(1)}, s32[512]{0:T(512)}, u32[]{:S(2)}) copy-start(s32[512]{0:T(512)} %param.16) | copy-start | bytes 6148
  3.8 36.8 %copy-start.1 = (f32[4,16,32,128]{3,2,1,0:T(8,128)S(1)}, f32[4,16,32,128]{3,2,1,0:T(8,128)}, u32[]{:S(2)}) copy-start(f32[4,16,32,128]{3,2,1,0:T(8,128)} %param.11) | copy-start | bytes 3145732
  3.8 36.8 %copy-start.4 = (f32[16,32,128]{2,1,0:T(8,128)S(1)}, f32[16,32,128]{2,1,0:T(8,128)}, u32[]{:S(2)}) copy-start(f32[16,32,128]{2,1,0:T(8,128)} %param.10) | copy-start | bytes 786436
  5.6 18.9 %collective-permute-start = (f32[224,128]{1,0:T(8,128)S(1)}, f32[224,128]{1,0:T(8,128)S(1)}, u32[]{:S(2)}, u32[]{:S(2)}) collective-permute-start(f32[224,128]{1,0:T(8,128)S(1)} %get-tuple-element.15), channel_id=1, source_target_pairs={{0,16},{16,32},{32,48},{48,64},{64,80},{80,96},{96,112},{1,17},{17... | collective-permute-start | bytes 344072 | tf_op jit(solution)/shard_map/ppermute | solution.py:360
  10.1 14.4 %collective-permute-start.1 = (f32[224,128]{1,0:T(8,128)S(1)}, f32[224,128]{1,0:T(8,128)S(1)}, u32[]{:S(2)}, u32[]{:S(2)}) collective-permute-start(f32[224,128]{1,0:T(8,128)S(1)} %get-tuple-element.16), channel_id=1, source_target_pairs={{16,0},{32,16},{48,32},{64,48},{80,64},{96,80},{112,96},{17,1},{33... | collective-permute-start | bytes 344072 | tf_op jit(solution)/shard_map/ppermute | solution.py:360
  12.1 9.0 %collective-permute-start.2 = (f32[96,128]{1,0:T(8,128)S(1)}, f32[96,128]{1,0:T(8,128)S(1)}, u32[]{:S(2)}, u32[]{:S(2)}) collective-permute-start(f32[96,128]{1,0:T(8,128)S(1)} %get-tuple-element.17), channel_id=1, source_target_pairs={{0,1},{1,2},{2,3},{3,4},{4,5},{5,6},{6,7},{7,8},{8,9},{9,10},{10,1... | collective-permute-start | bytes 147464 | tf_op jit(solution)/shard_map/ppermute | solution.py:360
  17.0 7.6 %collective-permute-start.3 = (f32[96,128]{1,0:T(8,128)S(1)}, f32[96,128]{1,0:T(8,128)S(1)}, u32[]{:S(2)}, u32[]{:S(2)}) collective-permute-start(f32[96,128]{1,0:T(8,128)S(1)} %get-tuple-element.18), channel_id=1, source_target_pairs={{1,0},{2,1},{3,2},{4,3},{5,4},{6,5},{7,6},{8,7},{9,8},{10,9},{11,1... | collective-permute-start | bytes 147464 | tf_op jit(solution)/shard_map/ppermute | solution.py:360
  18.3 2.8 %collective-permute-start.4 = (f32[24,128]{1,0:T(8,128)S(1)}, f32[24,128]{1,0:T(8,128)S(1)}, u32[]{:S(2)}, u32[]{:S(2)}) collective-permute-start(f32[24,128]{1,0:T(8,128)S(1)} %get-tuple-element.19), channel_id=1, source_target_pairs={{0,128},{128,0},{1,129},{129,1},{2,130},{130,2},{3,131},{131,3},{4... | collective-permute-start | bytes 36872 | tf_op jit(solution)/shard_map/ppermute | solution.py:389
  25.9 26.9 %all-to-all-start.1 = ((f32[256,1,128]{2,1,0:T(1,128)}), f32[256,1,128]{2,1,0:T(1,128)S(1)}, u32[]{:S(2)}, u32[]{:S(2)}) async-start(f32[256,1,128]{2,1,0:T(1,128)} %bitcast.13), calls=%async_computation.1 | async-start | bytes 262144 | tf_op jit(solution)/shard_map/all_to_all | solution.py:437
  40.7 3.4 %copy-start.2 = (bf16[512,64,128]{2,1,0:T(8,128)(2,1)S(1)}, bf16[512,64,128]{2,1,0:T(8,128)(2,1)}, u32[]{:S(2)}) copy-start(bf16[512,64,128]{2,1,0:T(8,128)(2,1)} %param.14) | copy-start | bytes 25165828
  52.9 42.5 %all-to-all-start = ((f32[128,16,128]{2,1,0:T(8,128)}), f32[128,16,128]{2,1,0:T(8,128)S(1)}, u32[]{:S(2)}, u32[]{:S(2)}) async-start(f32[128,16,128]{2,1,0:T(8,128)} %bitcast.8), calls=%async_computation | async-start | bytes 2097152 | tf_op jit(solution)/shard_map/all_to_all | solution.py:423

commit v2 on v1

v2 whole, which is shorter than its diff:
```python
import jax
import jax.numpy as jnp
from jax import lax
from jax.experimental import pallas as pl
from jax.experimental.pallas import tpu as pltpu
from jax.sharding import PartitionSpec as P

LES_STEP = 0.2
WAVE_STEP = 0.25
CAP = 10
ROWS = 17
F32 = jnp.float32
BF16 = jnp.bfloat16
ALL = ("sec", "gx", "row")
MIB = 1 << 20


def iota(shape, dim):
    return lax.broadcasted_iota(jnp.int32, shape, dim)


def as_column(line):
    return jnp.transpose(jnp.broadcast_to(line, (128, 128)))


def edge_line(block, high, eye):
    column = jnp.where(high, block[:, 127:128], block[:, 0:1])
    return jnp.sum(jnp.where(eye, column, 0.0), axis=0, keepdims=True)


def safe(density):
    return jnp.where(density == 0.0, 1.0, density)


def down(plane, halo):
    return jnp.where(iota(plane.shape, 0) == 0, halo, pltpu.roll(plane, 1, 0))


def up(plane, halo):
    last = plane.shape[0] - 1
    return jnp.where(iota(plane.shape, 0) == last, halo, pltpu.roll(plane, last, 0))


def derive_z(plane, halo, sec):
    lane = iota(plane.shape, 1)
    before = jnp.where(lane == 0, jnp.where(sec == 1, halo, 0.0), pltpu.roll(plane, 1, 1))
    after = jnp.where(lane == 127, jnp.where(sec == 0, halo, 0.0), pltpu.roll(plane, 127, 1))
    return 0.5 * (after - before)


def even(axis):
    return lax.rem(lax.axis_index(axis), 2) == 0


def pack_kernel(
    rho_hbm, rest_hbm, wave_hbm, x_even, x_odd, y_even, y_odd, z_face, rho, rest, wave, landed
):
    copies = [
        pltpu.make_async_copy(rho_hbm, rho, landed.at[0]),
        pltpu.make_async_copy(rest_hbm, rest, landed.at[1]),
        pltpu.make_async_copy(wave_hbm, wave, landed.at[2]),
    ]
    for copy in copies:
        copy.start()
    high = lax.axis_index("sec") == 0
    x_index, y_index = even("gx"), even("row")
    eye = iota((128, 128), 0) == iota((128, 128), 1)
    copies[0].wait()
    for piece in range(4):
        z_face[piece : piece + 1] = edge_line(rho[piece * 128 : piece * 128 + 128], high, eye)
    copies[2].wait()
    z_face[20:21] = edge_line(wave[0:128], high, eye)
    z_face[21:22] = edge_line(wave[384:512], high, eye)
    z_face[22:24] = jnp.zeros((2, 128), F32)
    copies[1].wait()
    for piece in range(16):
        z_face[piece + 4 : piece + 5] = edge_line(rest[piece * 128 : piece * 128 + 128], high, eye)
    for target, upper in ((x_even, x_index), (x_odd, jnp.logical_not(x_index))):
        at = pl.multiple_of(jnp.where(upper, 480, 0), 32)
        wave_at = pl.multiple_of(jnp.where(upper, 112, 0), 16)
        target[0:32] = rho[pl.ds(at, 32)]
        for part in range(4):
            target[32 * part + 32 : 32 * part + 64] = rest[pl.ds(part * 512 + at, 32)]
            target[160 + 16 * part : 176 + 16 * part] = wave[pl.ds(part * 128 + wave_at, 16)]
    for target, upper in ((y_even, y_index), (y_odd, jnp.logical_not(y_index))):
        def pick(ref, start, count, width):
            low = ref[pl.ds(start, count, stride=width)]
            return jnp.where(upper, ref[pl.ds(start + width - 1, count, stride=width)], low)

        target[0:16] = pick(rho, 0, 16, 32)
        for part in range(4):
            target[16 * part + 16 : 16 * part + 32] = pick(rest, part * 512, 16, 32)
        target[80:88] = pick(wave, 0, 8, 16)
        target[88:96] = pick(wave, 256, 8, 16)


def sides(x_even, x_odd, y_even, y_odd):
    x_index, y_index = even("gx"), even("row")
    return (
        jnp.where(x_index, x_odd[...], x_even[...]),
        jnp.where(x_index, x_even[...], x_odd[...]),
        jnp.where(y_index, y_odd[...], y_even[...]),
        jnp.where(y_index, y_even[...], y_odd[...]),
    )


def slot_kernel(owner, counts, patch, slots, valid, patches):
    below = iota((128, 128), 0) < iota((128, 128), 1)
    target = iota((128, 128), 0) * 16
    lane = iota((128, 128), 1)
    lines = [owner[piece : piece + 1].astype(F32) for piece in range(4)]
    columns = [as_column(line) for line in lines]
    for piece in range(4):
        rank = jnp.zeros((1, 128), F32)
        for other in range(piece + 1):
            same = columns[other] == lines[piece]
            if other == piece:
                same = same & below
            rank = rank + jnp.sum(same.astype(F32), axis=0, keepdims=True)
        code = (lines[piece] * 16.0 + rank).astype(jnp.int32)
        here = slice(piece * 128, piece * 128 + 128)
        for slot in range(CAP):
            hit = (target + slot) == code
            slots[slot * 128 : slot * 128 + 128, here] = hit.astype(F32).astype(BF16)
        limit = as_column(counts[piece : piece + 1].astype(F32))
        valid[here] = (lane.astype(F32) < limit).astype(F32)
        patches[here] = as_column(patch[piece : piece + 1].astype(F32)).astype(BF16)


def payload_kernel(
    rho, momentum, x_even, x_odd, y_even, y_odd, z_face, valid, weights,
    payload, speed, z_speed, y_speed, held, landed,
):
    steps = landed.shape[0]
    lines = 512 // steps
    sec = lax.axis_index("sec")

    def fetch(step):
        rows = pl.ds(pl.multiple_of(step * (lines * 64), 64), lines * 64)
        return pltpu.make_async_copy(weights.at[rows], held.at[rows], landed.at[step])

    for step in range(steps):
        fetch(step).start()
    x_low, x_high, y_low, y_high = sides(x_even, x_odd, y_even, y_odd)
    for side, face in enumerate((y_low, y_high)):
        for k, part in enumerate((0, 2)):
            y_speed[2 * side + k] = face[16 * part + 16 : 16 * part + 32] / safe(face[0:16])
    for part in range(3):
        speed[part, 32:544] = momentum[part * 512 : part * 512 + 512] / rho[...]
        for at, face in ((0, x_low), (544, x_high)):
            speed[part, at : at + 32] = (
                face[32 * part + 32 : 32 * part + 64] / safe(face[0:32])
            )
    for part in range(2):
        edge = z_face[4 * part + 4 : 4 * part + 8] / safe(z_face[0:4])
        for piece in range(4):
            z_speed[part, piece * 128 : piece * 128 + 128] = as_column(edge[piece : piece + 1])

    group = iota((16, 128), 0)
    half = iota((16, 128), 1) < 64
    keep = [(group // 4 == part).astype(F32).astype(BF16) for part in range(4)]
    wide = iota((16, 256), 1) // 64 == iota((16, 256), 0) % 4

    @pl.loop(0, steps)
    def _(step):
        fetch(step).wait()
        for plane in range(lines // 32):
            x = step * (lines // 32) + plane
            at = pl.multiple_of(x * 32, 32)
            v = [speed[part, pl.ds(at + 32, 32)] for part in range(3)]
            v_before = [speed[part, pl.ds(at, 32)] for part in range(3)]
            v_after = [speed[part, pl.ds(at + 64, 32)] for part in range(3)]
            y_before = {part: y_speed[part // 2, pl.ds(x, 1)] for part in (0, 2)}
            y_after = {part: y_speed[2 + part // 2, pl.ds(x, 1)] for part in (0, 2)}
            along = {part: 0.5 * (v_after[part] - v_before[part]) for part in (1, 2)}
            across = {
                part: 0.5 * (up(v[part], y_after[part]) - down(v[part], y_before[part]))
                for part in (0, 2)
            }
            deep = {part: derive_z(v[part], z_speed[part, pl.ds(at, 32)], sec) for part in (0, 1)}
            swirl_x = across[2] - deep[1]
            swirl_y = deep[0] - along[2]
            swirl_z = along[1] - across[0]
            mask = valid[pl.ds(at, 32)]
            lamb = [
                ((swirl_y * v[2] - swirl_z * v[1]) * mask).astype(BF16),
                ((swirl_z * v[0] - swirl_x * v[2]) * mask).astype(BF16),
                ((swirl_x * v[1] - swirl_y * v[0]) * mask).astype(BF16),
            ]
            for part in range(2):
                rows = slice(part * 16, part * 16 + 16)
                left = jnp.concatenate(
                    [
                        jnp.concatenate([lamb[c][rows] * keep[k] for k in range(4)], axis=1)
                        for c in range(3)
                    ],
                    axis=0,
                )
                first = (x * 32 + part * 16) * 64
                right = jnp.concatenate(
                    [
                        held[pl.ds(pl.multiple_of(first + 256 * k, 256), 256)]
                        for k in range(4)
                    ],
                    axis=1,
                )
                product = lax.dot_general(
                    left, right, (((1,), (1,)), ((), ())), preferred_element_type=F32
                )
                folded = []
                for c in range(3):
                    picked = jnp.where(wide, product[c * 16 : c * 16 + 16], 0.0)
                    both = picked[:, 0:128] + picked[:, 128:256]
                    folded.append(both + pltpu.roll(both, 64, 1))
                pair = jnp.where(half, folded[0], folded[1])
                pair_top = pair.astype(BF16)
                pair_rest = (pair - pair_top.astype(F32)).astype(BF16)
                single_top = folded[2].astype(BF16).astype(F32)
                single = jnp.where(half, single_top, folded[2] - single_top).astype(BF16)
                here = pl.ds(pl.multiple_of(at + part * 16, 16), 16)
                payload[here, 0:128] = pair_top
                payload[here, 128:256] = pair_rest
                payload[here, 256:384] = single


def place_kernel(slots, payload, patches, share, other, send):
    lane = iota((128, 128), 1)
    numbers = jnp.zeros((128, 128), F32)
    kept = None
    values = jnp.concatenate([payload[...], patches[...]], axis=1)
    for slot in range(CAP):
        placed = jnp.dot(
            slots[slot * 128 : slot * 128 + 128], values, preferred_element_type=F32
        )
        send[pl.ds(slot, 128, stride=ROWS)] = placed[:, 0:128] + placed[:, 128:256]
        third = placed[:, 256:384]
        third = third + pltpu.roll(third, 64, 1)
        if slot % 2 == 0:
            kept = third
        else:
            send[pl.ds(CAP + slot // 2, 128, stride=ROWS)] = jnp.where(lane < 64, kept, third)
        numbers = jnp.where(lane == slot, placed[:, 384:512], numbers)
    send[pl.ds(CAP * 3 // 2, 128, stride=ROWS)] = numbers
    both = share[0:1] + other[0:1]
    send[pl.ds(CAP * 3 // 2 + 1, 128, stride=ROWS)] = jnp.broadcast_to(both, (128, 128))


def wave_kernel(
    tile_class, wave, x_even, x_odd, y_even, y_odd, z_face, samples, far, base, share
):
    sec = lax.axis_index("sec")
    x_low, x_high, y_low, y_high = sides(x_even, x_odd, y_even, y_odd)
    level = tile_class[0, 0].astype(F32)
    mean_flow = 0.1 + 0.3 * level
    stiffness = 1.0 + 0.25 * level
    z_pressure = as_column(z_face[20:21])
    z_speed = as_column(z_face[21:22])
    for x in range(8):
        def row(part, at):
            start = part * 128 + at * 16
            if at < 0:
                return x_low[160 + 16 * part : 176 + 16 * part]
            if at > 7:
                return x_high[160 + 16 * part : 176 + 16 * part]
            return wave[start : start + 16]

        now = [row(part, x) for part in range(4)]
        along = [0.5 * (row(part, x + 1) - row(part, x - 1)) for part in range(4)]
        across = [
            0.5
            * (
                up(now[part], y_high[80 + 8 * k + x : 81 + 8 * k + x])
                - down(now[part], y_low[80 + 8 * k + x : 81 + 8 * k + x])
            )
            for k, part in enumerate((0, 2))
        ]
        here = slice(x * 16, x * 16 + 16)
        deep = [derive_z(now[0], z_pressure[here], sec), derive_z(now[3], z_speed[here], sec)]
        divergence = along[1] + across[1] + deep[1]
        base[here] = now[0] - WAVE_STEP * (mean_flow * along[0] + stiffness * divergence)
        for part, gradient in ((1, along[0]), (2, across[0]), (3, deep[0])):
            base[part * 128 + x * 16 : part * 128 + x * 16 + 16] = now[part] - WAVE_STEP * (
                mean_flow * along[part] + gradient
            )
    index = samples[...]
    line, cell = index // 128, index % 128
    picks = (iota((128, 128), 0) == line).astype(F32)
    columns = lax.dot_general(
        base[0:128], picks, (((0,), (0,)), ((), ())),
        precision=lax.Precision.HIGHEST, preferred_element_type=F32,
    )
    values = jnp.sum(
        jnp.where(iota((128, 128), 0) == cell, columns, 0.0), axis=0, keepdims=True
    )
    share[...] = lax.dot_general(
        jnp.broadcast_to(values, (8, 128)), far[...], (((1,), (1,)), ((), ())),
        precision=lax.Precision.HIGHEST, preferred_element_type=F32,
    )


def les_kernel(rho, rest, x_even, x_odd, y_even, y_odd, z_face, out):
    sec = lax.axis_index("sec")
    x_low, x_high, y_low, y_high = sides(x_even, x_odd, y_even, y_odd)
    lane = iota((32, 128), 1)
    z_rho = safe(z_face[0:4])
    z_v = z_face[12:16] / z_rho
    y_low_v = y_low[32:48] / safe(y_low[0:16])
    y_high_v = y_high[32:48] / safe(y_high[0:16])
    x_low_v = x_low[32:64] / safe(x_low[0:32])
    x_high_v = x_high[32:64] / safe(x_high[0:32])
    for part in range(5):
        def state(x):
            if part == 0:
                return rho[x * 32 : x * 32 + 32]
            return rest[part * 512 - 512 + x * 32 : part * 512 - 512 + x * 32 + 32]

        z_flux = z_face[4 * part : 4 * part + 4] * z_v
        y_low_flux = y_low[16 * part : 16 * part + 16] * y_low_v
        y_high_flux = y_high[16 * part : 16 * part + 16] * y_high_v
        for x in range(16):
            density = rho[x * 32 : x * 32 + 32]
            now = state(x)

            def stream(at):
                if at < 0:
                    return x_low[32 * part : 32 * part + 32] * x_low_v
                if at > 15:
                    return x_high[32 * part : 32 * part + 32] * x_high_v
                return state(at) * (rest[at * 32 : at * 32 + 32] / rho[at * 32 : at * 32 + 32])

            along = 0.5 * (stream(x + 1) - stream(x - 1))
            side = now * (rest[512 + x * 32 : 512 + x * 32 + 32] / density)
            across = 0.5 * (
                up(side, y_high_flux[x : x + 1]) - down(side, y_low_flux[x : x + 1])
            )
            depth = now * (rest[1024 + x * 32 : 1024 + x * 32 + 32] / density)
            if x % 4 == 0:
                z_column = as_column(z_flux[x // 4 : x // 4 + 1])
            deep = derive_z(depth, z_column[x % 4 * 32 : x % 4 * 32 + 32], sec)
            start = part * 512 + x * 32
            out[start : start + 32] = now - LES_STEP * (along + across + deep)


def finish_kernel(arrived, base, out, far):
    names = jnp.transpose(arrived[pl.ds(CAP * 3 // 2, 128, stride=ROWS)])
    place = iota((256, 128), 0)
    patch = (place % 128 * 2 + place // 128).astype(F32)
    half = iota((128, 128), 1) < 64
    total = jnp.zeros((256, 512), F32)
    for pair in range(CAP // 2):
        third = arrived[pl.ds(CAP + pair, 128, stride=ROWS)]
        left, right = [], []
        for slot in (2 * pair, 2 * pair + 1):
            left.append((patch == names[slot : slot + 1]).astype(F32).astype(BF16))
            both = arrived[pl.ds(slot, 128, stride=ROWS)]
            one = jnp.where(half == (slot % 2 == 0), third, 0.0)
            row = []
            for value in (both, one):
                top = value.astype(BF16)
                row += [top, (value - top.astype(F32)).astype(BF16)]
            right.append(jnp.concatenate(row, axis=1))
        total = total + jnp.dot(
            jnp.concatenate(left, axis=1),
            jnp.concatenate(right, axis=0),
            preferred_element_type=F32,
        )
    both = total[:, 0:128] + total[:, 128:256]
    third = total[:, 256:384] + total[:, 384:512]
    third = third + pltpu.roll(third, 64, 1)
    even, odd = both[0:128], both[128:256]
    source = [
        jnp.where(half, even, pltpu.roll(odd, 64, 1)),
        jnp.where(half, pltpu.roll(even, 64, 1), odd),
        jnp.where(half, third[0:128], third[128:256]),
    ]
    out[0:128] = base[0:128]
    for part in range(3):
        here = slice(part * 128 + 128, part * 128 + 256)
        out[here] = base[here] - WAVE_STEP * source[part]
    shares = arrived[pl.ds(CAP * 3 // 2 + 1, 128, stride=ROWS)]
    far[...] = jnp.sum(shares, axis=0, keepdims=True)


def call(kernel, outs, flops, moved, limit=16, **more):
    return pl.pallas_call(
        kernel,
        out_shape=[jax.ShapeDtypeStruct(shape, kind) for shape, kind in outs],
        compiler_params=pltpu.CompilerParams(vmem_limit_bytes=limit * MIB),
        cost_estimate=pl.CostEstimate(flops=flops, bytes_accessed=moved, transcendentals=0),
        **more,
    )


def exchange(face, axis, first):
    pairs = []
    for low in range(first, lax.axis_size(axis) - 1, 2):
        pairs += [(low, low + 1), (low + 1, low)]
    return lax.ppermute(face, axis, pairs)


def per_device(
    les_density,
    les_rest,
    acoustic,
    block_owner,
    block_weights,
    block_counts,
    block_patch,
    tile_class,
    sample_index,
    far_kernel,
):
    rho = les_density.reshape(512, 128)
    rest = les_rest.reshape(2048, 128)
    wave = acoustic.reshape(512, 128)
    weights = block_weights.reshape(512 * 64, 128)
    hbm = pl.BlockSpec(memory_space=pltpu.HBM)
    vmem = pl.BlockSpec(memory_space=pltpu.VMEM)
    smem = pl.BlockSpec(memory_space=pltpu.SMEM)
    pinned = lambda x: pltpu.with_memory_space_constraint(x, pltpu.HBM)
    with jax.named_scope("pack"):
        faces = call(
            pack_kernel,
            [((224, 128), F32)] * 2 + [((96, 128), F32)] * 2 + [((24, 128), F32)],
            1 << 20, 2 << 20,
            in_specs=[hbm] * 3,
            scratch_shapes=[
                pltpu.VMEM((512, 128), F32),
                pltpu.VMEM((2048, 128), F32),
                pltpu.VMEM((512, 128), F32),
                pltpu.SemaphoreType.DMA((3,)),
            ],
        )(pinned(rho), pinned(rest), pinned(wave))
    halos = [
        exchange(faces[0], "gx", 0),
        exchange(faces[1], "gx", 1),
        exchange(faces[2], "row", 0),
        exchange(faces[3], "row", 1),
        exchange(faces[4], "sec", 0),
    ]
    with jax.named_scope("slots"):
        slots, valid, patches = call(
            slot_kernel,
            [((CAP * 128, 512), BF16), ((512, 128), F32), ((512, 128), BF16)],
            1 << 22, 2 << 20,
        )(
            block_owner.reshape(4, 128),
            block_counts.reshape(4, 128),
            block_patch.reshape(4, 128),
        )
    with jax.named_scope("wave"):
        base, share = call(
            wave_kernel,
            [((512, 128), F32), ((8, 128), F32)],
            1 << 24, 2 << 20,
            in_specs=[smem] + [vmem] * 8,
        )(
            tile_class.reshape(1, 1), wave, *halos, sample_index.reshape(1, 128), far_kernel
        )
    other = exchange(share, "sec", 0)
    with jax.named_scope("payload"):
        (payload,) = call(
            payload_kernel,
            [((512, 384), BF16)],
            1 << 27, 16 << 20, 32,
            in_specs=[vmem] * 8 + [hbm],
            scratch_shapes=[
                pltpu.VMEM((3, 576, 128), F32),
                pltpu.VMEM((2, 512, 128), F32),
                pltpu.VMEM((4, 16, 128), F32),
                pltpu.VMEM((512 * 64, 128), BF16),
                pltpu.SemaphoreType.DMA((4,)),
            ],
        )(rho, rest, *halos, valid, pinned(weights))
    with jax.named_scope("place"):
        (send,) = call(place_kernel, [((128 * ROWS, 128), F32)], 1 << 28, 3 << 20)(
            slots, payload, patches, share, other
        )
    arrived = lax.all_to_all(
        send.reshape(128, 1, ROWS * 128), ("gx", "row"), split_axis=0, concat_axis=0, tiled=True
    )
    with jax.named_scope("les"):
        (les_next,) = call(les_kernel, [((2560, 128), F32)], 1 << 23, 4 << 20)(rho, rest, *halos)
    with jax.named_scope("finish"):
        wave_next, far_field = call(
            finish_kernel, [((512, 128), F32), ((1, 128), F32)], 1 << 28, 3 << 20,
        )(arrived.reshape(128 * ROWS, 128), base)
    return (
        les_next.reshape(5, 16, 32, 128),
        wave_next.reshape(4, 8, 16, 128),
        far_field.reshape(128),
    )


def solution(mesh):
    in_specs = (
        P("gx", "row", "sec"),
        P(None, "gx", "row", "sec"),
        P(None, "gx", "row", "sec"),
        P(("sec", "gx", "row"), None),
        P(("sec", "gx", "row"), None, None),
        P(("sec", "gx", "row")),
        P(("sec", "gx", "row")),
        P("sec", "gx", "row"),
        P(("sec", "gx", "row")),
        P(None, ("sec", "gx", "row")),
    )
    out_specs = (P(None, "gx", "row", "sec"), P(None, "gx", "row", "sec"), P())
    return jax.shard_map(
        per_device, mesh=mesh, in_specs=in_specs, out_specs=out_specs, check_vma=False
    )
```

time: 97.2 us -> 77.3 us (0.80)
  starting transfers between devices: 39.7 us -> 29.4 us
  local copies, waits for them, and re-layouts: 6.54 us -> 0.86 us
  waiting for transfers between devices: 35.6 us -> 30.1 us
  Pallas kernels: 13.5 us -> 15.2 us
    all_to_all x2 -> x1, starting transfers between devices: 25.4 us -> 18.1 us  [per_device(): lax.all_to_all(send.reshape(128, 1, ROWS * 128), ('gx', 'row'), split_axi...]
    unnamed x22 -> x16, local copies, waits for them, and re-layouts: 6.54 us -> 0.86 us
    ppermute x5 -> x6, waiting for transfers between devices: 3.92 us -> 0.02 us  [exchange(): return lax.ppermute(face, axis, pairs)]
    ppermute x5 -> x6, starting transfers between devices: 14.3 us -> 11.3 us  [exchange(): return lax.ppermute(face, axis, pairs)]
    all_to_all x2 -> x1, waiting for transfers between devices: 31.6 us -> 30.1 us  [per_device(): lax.all_to_all(send.reshape(128, 1, ROWS * 128), ('gx', 'row'), split_axi...]
    pallas_call x1, Pallas kernels: 1.81 us -> 3.02 us  [per_device(): call(pack_kernel, [((224, 128), F32)] * 2 + [((96, 128), F32)] * 2 + [((2...]
    pallas_call x2 -> x3, Pallas kernels: 7.03 us -> 7.56 us  [the longest x1 4.94 us: per_device(): call(payload_kernel, [((512, 384), BF16)], 1 << 27, 16 << 20, 32, in_spec...]
  transfers between devices with their start and end apart: 7 -> 7, of which waited for: 4 -> 1; matrix products, arithmetic and copies ran while one was open for 0% -> 0% of each run, Pallas kernels for 3% -> 11%
where the time goes in v2:
time: 77.3 us; the launch traced here: 77 us
  waiting for transfers between devices  30.1 us (39%)
  starting transfers between devices  29.4 us (38%)
  Pallas kernels  15.2 us (20%)
  between operations  1.49 us (2%)
  local copies, waits for them, and re-layouts  0.86 us (1%)
    all_to_all x1, waiting for transfers between devices, per_device(): lax.all_to_all(send.reshape(128, 1, ROWS * 128), ('gx', 'row'), split_axi...  30.1 us
    all_to_all x1, starting transfers between devices, per_device(): lax.all_to_all(send.reshape(128, 1, ROWS * 128), ('gx', 'row'), split_axi...  18.1 us
    ppermute x6, starting transfers between devices, exchange(): return lax.ppermute(face, axis, pairs)  11.3 us
    pallas_call x1, Pallas kernels, per_device(): call(payload_kernel, [((512, 384), BF16)], 1 << 27, 16 << 20, 32, in_spec...  4.94 us
    pallas_call x1, Pallas kernels, per_device(): call(pack_kernel, [((224, 128), F32)] * 2 + [((96, 128), F32)] * 2 + [((2...  3.02 us
    pallas_call x1, Pallas kernels, per_device(): call(les_kernel, [((2560, 128), F32)], 1 << 23, 4 << 20)(rho, rest, *halos)  2.69 us
    pallas_call x1, Pallas kernels, per_device(): call(place_kernel, [((128 * ROWS, 128), F32)], 1 << 28, 3 << 20)  1.94 us
  transfers between devices with their start and end apart: 7, of which 1 were waited for; matrix products, arithmetic and copies ran while one was open for 0% of the time, Pallas kernels for 11%

profile of v2, /device:TPU:1, one launch (start us, length us, event | category | flops | bytes accessed | tf_op | source)
XLA Modules:
  0.0 77.0 jit_solution(2850500066053072347)
XLA Ops:
  0.6 0.0 copy-start.1
  0.7 3.0 %pack.1 = (f32[224,128]{1,0:T(8,128)S(1)}, f32[224,128]{1,0:T(8,128)S(1)}, f32[96,128]{1,0:T(8,128)S(1)}, f32[96,128]{1,0:T(8,128)S(1)}, f32[24,128]{1,0:T(8,128)S(1)}) custom-call(f32[512,128]{1,0:T(8,128)} %bitcast.19, f32[2048,128]{1,0:T(8,128)} %bitcast.15, f32[512,128]{1,0:T(8,128)} %bitcast.22), custom_call_target="tpu_custom_call" | custom-call | flops 1048576 | bytes 2097152 | tf_op jit(solution)/shard_map/pack/pallas_call | solution.py:422
  3.7 3.3 %collective-permute-start = (f32[224,128]{1,0:T(8,128)S(1)}, f32[224,128]{1,0:T(8,128)S(1)}, u32[]{:S(2)}, u32[]{:S(2)}) collective-permute-start(f32[224,128]{1,0:T(8,128)S(1)} %get-tuple-element.15), channel_id=1, source_target_pairs={{0,16},{16,0},{32,48},{48,32},{64,80},{80,64},{96,112},{112,96},{1... | collective-permute-start | bytes 344072 | tf_op jit(solution)/shard_map/ppermute | solution.py:398
  7.1 1.9 %collective-permute-start.1 = (f32[224,128]{1,0:T(8,128)S(1)}, f32[224,128]{1,0:T(8,128)S(1)}, u32[]{:S(2)}, u32[]{:S(2)}) collective-permute-start(f32[224,128]{1,0:T(8,128)S(1)} %get-tuple-element.16), channel_id=1, source_target_pairs={{16,32},{32,16},{48,64},{64,48},{80,96},{96,80},{17,33},{33,17},{4... | collective-permute-start | bytes 344072 | tf_op jit(solution)/shard_map/ppermute | solution.py:398
  9.0 2.5 %collective-permute-start.2 = (f32[96,128]{1,0:T(8,128)S(1)}, f32[96,128]{1,0:T(8,128)S(1)}, u32[]{:S(2)}, u32[]{:S(2)}) collective-permute-start(f32[96,128]{1,0:T(8,128)S(1)} %get-tuple-element.17), channel_id=1, source_target_pairs={{0,1},{1,0},{2,3},{3,2},{4,5},{5,4},{6,7},{7,6},{8,9},{9,8},{10,11... | collective-permute-start | bytes 147464 | tf_op jit(solution)/shard_map/ppermute | solution.py:398
  11.4 0.7 collective-permute-start.3
  12.1 1.7 %collective-permute-start.4 = (f32[24,128]{1,0:T(8,128)S(1)}, f32[24,128]{1,0:T(8,128)S(1)}, u32[]{:S(2)}, u32[]{:S(2)}) collective-permute-start(f32[24,128]{1,0:T(8,128)S(1)} %get-tuple-element.19), channel_id=1, source_target_pairs={{0,128},{128,0},{1,129},{129,1},{2,130},{130,2},{3,131},{131,3},{4... | collective-permute-start | bytes 36872 | tf_op jit(solution)/shard_map/ppermute | solution.py:398
  14.5 0.6 slots.1
  15.1 0.0 collective-permute-done.4.z_face
  15.1 0.0 collective-permute-done.2.y_even
  15.1 0.0 collective-permute-done.3.y_odd
  15.1 0.0 collective-permute-done.x_even
  15.1 0.0 collective-permute-done.1.x_odd
  15.2 0.0 copy-start.3
  15.2 0.8 %copy-done.3 = f32[128,128]{1,0:T(8,128)S(1)} copy-done((f32[128,128]{1,0:T(8,128)S(1)}, f32[128,128]{1,0:T(8,128)}, u32[]{:S(2)}) %copy-start.3) | copy-done | bytes 65560
  16.0 0.7 wave.1
  16.7 1.2 %collective-permute-start.5 = (f32[8,128]{1,0:T(8,128)S(1)}, f32[8,128]{1,0:T(8,128)S(1)}, u32[]{:S(2)}, u32[]{:S(2)}) collective-permute-start(f32[8,128]{1,0:T(8,128)S(1)} %get-tuple-element.23.share), channel_id=1, source_target_pairs={{0,128},{128,0},{1,129},{129,1},{2,130},{130,2},{3,131},{131,3},{4... | collective-permute-start | bytes 12296 | tf_op jit(solution)/shard_map/ppermute | solution.py:398
  17.9 4.9 %payload.1 = bf16[512,384]{1,0:T(8,128)(2,1)S(1)} custom-call(f32[512,128]{1,0:T(8,128)S(1)} %bitcast.20, f32[2048,128]{1,0:T(8,128)S(1)} %bitcast.16, f32[224,128]{1,0:T(8,128)S(1)} %collective-permute-done.x_even, f32[224,128]{1,0:T(8,128)S(1)} %collective-permute-done.1.x_odd, f32[96,128]{1,0:T(8,128)S(1)} %collective-permute-done.2.y_even, ...), custom_call_target="tpu_custom_call" | custom-call | flops 134217728 | bytes 16777216 | tf_op jit(solution)/shard_map/payload/pallas_call | solution.py:462
  22.9 0.0 collective-permute-done.5.other
  22.9 1.9 %place.1 = f32[2176,128]{1,0:T(8,128)} custom-call(bf16[1280,512]{1,0:T(8,128)(2,1)S(1)} %get-tuple-element.20.slots, bf16[512,384]{1,0:T(8,128)(2,1)S(1)} %payload.1, bf16[512,128]{1,0:T(8,128)(2,1)S(1)} %get-tuple-element.22.patches, f32[8,128]{1,0:T(8,128)S(1)} %get-tuple-element.23.share, f32[8,128]{1,0:T(8,128)S(1)} %collective-permute-done.5.other), custom_call_target="tpu_custom_call" | custom-call | flops 268435456 | bytes 3145728 | tf_op jit(solution)/shard_map/place/pallas_call | solution.py:476
  24.8 18.1 %all-to-all-start = ((f32[128,1,2176]{2,1,0:T(1,128)}), f32[128,1,2176]{2,1,0:T(1,128)S(1)}, u32[]{:S(2)}, u32[]{:S(2)}) async-start(f32[128,1,2176]{2,1,0:T(1,128)} %bitcast.10), calls=%async_computation | async-start | bytes 2228224 | tf_op jit(solution)/shard_map/all_to_all | solution.py:479
  42.9 2.7 %les.1 = f32[2560,128]{1,0:T(8,128)} custom-call(f32[512,128]{1,0:T(8,128)S(1)} %bitcast.21, f32[2048,128]{1,0:T(8,128)S(1)} %bitcast.17, f32[224,128]{1,0:T(8,128)S(1)} %collective-permute-done.x_even, f32[224,128]{1,0:T(8,128)S(1)} %collective-permute-done.1.x_odd, f32[96,128]{1,0:T(8,128)S(1)} %collective-permute-done.2.y_even, ...), custom_call_target="tpu_custom_call" | custom-call | flops 8388608 | bytes 4194304 | tf_op jit(solution)/shard_map/les/pallas_call | solution.py:483
  45.6 30.1 %all-to-all-done = f32[128,1,2176]{2,1,0:T(1,128)S(1)} async-done(((f32[128,1,2176]{2,1,0:T(1,128)}), f32[128,1,2176]{2,1,0:T(1,128)S(1)}, u32[]{:S(2)}, u32[]{:S(2)}) %all-to-all-start) | async-done | bytes 1114144 | tf_op jit(solution)/shard_map/all_to_all | solution.py:479
  75.7 1.3 %finish.1 = (f32[512,128]{1,0:T(8,128)}, f32[1,128]{1,0:T(1,128)}) custom-call(f32[2176,128]{1,0:T(8,128)S(1)} %bitcast.18, f32[512,128]{1,0:T(8,128)S(1)} %get-tuple-element.24.base), custom_call_target="tpu_custom_call" | custom-call | flops 268435456 | bytes 3145728 | tf_op jit(solution)/shard_map/finish/pallas_call | solution.py:485
  (13 shorter events, 0.0 us)
Async XLA Ops:
  0.6 17.3 %copy-start.1 = (f32[16,32,128]{2,1,0:T(8,128)S(1)}, f32[16,32,128]{2,1,0:T(8,128)}, u32[]{:S(2)}) copy-start(f32[16,32,128]{2,1,0:T(8,128)} %param.10) | copy-start | bytes 786436
  0.6 17.3 %copy-start = (f32[4,16,32,128]{3,2,1,0:T(8,128)S(1)}, f32[4,16,32,128]{3,2,1,0:T(8,128)}, u32[]{:S(2)}) copy-start(f32[4,16,32,128]{3,2,1,0:T(8,128)} %param.11) | copy-start | bytes 3145732
  0.7 14.5 %copy-start.2 = (f32[4,8,16,128]{3,2,1,0:T(8,128)S(1)}, f32[4,8,16,128]{3,2,1,0:T(8,128)}, u32[]{:S(2)}) copy-start(f32[4,8,16,128]{3,2,1,0:T(8,128)} %param.12) | copy-start | bytes 786436
  0.7 13.8 %copy-start.5 = (s32[512,1]{0,1:T(1,128)S(1)}, s32[512,1]{0,1:T(1,128)}, u32[]{:S(2)}) copy-start(s32[512,1]{0,1:T(1,128)} %param.13) | copy-start | bytes 6148
  0.7 13.8 %copy-start.6 = (s32[512]{0:T(512)S(1)}, s32[512]{0:T(512)}, u32[]{:S(2)}) copy-start(s32[512]{0:T(512)} %param.15) | copy-start | bytes 6148
  0.7 13.8 %copy-start.7 = (s32[512]{0:T(512)S(1)}, s32[512]{0:T(512)}, u32[]{:S(2)}) copy-start(s32[512]{0:T(512)} %param.16) | copy-start | bytes 6148
  0.7 14.5 %copy-start.4 = (s32[128]{0:T(128)S(1)}, s32[128]{0:T(128)}, u32[]{:S(2)}) copy-start(s32[128]{0:T(128)} %param.18) | copy-start | bytes 1540
  3.7 11.4 %collective-permute-start = (f32[224,128]{1,0:T(8,128)S(1)}, f32[224,128]{1,0:T(8,128)S(1)}, u32[]{:S(2)}, u32[]{:S(2)}) collective-permute-start(f32[224,128]{1,0:T(8,128)S(1)} %get-tuple-element.15), channel_id=1, source_target_pairs={{0,16},{16,0},{32,48},{48,32},{64,80},{80,64},{96,112},{112,96},{1... | collective-permute-start | bytes 344072 | tf_op jit(solution)/shard_map/ppermute | solution.py:398
  7.1 8.1 %collective-permute-start.1 = (f32[224,128]{1,0:T(8,128)S(1)}, f32[224,128]{1,0:T(8,128)S(1)}, u32[]{:S(2)}, u32[]{:S(2)}) collective-permute-start(f32[224,128]{1,0:T(8,128)S(1)} %get-tuple-element.16), channel_id=1, source_target_pairs={{16,32},{32,16},{48,64},{64,48},{80,96},{96,80},{17,33},{33,17},{4... | collective-permute-start | bytes 344072 | tf_op jit(solution)/shard_map/ppermute | solution.py:398
  9.0 6.1 %collective-permute-start.2 = (f32[96,128]{1,0:T(8,128)S(1)}, f32[96,128]{1,0:T(8,128)S(1)}, u32[]{:S(2)}, u32[]{:S(2)}) collective-permute-start(f32[96,128]{1,0:T(8,128)S(1)} %get-tuple-element.17), channel_id=1, source_target_pairs={{0,1},{1,0},{2,3},{3,2},{4,5},{5,4},{6,7},{7,6},{8,9},{9,8},{10,11... | collective-permute-start | bytes 147464 | tf_op jit(solution)/shard_map/ppermute | solution.py:398
  11.4 3.7 %collective-permute-start.3 = (f32[96,128]{1,0:T(8,128)S(1)}, f32[96,128]{1,0:T(8,128)S(1)}, u32[]{:S(2)}, u32[]{:S(2)}) collective-permute-start(f32[96,128]{1,0:T(8,128)S(1)} %get-tuple-element.18), channel_id=1, source_target_pairs={{1,2},{2,1},{3,4},{4,3},{5,6},{6,5},{7,8},{8,7},{9,10},{10,9},{11,... | collective-permute-start | bytes 147464 | tf_op jit(solution)/shard_map/ppermute | solution.py:398
  12.1 3.0 %collective-permute-start.4 = (f32[24,128]{1,0:T(8,128)S(1)}, f32[24,128]{1,0:T(8,128)S(1)}, u32[]{:S(2)}, u32[]{:S(2)}) collective-permute-start(f32[24,128]{1,0:T(8,128)S(1)} %get-tuple-element.19), channel_id=1, source_target_pairs={{0,128},{128,0},{1,129},{129,1},{2,130},{130,2},{3,131},{131,3},{4... | collective-permute-start | bytes 36872 | tf_op jit(solution)/shard_map/ppermute | solution.py:398
  15.2 0.8 %copy-start.3 = (f32[128,128]{1,0:T(8,128)S(1)}, f32[128,128]{1,0:T(8,128)}, u32[]{:S(2)}) copy-start(f32[128,128]{1,0:T(8,128)} %far.1) | copy-start | bytes 196612
  16.7 6.2 %collective-permute-start.5 = (f32[8,128]{1,0:T(8,128)S(1)}, f32[8,128]{1,0:T(8,128)S(1)}, u32[]{:S(2)}, u32[]{:S(2)}) collective-permute-start(f32[8,128]{1,0:T(8,128)S(1)} %get-tuple-element.23.share), channel_id=1, source_target_pairs={{0,128},{128,0},{1,129},{129,1},{2,130},{130,2},{3,131},{131,3},{4... | collective-permute-start | bytes 12296 | tf_op jit(solution)/shard_map/ppermute | solution.py:398
  24.8 50.9 %all-to-all-start = ((f32[128,1,2176]{2,1,0:T(1,128)}), f32[128,1,2176]{2,1,0:T(1,128)S(1)}, u32[]{:S(2)}, u32[]{:S(2)}) async-start(f32[128,1,2176]{2,1,0:T(1,128)} %bitcast.10), calls=%async_computation | async-start | bytes 2228224 | tf_op jit(solution)/shard_map/all_to_all | solution.py:479

commit v3 on v2

--- a/solution.py
+++ b/solution.py
@@ -53,45 +53,48 @@
 
 
 def pack_kernel(
-    rho_hbm, rest_hbm, wave_hbm, x_even, x_odd, y_even, y_odd, z_face, rho, rest, wave, landed
+    rho_hbm, rest_hbm, wave_hbm, far, x_even, x_odd, y_even, y_odd, z_face, rho, rest, wave, landed
 ):
-    copies = [
-        pltpu.make_async_copy(rho_hbm, rho, landed.at[0]),
-        pltpu.make_async_copy(rest_hbm, rest, landed.at[1]),
-        pltpu.make_async_copy(wave_hbm, wave, landed.at[2]),
-    ]
+    copies = [pltpu.make_async_copy(rho_hbm, rho, landed.at[0])]
+    for part in range(4):
+        rows = pl.ds(part * 512, 512)
+        copies.append(pltpu.make_async_copy(rest_hbm.at[rows], rest.at[rows], landed.at[part + 1]))
+    copies.append(pltpu.make_async_copy(wave_hbm, wave, landed.at[5]))
     for copy in copies:
         copy.start()
     high = lax.axis_index("sec") == 0
     x_index, y_index = even("gx"), even("row")
+    x_targets = (x_even, x_index), (x_odd, jnp.logical_not(x_index))
+    y_targets = (y_even, y_index), (y_odd, jnp.logical_not(y_index))
     eye = iota((128, 128), 0) == iota((128, 128), 1)
-    copies[0].wait()
-    for piece in range(4):
-        z_face[piece : piece + 1] = edge_line(rho[piece * 128 : piece * 128 + 128], high, eye)
-    copies[2].wait()
+
+    def pick(ref, start, count, width, upper):
+        low = ref[pl.ds(start, count, stride=width)]
+        return jnp.where(upper, ref[pl.ds(start + width - 1, count, stride=width)], low)
+
+    for field in range(5):
+        copies[field].wait()
+        ref, first = (rho, 0) if field == 0 else (rest, field * 512 - 512)
+        for target, upper in x_targets:
+            at = pl.multiple_of(first + jnp.where(upper, 480, 0), 32)
+            target[field * 32 : field * 32 + 32] = ref[pl.ds(at, 32)]
+        for target, upper in y_targets:
+            target[field * 16 : field * 16 + 16] = pick(ref, first, 16, 32, upper)
+        for piece in range(4):
+            here = first + piece * 128
+            line = edge_line(ref[here : here + 128], high, eye)
+            z_face[field * 4 + piece : field * 4 + piece + 1] = line
+    copies[5].wait()
+    for target, upper in x_targets:
+        at = pl.multiple_of(jnp.where(upper, 112, 0), 16)
+        for part in range(4):
+            target[160 + 16 * part : 176 + 16 * part] = wave[pl.ds(part * 128 + at, 16)]
+    for target, upper in y_targets:
+        target[80:88] = pick(wave, 0, 8, 16, upper)
+        target[88:96] = pick(wave, 256, 8, 16, upper)
     z_face[20:21] = edge_line(wave[0:128], high, eye)
     z_face[21:22] = edge_line(wave[384:512], high, eye)
     z_face[22:24] = jnp.zeros((2, 128), F32)
-    copies[1].wait()
-    for piece in range(16):
-        z_face[piece + 4 : piece + 5] = edge_line(rest[piece * 128 : piece * 128 + 128], high, eye)
-    for target, upper in ((x_even, x_index), (x_odd, jnp.logical_not(x_index))):
-        at = pl.multiple_of(jnp.where(upper, 480, 0), 32)
-        wave_at = pl.multiple_of(jnp.where(upper, 112, 0), 16)
-        target[0:32] = rho[pl.ds(at, 32)]
-        for part in range(4):
-            target[32 * part + 32 : 32 * part + 64] = rest[pl.ds(part * 512 + at, 32)]
-            target[160 + 16 * part : 176 + 16 * part] = wave[pl.ds(part * 128 + wave_at, 16)]
-    for target, upper in ((y_even, y_index), (y_odd, jnp.logical_not(y_index))):
-        def pick(ref, start, count, width):
-            low = ref[pl.ds(start, count, stride=width)]
-            return jnp.where(upper, ref[pl.ds(start + width - 1, count, stride=width)], low)
-
-        target[0:16] = pick(rho, 0, 16, 32)
-        for part in range(4):
-            target[16 * part + 16 : 16 * part + 32] = pick(rest, part * 512, 16, 32)
-        target[80:88] = pick(wave, 0, 8, 16)
-        target[88:96] = pick(wave, 256, 8, 16)
 
 
 def sides(x_even, x_odd, y_even, y_odd):
@@ -104,7 +107,7 @@
     )
 
 
-def slot_kernel(owner, counts, patch, slots, valid, patches):
+def slot_kernel(owner, counts, patch, weights, slots, valid, patches):
     below = iota((128, 128), 0) < iota((128, 128), 1)
     target = iota((128, 128), 0) * 16
     lane = iota((128, 128), 1)
@@ -129,24 +132,17 @@
 
 def payload_kernel(
     rho, momentum, x_even, x_odd, y_even, y_odd, z_face, valid, weights,
-    payload, speed, z_speed, y_speed, held, landed,
+    payload, speed, z_speed, y_speed,
 ):
-    steps = landed.shape[0]
-    lines = 512 // steps
     sec = lax.axis_index("sec")
 
-    def fetch(step):
-        rows = pl.ds(pl.multiple_of(step * (lines * 64), 64), lines * 64)
-        return pltpu.make_async_copy(weights.at[rows], held.at[rows], landed.at[step])
-
-    for step in range(steps):
-        fetch(step).start()
     x_low, x_high, y_low, y_high = sides(x_even, x_odd, y_even, y_odd)
     for side, face in enumerate((y_low, y_high)):
         for k, part in enumerate((0, 2)):
             y_speed[2 * side + k] = face[16 * part + 16 : 16 * part + 32] / safe(face[0:16])
+    inverse = 1.0 / rho[...]
     for part in range(3):
-        speed[part, 32:544] = momentum[part * 512 : part * 512 + 512] / rho[...]
+        speed[part, 32:544] = momentum[part * 512 : part * 512 + 512] * inverse
         for at, face in ((0, x_low), (544, x_high)):
             speed[part, at : at + 32] = (
                 face[32 * part + 32 : 32 * part + 64] / safe(face[0:32])
@@ -161,88 +157,95 @@
     keep = [(group // 4 == part).astype(F32).astype(BF16) for part in range(4)]
     wide = iota((16, 256), 1) // 64 == iota((16, 256), 0) % 4
 
-    @pl.loop(0, steps)
-    def _(step):
-        fetch(step).wait()
-        for plane in range(lines // 32):
-            x = step * (lines // 32) + plane
-            at = pl.multiple_of(x * 32, 32)
-            v = [speed[part, pl.ds(at + 32, 32)] for part in range(3)]
-            v_before = [speed[part, pl.ds(at, 32)] for part in range(3)]
-            v_after = [speed[part, pl.ds(at + 64, 32)] for part in range(3)]
-            y_before = {part: y_speed[part // 2, pl.ds(x, 1)] for part in (0, 2)}
-            y_after = {part: y_speed[2 + part // 2, pl.ds(x, 1)] for part in (0, 2)}
-            along = {part: 0.5 * (v_after[part] - v_before[part]) for part in (1, 2)}
-            across = {
-                part: 0.5 * (up(v[part], y_after[part]) - down(v[part], y_before[part]))
-                for part in (0, 2)
-            }
-            deep = {part: derive_z(v[part], z_speed[part, pl.ds(at, 32)], sec) for part in (0, 1)}
-            swirl_x = across[2] - deep[1]
-            swirl_y = deep[0] - along[2]
-            swirl_z = along[1] - across[0]
-            mask = valid[pl.ds(at, 32)]
-            lamb = [
-                ((swirl_y * v[2] - swirl_z * v[1]) * mask).astype(BF16),
-                ((swirl_z * v[0] - swirl_x * v[2]) * mask).astype(BF16),
-                ((swirl_x * v[1] - swirl_y * v[0]) * mask).astype(BF16),
-            ]
-            for part in range(2):
-                rows = slice(part * 16, part * 16 + 16)
-                left = jnp.concatenate(
-                    [
-                        jnp.concatenate([lamb[c][rows] * keep[k] for k in range(4)], axis=1)
-                        for c in range(3)
-                    ],
-                    axis=0,
+    for x in range(16):
+        at = x * 32
+        v = [speed[part, pl.ds(at + 32, 32)] for part in range(3)]
+        v_before = [speed[part, pl.ds(at, 32)] for part in range(3)]
+        v_after = [speed[part, pl.ds(at + 64, 32)] for part in range(3)]
+        y_before = {part: y_speed[part // 2, pl.ds(x, 1)] for part in (0, 2)}
+        y_after = {part: y_speed[2 + part // 2, pl.ds(x, 1)] for part in (0, 2)}
+        along = {part: 0.5 * (v_after[part] - v_before[part]) for part in (1, 2)}
+        across = {
+            part: 0.5 * (up(v[part], y_after[part]) - down(v[part], y_before[part]))
+            for part in (0, 2)
+        }
+        deep = {part: derive_z(v[part], z_speed[part, pl.ds(at, 32)], sec) for part in (0, 1)}
+        swirl_x = across[2] - deep[1]
+        swirl_y = deep[0] - along[2]
+        swirl_z = along[1] - across[0]
+        mask = valid[pl.ds(at, 32)]
+        lamb = [
+            ((swirl_y * v[2] - swirl_z * v[1]) * mask).astype(BF16),
+            ((swirl_z * v[0] - swirl_x * v[2]) * mask).astype(BF16),
+            ((swirl_x * v[1] - swirl_y * v[0]) * mask).astype(BF16),
+        ]
+        for part in range(2):
+            rows = slice(part * 16, part * 16 + 16)
+            left = jnp.concatenate(
+                [
+                    jnp.concatenate([lamb[c][rows] * keep[k] for k in range(4)], axis=1)
+                    for c in range(3)
+                ],
+                axis=0,
+            )
+            first = (x * 32 + part * 16) * 64
+            right = jnp.concatenate(
+                [
+                    weights[first + 256 * k : first + 256 * k + 256]
+                    for k in range(4)
+                ],
+                axis=1,
+            )
+            product = lax.dot_general(
+                left, right, (((1,), (1,)), ((), ())), preferred_element_type=F32
+            )
+            folded = []
+            for c in range(3):
+                picked = jnp.where(wide, product[c * 16 : c * 16 + 16], 0.0)
+                both = picked[:, 0:128] + picked[:, 128:256]
+                folded.append(both + pltpu.roll(both, 64, 1))
+            pair = jnp.where(half, folded[0], folded[1])
+            pair_top = pair.astype(BF16)
+            pair_rest = (pair - pair_top.astype(F32)).astype(BF16)
+            single_top = folded[2].astype(BF16).astype(F32)
+            single = jnp.where(half, single_top, folded[2] - single_top).astype(BF16)
+            here = slice(at + part * 16, at + part * 16 + 16)
+            payload[here, 0:128] = pair_top
+            payload[here, 128:256] = pair_rest
+            payload[here, 256:384] = single
+
+
+def place_kernel(slots, payload, patches, share, other, send, rows, sent):
+    half = iota((32, 128), 1) < 64
+    lane = iota((32, 128), 1)
+    values = jnp.concatenate([payload[...], patches[...]], axis=1)
+    both = jnp.broadcast_to(share[0:1] + other[0:1], (32, 128))
+    copies = []
+    for block in range(4):
+        hits = [slots[slot * 128 + block * 32 : slot * 128 + block * 32 + 32] for slot in range(CAP)]
+        placed = jnp.dot(jnp.concatenate(hits, axis=0), values, preferred_element_type=F32)
+        first = block * 32 * ROWS
+        numbers = jnp.zeros((32, 128), F32)
+        for slot in range(CAP):
+            mine = placed[slot * 32 : slot * 32 + 32]
+            rows[pl.ds(first + slot, 32, stride=ROWS)] = mine[:, 0:128] + mine[:, 128:256]
+            third = mine[:, 256:384]
+            third = third + pltpu.roll(third, 64, 1)
+            if slot % 2 == 0:
+                kept = third
+            else:
+                rows[pl.ds(first + CAP + slot // 2, 32, stride=ROWS)] = jnp.where(
+                    half, kept, third
                 )
-                first = (x * 32 + part * 16) * 64
-                right = jnp.concatenate(
-                    [
-                        held[pl.ds(pl.multiple_of(first + 256 * k, 256), 256)]
-                        for k in range(4)
-                    ],
-                    axis=1,
-                )
-                product = lax.dot_general(
-                    left, right, (((1,), (1,)), ((), ())), preferred_element_type=F32
-                )
-                folded = []
-                for c in range(3):
-                    picked = jnp.where(wide, product[c * 16 : c * 16 + 16], 0.0)
-                    both = picked[:, 0:128] + picked[:, 128:256]
-                    folded.append(both + pltpu.roll(both, 64, 1))
-                pair = jnp.where(half, folded[0], folded[1])
-                pair_top = pair.astype(BF16)
-                pair_rest = (pair - pair_top.astype(F32)).astype(BF16)
-                single_top = folded[2].astype(BF16).astype(F32)
-                single = jnp.where(half, single_top, folded[2] - single_top).astype(BF16)
-                here = pl.ds(pl.multiple_of(at + part * 16, 16), 16)
-                payload[here, 0:128] = pair_top
-                payload[here, 128:256] = pair_rest
-                payload[here, 256:384] = single
-
-
-def place_kernel(slots, payload, patches, share, other, send):
-    lane = iota((128, 128), 1)
-    numbers = jnp.zeros((128, 128), F32)
-    kept = None
-    values = jnp.concatenate([payload[...], patches[...]], axis=1)
-    for slot in range(CAP):
-        placed = jnp.dot(
-            slots[slot * 128 : slot * 128 + 128], values, preferred_element_type=F32
-        )
-        send[pl.ds(slot, 128, stride=ROWS)] = placed[:, 0:128] + placed[:, 128:256]
-        third = placed[:, 256:384]
-        third = third + pltpu.roll(third, 64, 1)
-        if slot % 2 == 0:
-            kept = third
-        else:
-            send[pl.ds(CAP + slot // 2, 128, stride=ROWS)] = jnp.where(lane < 64, kept, third)
-        numbers = jnp.where(lane == slot, placed[:, 384:512], numbers)
-    send[pl.ds(CAP * 3 // 2, 128, stride=ROWS)] = numbers
-    both = share[0:1] + other[0:1]
-    send[pl.ds(CAP * 3 // 2 + 1, 128, stride=ROWS)] = jnp.broadcast_to(both, (128, 128))
+            numbers = jnp.where(lane == slot, mine[:, 384:512], numbers)
+        rows[pl.ds(first + CAP * 3 // 2, 32, stride=ROWS)] = numbers
+        rows[pl.ds(first + CAP * 3 // 2 + 1, 32, stride=ROWS)] = both
+        here = pl.ds(first, 32 * ROWS)
+        copy = pltpu.make_async_copy(rows.at[here], send.at[here], sent.at[block])
+        copy.start()
+        copies.append(copy)
+    for copy in copies:
+        copy.wait()
 
 
 def wave_kernel(
@@ -423,14 +426,14 @@
             pack_kernel,
             [((224, 128), F32)] * 2 + [((96, 128), F32)] * 2 + [((24, 128), F32)],
             1 << 20, 2 << 20,
-            in_specs=[hbm] * 3,
+            in_specs=[hbm] * 4,
             scratch_shapes=[
                 pltpu.VMEM((512, 128), F32),
                 pltpu.VMEM((2048, 128), F32),
                 pltpu.VMEM((512, 128), F32),
-                pltpu.SemaphoreType.DMA((3,)),
+                pltpu.SemaphoreType.DMA((6,)),
             ],
-        )(pinned(rho), pinned(rest), pinned(wave))
+        )(pinned(rho), pinned(rest), pinned(wave), pinned(far_kernel))
     halos = [
         exchange(faces[0], "gx", 0),
         exchange(faces[1], "gx", 1),
@@ -443,10 +446,12 @@
             slot_kernel,
             [((CAP * 128, 512), BF16), ((512, 128), F32), ((512, 128), BF16)],
             1 << 22, 2 << 20,
+            in_specs=[vmem] * 3 + [hbm],
         )(
             block_owner.reshape(4, 128),
             block_counts.reshape(4, 128),
             block_patch.reshape(4, 128),
+            pinned(weights),
         )
     with jax.named_scope("wave"):
         base, share = call(
@@ -462,20 +467,25 @@
         (payload,) = call(
             payload_kernel,
             [((512, 384), BF16)],
-            1 << 27, 16 << 20, 32,
-            in_specs=[vmem] * 8 + [hbm],
+            1 << 27, 16 << 20, 24,
+            in_specs=[vmem] * 9,
             scratch_shapes=[
                 pltpu.VMEM((3, 576, 128), F32),
                 pltpu.VMEM((2, 512, 128), F32),
                 pltpu.VMEM((4, 16, 128), F32),
-                pltpu.VMEM((512 * 64, 128), BF16),
+            ],
+        )(rho, rest, *halos, valid, weights)
+    with jax.named_scope("place"):
+        (send,) = call(
+            place_kernel,
+            [((128 * ROWS, 128), F32)],
+            1 << 28, 3 << 20,
+            out_specs=[hbm],
+            scratch_shapes=[
+                pltpu.VMEM((128 * ROWS, 128), F32),
                 pltpu.SemaphoreType.DMA((4,)),
             ],
-        )(rho, rest, *halos, valid, pinned(weights))
-    with jax.named_scope("place"):
-        (send,) = call(place_kernel, [((128 * ROWS, 128), F32)], 1 << 28, 3 << 20)(
-            slots, payload, patches, share, other
-        )
+        )(slots, payload, patches, share, other)
     arrived = lax.all_to_all(
         send.reshape(128, 1, ROWS * 128), ("gx", "row"), split_axis=0, concat_axis=0, tiled=True
     )

time: 77.3 us -> 73.8 us (0.955)
  Pallas kernels: 15.2 us -> 12.5 us
  starting transfers between devices: 29.4 us -> 28.6 us
    pallas_call x2, Pallas kernels: 6.88 us -> 4.45 us  [the longest x1 2.77 us: per_device(): call(payload_kernel, [((512, 384), BF16)], 1 << 27, 16 << 20, 24, in_spec...]
  transfers between devices with their start and end apart: 7 -> 7, of which waited for: 1 -> 1; matrix products, arithmetic and copies ran while one was open for 0% -> 0% of each run, Pallas kernels for 11% -> 8%
where the time goes in v3:
time: 73.8 us; the launch traced here: 73.5 us
  waiting for transfers between devices  30.1 us (41%)
  starting transfers between devices  28.6 us (39%)
  Pallas kernels  12.5 us (17%)
  between operations  1.51 us (2%)
  local copies, waits for them, and re-layouts  0.82 us (1%)
    all_to_all x1, waiting for transfers between devices, per_device(): lax.all_to_all(send.reshape(128, 1, ROWS * 128), ('gx', 'row'), split_axi...  30.1 us
    all_to_all x1, starting transfers between devices, per_device(): lax.all_to_all(send.reshape(128, 1, ROWS * 128), ('gx', 'row'), split_axi...  17.3 us
    ppermute x6, starting transfers between devices, exchange(): return lax.ppermute(face, axis, pairs)  11.3 us
    pallas_call x1, Pallas kernels, per_device(): call(payload_kernel, [((512, 384), BF16)], 1 << 27, 16 << 20, 24, in_spec...  2.77 us
    pallas_call x1, Pallas kernels, per_device(): call(pack_kernel, [((224, 128), F32)] * 2 + [((96, 128), F32)] * 2 + [((2...  2.74 us
    pallas_call x1, Pallas kernels, per_device(): call(les_kernel, [((2560, 128), F32)], 1 << 23, 4 << 20)(rho, rest, *halos)  2.69 us
    pallas_call x1, Pallas kernels, per_device(): call(place_kernel, [((128 * ROWS, 128), F32)], 1 << 28, 3 << 20, out_spec...  1.67 us
  transfers between devices with their start and end apart: 7, of which 1 were waited for; matrix products, arithmetic and copies ran while one was open for 0% of the time, Pallas kernels for 8%

profile of v3, /device:TPU:1, one launch (start us, length us, event | category | flops | bytes accessed | tf_op | source)
XLA Modules:
  0.0 73.5 jit_solution(3689421515181605893)
XLA Ops:
  0.7 2.7 %pack.1 = (f32[224,128]{1,0:T(8,128)S(1)}, f32[224,128]{1,0:T(8,128)S(1)}, f32[96,128]{1,0:T(8,128)S(1)}, f32[96,128]{1,0:T(8,128)S(1)}, f32[24,128]{1,0:T(8,128)S(1)}) custom-call(f32[512,128]{1,0:T(8,128)} %bitcast.21, f32[2048,128]{1,0:T(8,128)} %bitcast.17, f32[512,128]{1,0:T(8,128)} %bitcast.24, f32[128,128]{1,0:T(8,128)} %far.3), custom_call_target="tpu_custom_call" | custom-call | flops 1048576 | bytes 2097152 | tf_op jit(solution)/shard_map/pack/pallas_call | solution.py:425
  3.5 3.3 %collective-permute-start = (f32[224,128]{1,0:T(8,128)S(1)}, f32[224,128]{1,0:T(8,128)S(1)}, u32[]{:S(2)}, u32[]{:S(2)}) collective-permute-start(f32[224,128]{1,0:T(8,128)S(1)} %get-tuple-element.15), channel_id=1, source_target_pairs={{0,16},{16,0},{32,48},{48,32},{64,80},{80,64},{96,112},{112,96},{1... | collective-permute-start | bytes 344072 | tf_op jit(solution)/shard_map/ppermute | solution.py:401
  6.8 1.9 %collective-permute-start.1 = (f32[224,128]{1,0:T(8,128)S(1)}, f32[224,128]{1,0:T(8,128)S(1)}, u32[]{:S(2)}, u32[]{:S(2)}) collective-permute-start(f32[224,128]{1,0:T(8,128)S(1)} %get-tuple-element.16), channel_id=1, source_target_pairs={{16,32},{32,16},{48,64},{64,48},{80,96},{96,80},{17,33},{33,17},{4... | collective-permute-start | bytes 344072 | tf_op jit(solution)/shard_map/ppermute | solution.py:401
  8.7 2.5 %collective-permute-start.2 = (f32[96,128]{1,0:T(8,128)S(1)}, f32[96,128]{1,0:T(8,128)S(1)}, u32[]{:S(2)}, u32[]{:S(2)}) collective-permute-start(f32[96,128]{1,0:T(8,128)S(1)} %get-tuple-element.17), channel_id=1, source_target_pairs={{0,1},{1,0},{2,3},{3,2},{4,5},{5,4},{6,7},{7,6},{8,9},{9,8},{10,11... | collective-permute-start | bytes 147464 | tf_op jit(solution)/shard_map/ppermute | solution.py:401
  11.1 0.7 collective-permute-start.3
  11.8 1.7 %collective-permute-start.4 = (f32[24,128]{1,0:T(8,128)S(1)}, f32[24,128]{1,0:T(8,128)S(1)}, u32[]{:S(2)}, u32[]{:S(2)}) collective-permute-start(f32[24,128]{1,0:T(8,128)S(1)} %get-tuple-element.19), channel_id=1, source_target_pairs={{0,128},{128,0},{1,129},{129,1},{2,130},{130,2},{3,131},{131,3},{4... | collective-permute-start | bytes 36872 | tf_op jit(solution)/shard_map/ppermute | solution.py:401
  14.2 0.0 copy-start
  14.2 0.0 copy-start.2
  14.2 0.6 slots.1
  14.8 0.0 collective-permute-done.4.z_face
  14.8 0.0 collective-permute-done.2.y_even
  14.9 0.0 collective-permute-done.3.y_odd
  14.9 0.0 collective-permute-done.x_even
  14.9 0.0 collective-permute-done.1.x_odd
  14.9 0.7 wave.1
  15.6 1.2 %collective-permute-start.5 = (f32[8,128]{1,0:T(8,128)S(1)}, f32[8,128]{1,0:T(8,128)S(1)}, u32[]{:S(2)}, u32[]{:S(2)}) collective-permute-start(f32[8,128]{1,0:T(8,128)S(1)} %get-tuple-element.23.share), channel_id=1, source_target_pairs={{0,128},{128,0},{1,129},{129,1},{2,130},{130,2},{3,131},{131,3},{4... | collective-permute-start | bytes 12296 | tf_op jit(solution)/shard_map/ppermute | solution.py:401
  16.8 0.8 %copy-done = bf16[512,64,128]{2,1,0:T(8,128)(2,1)S(1)} copy-done((bf16[512,64,128]{2,1,0:T(8,128)(2,1)S(1)}, bf16[512,64,128]{2,1,0:T(8,128)(2,1)}, u32[]{:S(2)}) %copy-start) | copy-done | bytes 8388632
  17.6 2.8 %payload.1 = bf16[512,384]{1,0:T(8,128)(2,1)S(1)} custom-call(f32[512,128]{1,0:T(8,128)S(1)} %bitcast.22, f32[2048,128]{1,0:T(8,128)S(1)} %bitcast.18, f32[224,128]{1,0:T(8,128)S(1)} %collective-permute-done.x_even, f32[224,128]{1,0:T(8,128)S(1)} %collective-permute-done.1.x_odd, f32[96,128]{1,0:T(8,128)S(1)} %collective-permute-done.2.y_even, ...), custom_call_target="tpu_custom_call" | custom-call | flops 134217728 | bytes 16777216 | tf_op jit(solution)/shard_map/payload/pallas_call | solution.py:467
  20.4 0.0 collective-permute-done.5.other
  20.4 1.7 %place.1 = f32[2176,128]{1,0:T(8,128)} custom-call(bf16[1280,512]{1,0:T(8,128)(2,1)S(1)} %get-tuple-element.20.slots, bf16[512,384]{1,0:T(8,128)(2,1)S(1)} %payload.1, bf16[512,128]{1,0:T(8,128)(2,1)S(1)} %get-tuple-element.22.patches, f32[8,128]{1,0:T(8,128)S(1)} %get-tuple-element.23.share, f32[8,128]{1,0:T(8,128)S(1)} %collective-permute-done.5.other), custom_call_target="tpu_custom_call" | custom-call | flops 268435456 | bytes 3145728 | tf_op jit(solution)/shard_map/place/pallas_call | solution.py:479
  22.1 17.3 %all-to-all-start = ((f32[128,1,2176]{2,1,0:T(1,128)}), f32[128,1,2176]{2,1,0:T(1,128)S(1)}, u32[]{:S(2)}, u32[]{:S(2)}) async-start(f32[128,1,2176]{2,1,0:T(1,128)} %bitcast.10), calls=%async_computation | async-start | bytes 2228224 | tf_op jit(solution)/shard_map/all_to_all | solution.py:489
  39.4 2.7 %les.1 = f32[2560,128]{1,0:T(8,128)} custom-call(f32[512,128]{1,0:T(8,128)S(1)} %bitcast.23, f32[2048,128]{1,0:T(8,128)S(1)} %bitcast.19, f32[224,128]{1,0:T(8,128)S(1)} %collective-permute-done.x_even, f32[224,128]{1,0:T(8,128)S(1)} %collective-permute-done.1.x_odd, f32[96,128]{1,0:T(8,128)S(1)} %collective-permute-done.2.y_even, ...), custom_call_target="tpu_custom_call" | custom-call | flops 8388608 | bytes 4194304 | tf_op jit(solution)/shard_map/les/pallas_call | solution.py:493
  42.1 30.1 %all-to-all-done = f32[128,1,2176]{2,1,0:T(1,128)S(1)} async-done(((f32[128,1,2176]{2,1,0:T(1,128)}), f32[128,1,2176]{2,1,0:T(1,128)S(1)}, u32[]{:S(2)}, u32[]{:S(2)}) %all-to-all-start) | async-done | bytes 1114144 | tf_op jit(solution)/shard_map/all_to_all | solution.py:489
  72.2 1.3 %finish.1 = (f32[512,128]{1,0:T(8,128)}, f32[1,128]{1,0:T(1,128)}) custom-call(f32[2176,128]{1,0:T(8,128)S(1)} %bitcast.20, f32[512,128]{1,0:T(8,128)S(1)} %get-tuple-element.24.base), custom_call_target="tpu_custom_call" | custom-call | flops 268435456 | bytes 3145728 | tf_op jit(solution)/shard_map/finish/pallas_call | solution.py:495
  (15 shorter events, 0.0 us)
Async XLA Ops:
  0.6 13.6 %copy-start.5 = (s32[512,1]{0,1:T(1,128)S(1)}, s32[512,1]{0,1:T(1,128)}, u32[]{:S(2)}) copy-start(s32[512,1]{0,1:T(1,128)} %param.13) | copy-start | bytes 6148
  0.6 13.6 %copy-start.6 = (s32[512]{0:T(512)S(1)}, s32[512]{0:T(512)}, u32[]{:S(2)}) copy-start(s32[512]{0:T(512)} %param.15) | copy-start | bytes 6148
  0.7 13.6 %copy-start.7 = (s32[512]{0:T(512)S(1)}, s32[512]{0:T(512)}, u32[]{:S(2)}) copy-start(s32[512]{0:T(512)} %param.16) | copy-start | bytes 6148
  0.7 14.2 %copy-start.3 = (f32[4,8,16,128]{3,2,1,0:T(8,128)S(1)}, f32[4,8,16,128]{3,2,1,0:T(8,128)}, u32[]{:S(2)}) copy-start(f32[4,8,16,128]{3,2,1,0:T(8,128)} %param.12) | copy-start | bytes 786436
  0.7 14.2 %copy-start.4 = (f32[128,128]{1,0:T(8,128)S(1)}, f32[128,128]{1,0:T(8,128)}, u32[]{:S(2)}) copy-start(f32[128,128]{1,0:T(8,128)} %far.3) | copy-start | bytes 196612
  0.7 14.2 %copy-start.8 = (s32[128]{0:T(128)S(1)}, s32[128]{0:T(128)}, u32[]{:S(2)}) copy-start(s32[128]{0:T(128)} %param.18) | copy-start | bytes 1540
  0.7 16.1 %copy-start.1 = (f32[4,16,32,128]{3,2,1,0:T(8,128)S(1)}, f32[4,16,32,128]{3,2,1,0:T(8,128)}, u32[]{:S(2)}) copy-start(f32[4,16,32,128]{3,2,1,0:T(8,128)} %param.11) | copy-start | bytes 3145732
  3.5 11.4 %collective-permute-start = (f32[224,128]{1,0:T(8,128)S(1)}, f32[224,128]{1,0:T(8,128)S(1)}, u32[]{:S(2)}, u32[]{:S(2)}) collective-permute-start(f32[224,128]{1,0:T(8,128)S(1)} %get-tuple-element.15), channel_id=1, source_target_pairs={{0,16},{16,0},{32,48},{48,32},{64,80},{80,64},{96,112},{112,96},{1... | collective-permute-start | bytes 344072 | tf_op jit(solution)/shard_map/ppermute | solution.py:401
  6.8 8.1 %collective-permute-start.1 = (f32[224,128]{1,0:T(8,128)S(1)}, f32[224,128]{1,0:T(8,128)S(1)}, u32[]{:S(2)}, u32[]{:S(2)}) collective-permute-start(f32[224,128]{1,0:T(8,128)S(1)} %get-tuple-element.16), channel_id=1, source_target_pairs={{16,32},{32,16},{48,64},{64,48},{80,96},{96,80},{17,33},{33,17},{4... | collective-permute-start | bytes 344072 | tf_op jit(solution)/shard_map/ppermute | solution.py:401
  8.7 6.2 %collective-permute-start.2 = (f32[96,128]{1,0:T(8,128)S(1)}, f32[96,128]{1,0:T(8,128)S(1)}, u32[]{:S(2)}, u32[]{:S(2)}) collective-permute-start(f32[96,128]{1,0:T(8,128)S(1)} %get-tuple-element.17), channel_id=1, source_target_pairs={{0,1},{1,0},{2,3},{3,2},{4,5},{5,4},{6,7},{7,6},{8,9},{9,8},{10,11... | collective-permute-start | bytes 147464 | tf_op jit(solution)/shard_map/ppermute | solution.py:401
  11.1 3.7 %collective-permute-start.3 = (f32[96,128]{1,0:T(8,128)S(1)}, f32[96,128]{1,0:T(8,128)S(1)}, u32[]{:S(2)}, u32[]{:S(2)}) collective-permute-start(f32[96,128]{1,0:T(8,128)S(1)} %get-tuple-element.18), channel_id=1, source_target_pairs={{1,2},{2,1},{3,4},{4,3},{5,6},{6,5},{7,8},{8,7},{9,10},{10,9},{11,... | collective-permute-start | bytes 147464 | tf_op jit(solution)/shard_map/ppermute | solution.py:401
  11.8 3.0 %collective-permute-start.4 = (f32[24,128]{1,0:T(8,128)S(1)}, f32[24,128]{1,0:T(8,128)S(1)}, u32[]{:S(2)}, u32[]{:S(2)}) collective-permute-start(f32[24,128]{1,0:T(8,128)S(1)} %get-tuple-element.19), channel_id=1, source_target_pairs={{0,128},{128,0},{1,129},{129,1},{2,130},{130,2},{3,131},{131,3},{4... | collective-permute-start | bytes 36872 | tf_op jit(solution)/shard_map/ppermute | solution.py:401
  14.2 3.4 %copy-start = (bf16[512,64,128]{2,1,0:T(8,128)(2,1)S(1)}, bf16[512,64,128]{2,1,0:T(8,128)(2,1)}, u32[]{:S(2)}) copy-start(bf16[512,64,128]{2,1,0:T(8,128)(2,1)} %param.14) | copy-start | bytes 25165828
  14.2 3.4 %copy-start.2 = (f32[16,32,128]{2,1,0:T(8,128)S(1)}, f32[16,32,128]{2,1,0:T(8,128)}, u32[]{:S(2)}) copy-start(f32[16,32,128]{2,1,0:T(8,128)} %param.10) | copy-start | bytes 786436
  15.6 4.8 %collective-permute-start.5 = (f32[8,128]{1,0:T(8,128)S(1)}, f32[8,128]{1,0:T(8,128)S(1)}, u32[]{:S(2)}, u32[]{:S(2)}) collective-permute-start(f32[8,128]{1,0:T(8,128)S(1)} %get-tuple-element.23.share), channel_id=1, source_target_pairs={{0,128},{128,0},{1,129},{129,1},{2,130},{130,2},{3,131},{131,3},{4... | collective-permute-start | bytes 12296 | tf_op jit(solution)/shard_map/ppermute | solution.py:401
  22.1 50.1 %all-to-all-start = ((f32[128,1,2176]{2,1,0:T(1,128)}), f32[128,1,2176]{2,1,0:T(1,128)S(1)}, u32[]{:S(2)}, u32[]{:S(2)}) async-start(f32[128,1,2176]{2,1,0:T(1,128)} %bitcast.10), calls=%async_computation | async-start | bytes 2228224 | tf_op jit(solution)/shard_map/all_to_all | solution.py:489

commit v4 on v3

--- a/solution.py
+++ b/solution.py
@@ -23,9 +23,8 @@
     return jnp.transpose(jnp.broadcast_to(line, (128, 128)))
 
 
-def edge_line(block, high, eye):
-    column = jnp.where(high, block[:, 127:128], block[:, 0:1])
-    return jnp.sum(jnp.where(eye, column, 0.0), axis=0, keepdims=True)
+def edge_line(block, lane, eye):
+    return jnp.sum(jnp.where(eye, block[:, lane : lane + 1], 0.0), axis=0, keepdims=True)
 
 
 def safe(density):
@@ -52,48 +51,49 @@
     return lax.rem(lax.axis_index(axis), 2) == 0
 
 
-def pack_kernel(
-    rho_hbm, rest_hbm, wave_hbm, far, x_even, x_odd, y_even, y_odd, z_face, rho, rest, wave, landed
-):
-    copies = [pltpu.make_async_copy(rho_hbm, rho, landed.at[0])]
-    for part in range(4):
-        rows = pl.ds(part * 512, 512)
-        copies.append(pltpu.make_async_copy(rest_hbm.at[rows], rest.at[rows], landed.at[part + 1]))
-    copies.append(pltpu.make_async_copy(wave_hbm, wave, landed.at[5]))
+def pack_x_kernel(rho, rest, wave, far, x_even, x_odd, landed):
+    index = even("gx")
+    copies = []
+    for order, (target, upper) in enumerate(((x_even, index), (x_odd, jnp.logical_not(index)))):
+        at = pl.multiple_of(jnp.where(upper, 480, 0), 32)
+        wave_at = pl.multiple_of(jnp.where(upper, 112, 0), 16)
+        moves = [(rho.at[pl.ds(at, 32)], target.at[0:32])]
+        for part in range(4):
+            here = target.at[32 * part + 32 : 32 * part + 64]
+            moves.append((rest.at[pl.ds(part * 512 + at, 32)], here))
+            here = target.at[16 * part + 160 : 16 * part + 176]
+            moves.append((wave.at[pl.ds(part * 128 + wave_at, 16)], here))
+        for k, (here, there) in enumerate(moves):
+            copies.append(pltpu.make_async_copy(here, there, landed.at[order, k]))
     for copy in copies:
         copy.start()
+    for copy in copies:
+        copy.wait()
+
+
+def pack_kernel(rho, rest, wave, y_even, y_odd, z_face):
     high = lax.axis_index("sec") == 0
-    x_index, y_index = even("gx"), even("row")
-    x_targets = (x_even, x_index), (x_odd, jnp.logical_not(x_index))
-    y_targets = (y_even, y_index), (y_odd, jnp.logical_not(y_index))
+    index = even("row")
     eye = iota((128, 128), 0) == iota((128, 128), 1)
 
     def pick(ref, start, count, width, upper):
-        low = ref[pl.ds(start, count, stride=width)]
-        return jnp.where(upper, ref[pl.ds(start + width - 1, count, stride=width)], low)
-
-    for field in range(5):
-        copies[field].wait()
-        ref, first = (rho, 0) if field == 0 else (rest, field * 512 - 512)
-        for target, upper in x_targets:
-            at = pl.multiple_of(first + jnp.where(upper, 480, 0), 32)
-            target[field * 32 : field * 32 + 32] = ref[pl.ds(at, 32)]
-        for target, upper in y_targets:
-            target[field * 16 : field * 16 + 16] = pick(ref, first, 16, 32, upper)
-        for piece in range(4):
-            here = first + piece * 128
-            line = edge_line(ref[here : here + 128], high, eye)
-            z_face[field * 4 + piece : field * 4 + piece + 1] = line
-    copies[5].wait()
-    for target, upper in x_targets:
-        at = pl.multiple_of(jnp.where(upper, 112, 0), 16)
+        return ref[pl.ds(start + jnp.where(upper, width - 1, 0), count, stride=width)]
+
+    for target, upper in ((y_even, index), (y_odd, jnp.logical_not(index))):
+        target[0:16] = pick(rho, 0, 16, 32, upper)
         for part in range(4):
-            target[160 + 16 * part : 176 + 16 * part] = wave[pl.ds(part * 128 + at, 16)]
-    for target, upper in y_targets:
+            target[16 * part + 16 : 16 * part + 32] = pick(rest, part * 512, 16, 32, upper)
         target[80:88] = pick(wave, 0, 8, 16, upper)
         target[88:96] = pick(wave, 256, 8, 16, upper)
-    z_face[20:21] = edge_line(wave[0:128], high, eye)
-    z_face[21:22] = edge_line(wave[384:512], high, eye)
+    blocks = [(rho, piece) for piece in range(4)] + [(rest, piece) for piece in range(16)]
+    blocks += [(wave, 0), (wave, 3)]
+    for lane, here in ((127, high), (0, jnp.logical_not(high))):
+        @pl.when(here)
+        def _():
+            for line, (ref, piece) in enumerate(blocks):
+                z_face[line : line + 1] = edge_line(
+                    ref[piece * 128 : piece * 128 + 128], lane, eye
+                )
     z_face[22:24] = jnp.zeros((2, 128), F32)
 
 
@@ -155,7 +155,7 @@
     group = iota((16, 128), 0)
     half = iota((16, 128), 1) < 64
     keep = [(group // 4 == part).astype(F32).astype(BF16) for part in range(4)]
-    wide = iota((16, 256), 1) // 64 == iota((16, 256), 0) % 4
+    column = iota((64, 48), 1) % 4
 
     for x in range(16):
         at = x * 32
@@ -197,13 +197,13 @@
                 axis=1,
             )
             product = lax.dot_general(
-                left, right, (((1,), (1,)), ((), ())), preferred_element_type=F32
-            )
-            folded = []
-            for c in range(3):
-                picked = jnp.where(wide, product[c * 16 : c * 16 + 16], 0.0)
-                both = picked[:, 0:128] + picked[:, 128:256]
-                folded.append(both + pltpu.roll(both, 64, 1))
+                right, left, (((1,), (1,)), ((), ())), preferred_element_type=F32
+            )
+            merged = product[0:64]
+            for k in range(1, 4):
+                merged = jnp.where(column == k, product[k * 64 : k * 64 + 64], merged)
+            turned = jnp.transpose(jnp.concatenate([merged, merged], axis=0))
+            folded = [turned[c * 16 : c * 16 + 16] for c in range(3)]
             pair = jnp.where(half, folded[0], folded[1])
             pair_top = pair.astype(BF16)
             pair_rest = (pair - pair_top.astype(F32)).astype(BF16)
@@ -421,26 +421,26 @@
     vmem = pl.BlockSpec(memory_space=pltpu.VMEM)
     smem = pl.BlockSpec(memory_space=pltpu.SMEM)
     pinned = lambda x: pltpu.with_memory_space_constraint(x, pltpu.HBM)
+    with jax.named_scope("pack_x"):
+        faces = call(
+            pack_x_kernel,
+            [((224, 128), F32)] * 2,
+            1 << 10, 1 << 20,
+            in_specs=[hbm] * 4,
+            scratch_shapes=[pltpu.SemaphoreType.DMA((2, 9))],
+        )(pinned(rho), pinned(rest), pinned(wave), pinned(far_kernel))
+    x_even = exchange(faces[0], "gx", 0)
+    x_odd = exchange(faces[1], "gx", 1)
     with jax.named_scope("pack"):
         faces = call(
             pack_kernel,
-            [((224, 128), F32)] * 2 + [((96, 128), F32)] * 2 + [((24, 128), F32)],
+            [((96, 128), F32)] * 2 + [((24, 128), F32)],
             1 << 20, 2 << 20,
-            in_specs=[hbm] * 4,
-            scratch_shapes=[
-                pltpu.VMEM((512, 128), F32),
-                pltpu.VMEM((2048, 128), F32),
-                pltpu.VMEM((512, 128), F32),
-                pltpu.SemaphoreType.DMA((6,)),
-            ],
-        )(pinned(rho), pinned(rest), pinned(wave), pinned(far_kernel))
-    halos = [
-        exchange(faces[0], "gx", 0),
-        exchange(faces[1], "gx", 1),
-        exchange(faces[2], "row", 0),
-        exchange(faces[3], "row", 1),
-        exchange(faces[4], "sec", 0),
-    ]
+        )(rho, rest, wave)
+    y_even = exchange(faces[0], "row", 0)
+    y_odd = exchange(faces[1], "row", 1)
+    z_face = exchange(faces[2], "sec", 0)
+    halos = [x_even, x_odd, y_even, y_odd, z_face]
     with jax.named_scope("slots"):
         slots, valid, patches = call(
             slot_kernel,

time: 73.8 us -> 72.5 us (0.982)
  Pallas kernels: 12.5 us -> 11.2 us
    pallas_call x1 -> x2, Pallas kernels: 2.74 us -> 1.65 us  [the longest x1 1.1 us: per_device(): call(pack_x_kernel, [((224, 128), F32)] * 2, 1 << 10, 1 << 20, in_specs=[...]
  transfers between devices with their start and end apart: 7 -> 7, of which waited for: 1 -> 1; matrix products, arithmetic and copies ran while one was open for 0% -> 0% of each run, Pallas kernels for 8% -> 9%
where the time goes in v4:
time: 72.5 us; the launch traced here: 72.2 us
  waiting for transfers between devices  30.1 us (42%)
  starting transfers between devices  28.6 us (39%)
  Pallas kernels  11.2 us (15%)
  between operations  1.53 us (2%)
  local copies, waits for them, and re-layouts  0.85 us (1%)
    all_to_all x1, waiting for transfers between devices, per_device(): lax.all_to_all(send.reshape(128, 1, ROWS * 128), ('gx', 'row'), split_axi...  30.1 us
    all_to_all x1, starting transfers between devices, per_device(): lax.all_to_all(send.reshape(128, 1, ROWS * 128), ('gx', 'row'), split_axi...  17.3 us
    ppermute x6, starting transfers between devices, exchange(): return lax.ppermute(face, axis, pairs)  11.3 us
    pallas_call x1, Pallas kernels, per_device(): call(les_kernel, [((2560, 128), F32)], 1 << 23, 4 << 20)(rho, rest, *halos)  2.69 us
    pallas_call x1, Pallas kernels, per_device(): call(payload_kernel, [((512, 384), BF16)], 1 << 27, 16 << 20, 24, in_spec...  2.59 us
    pallas_call x1, Pallas kernels, per_device(): call(place_kernel, [((128 * ROWS, 128), F32)], 1 << 28, 3 << 20, out_spec...  1.67 us
  transfers between devices with their start and end apart: 7, of which 1 were waited for; matrix products, arithmetic and copies ran while one was open for 0% of the time, Pallas kernels for 9%

profile of v4, /device:TPU:1, one launch (start us, length us, event | category | flops | bytes accessed | tf_op | source)
XLA Modules:
  0.0 72.2 jit_solution(11967839768152256767)
XLA Ops:
  0.7 1.1 %pack_x.1 = (f32[224,128]{1,0:T(8,128)S(1)}, f32[224,128]{1,0:T(8,128)S(1)}) custom-call(f32[512,128]{1,0:T(8,128)} %bitcast.22, f32[2048,128]{1,0:T(8,128)} %bitcast.17, f32[512,128]{1,0:T(8,128)} %bitcast.26, f32[128,128]{1,0:T(8,128)} %far.3), custom_call_target="tpu_custom_call" | custom-call | flops 1024 | bytes 1048576 | tf_op jit(solution)/shard_map/pack_x/pallas_call | solution.py:425
  1.8 3.3 %collective-permute-start = (f32[224,128]{1,0:T(8,128)S(1)}, f32[224,128]{1,0:T(8,128)S(1)}, u32[]{:S(2)}, u32[]{:S(2)}) collective-permute-start(f32[224,128]{1,0:T(8,128)S(1)} %get-tuple-element.15), channel_id=1, source_target_pairs={{0,16},{16,0},{32,48},{48,32},{64,80},{80,64},{96,112},{112,96},{1... | collective-permute-start | bytes 344072 | tf_op jit(solution)/shard_map/ppermute | solution.py:401
  5.1 1.9 %collective-permute-start.1 = (f32[224,128]{1,0:T(8,128)S(1)}, f32[224,128]{1,0:T(8,128)S(1)}, u32[]{:S(2)}, u32[]{:S(2)}) collective-permute-start(f32[224,128]{1,0:T(8,128)S(1)} %get-tuple-element.16), channel_id=1, source_target_pairs={{16,32},{32,16},{48,64},{64,48},{80,96},{96,80},{17,33},{33,17},{4... | collective-permute-start | bytes 344072 | tf_op jit(solution)/shard_map/ppermute | solution.py:401
  7.1 0.0 copy-start.4
  7.1 0.5 pack.1
  7.6 2.5 %collective-permute-start.2 = (f32[96,128]{1,0:T(8,128)S(1)}, f32[96,128]{1,0:T(8,128)S(1)}, u32[]{:S(2)}, u32[]{:S(2)}) collective-permute-start(f32[96,128]{1,0:T(8,128)S(1)} %get-tuple-element.17), channel_id=1, source_target_pairs={{0,1},{1,0},{2,3},{3,2},{4,5},{5,4},{6,7},{7,6},{8,9},{9,8},{10,11... | collective-permute-start | bytes 147464 | tf_op jit(solution)/shard_map/ppermute | solution.py:401
  10.1 0.7 collective-permute-start.3
  10.8 1.7 %collective-permute-start.4 = (f32[24,128]{1,0:T(8,128)S(1)}, f32[24,128]{1,0:T(8,128)S(1)}, u32[]{:S(2)}, u32[]{:S(2)}) collective-permute-start(f32[24,128]{1,0:T(8,128)S(1)} %get-tuple-element.19), channel_id=1, source_target_pairs={{0,128},{128,0},{1,129},{129,1},{2,130},{130,2},{3,131},{131,3},{4... | collective-permute-start | bytes 36872 | tf_op jit(solution)/shard_map/ppermute | solution.py:401
  13.2 0.0 copy-start.8
  13.2 0.0 copy-start
  13.2 0.6 slots.1
  13.8 0.0 collective-permute-done.4.z_face
  13.8 0.0 collective-permute-done.2.y_even
  13.8 0.0 collective-permute-done.3.y_odd
  13.8 0.0 collective-permute-done.x_even
  13.9 0.7 wave.1
  14.5 1.2 %collective-permute-start.5 = (f32[8,128]{1,0:T(8,128)S(1)}, f32[8,128]{1,0:T(8,128)S(1)}, u32[]{:S(2)}, u32[]{:S(2)}) collective-permute-start(f32[8,128]{1,0:T(8,128)S(1)} %get-tuple-element.23.share), channel_id=1, source_target_pairs={{0,128},{128,0},{1,129},{129,1},{2,130},{130,2},{3,131},{131,3},{4... | collective-permute-start | bytes 12296 | tf_op jit(solution)/shard_map/ppermute | solution.py:401
  15.7 0.8 %copy-done = bf16[512,64,128]{2,1,0:T(8,128)(2,1)S(1)} copy-done((bf16[512,64,128]{2,1,0:T(8,128)(2,1)S(1)}, bf16[512,64,128]{2,1,0:T(8,128)(2,1)}, u32[]{:S(2)}) %copy-start) | copy-done | bytes 8388632
  16.6 2.6 %payload.1 = bf16[512,384]{1,0:T(8,128)(2,1)S(1)} custom-call(f32[512,128]{1,0:T(8,128)S(1)} %bitcast.24, f32[2048,128]{1,0:T(8,128)S(1)} %bitcast.19, f32[224,128]{1,0:T(8,128)S(1)} %collective-permute-done.x_even, f32[224,128]{1,0:T(8,128)S(1)} %collective-permute-done.1.x_odd, f32[96,128]{1,0:T(8,128)S(1)} %collective-permute-done.2.y_even, ...), custom_call_target="tpu_custom_call" | custom-call | flops 134217728 | bytes 16777216 | tf_op jit(solution)/shard_map/payload/pallas_call | solution.py:467
  19.2 1.7 %place.1 = f32[2176,128]{1,0:T(8,128)} custom-call(bf16[1280,512]{1,0:T(8,128)(2,1)S(1)} %get-tuple-element.20.slots, bf16[512,384]{1,0:T(8,128)(2,1)S(1)} %payload.1, bf16[512,128]{1,0:T(8,128)(2,1)S(1)} %get-tuple-element.22.patches, f32[8,128]{1,0:T(8,128)S(1)} %get-tuple-element.23.share, f32[8,128]{1,0:T(8,128)S(1)} %collective-permute-done.5.other), custom_call_target="tpu_custom_call" | custom-call | flops 268435456 | bytes 3145728 | tf_op jit(solution)/shard_map/place/pallas_call | solution.py:479
  20.8 17.3 %all-to-all-start = ((f32[128,1,2176]{2,1,0:T(1,128)}), f32[128,1,2176]{2,1,0:T(1,128)S(1)}, u32[]{:S(2)}, u32[]{:S(2)}) async-start(f32[128,1,2176]{2,1,0:T(1,128)} %bitcast.10), calls=%async_computation | async-start | bytes 2228224 | tf_op jit(solution)/shard_map/all_to_all | solution.py:489
  38.2 2.7 %les.1 = f32[2560,128]{1,0:T(8,128)} custom-call(f32[512,128]{1,0:T(8,128)S(1)} %bitcast.25, f32[2048,128]{1,0:T(8,128)S(1)} %bitcast.20, f32[224,128]{1,0:T(8,128)S(1)} %collective-permute-done.x_even, f32[224,128]{1,0:T(8,128)S(1)} %collective-permute-done.1.x_odd, f32[96,128]{1,0:T(8,128)S(1)} %collective-permute-done.2.y_even, ...), custom_call_target="tpu_custom_call" | custom-call | flops 8388608 | bytes 4194304 | tf_op jit(solution)/shard_map/les/pallas_call | solution.py:493
  40.8 30.1 %all-to-all-done = f32[128,1,2176]{2,1,0:T(1,128)S(1)} async-done(((f32[128,1,2176]{2,1,0:T(1,128)}), f32[128,1,2176]{2,1,0:T(1,128)S(1)}, u32[]{:S(2)}, u32[]{:S(2)}) %all-to-all-start) | async-done | bytes 1114144 | tf_op jit(solution)/shard_map/all_to_all | solution.py:489
  70.9 1.3 %finish.1 = (f32[512,128]{1,0:T(8,128)}, f32[1,128]{1,0:T(1,128)}) custom-call(f32[2176,128]{1,0:T(8,128)S(1)} %bitcast.21, f32[512,128]{1,0:T(8,128)S(1)} %get-tuple-element.24.base), custom_call_target="tpu_custom_call" | custom-call | flops 268435456 | bytes 3145728 | tf_op jit(solution)/shard_map/finish/pallas_call | solution.py:495
  (16 shorter events, 0.0 us)
Async XLA Ops:
  0.6 6.4 %copy-start.2 = (f32[16,32,128]{2,1,0:T(8,128)S(1)}, f32[16,32,128]{2,1,0:T(8,128)}, u32[]{:S(2)}) copy-start(f32[16,32,128]{2,1,0:T(8,128)} %param.10) | copy-start | bytes 786436
  0.6 6.4 %copy-start.1 = (f32[4,16,32,128]{3,2,1,0:T(8,128)S(1)}, f32[4,16,32,128]{3,2,1,0:T(8,128)}, u32[]{:S(2)}) copy-start(f32[4,16,32,128]{3,2,1,0:T(8,128)} %param.11) | copy-start | bytes 3145732
  0.7 6.4 %copy-start.3 = (f32[4,8,16,128]{3,2,1,0:T(8,128)S(1)}, f32[4,8,16,128]{3,2,1,0:T(8,128)}, u32[]{:S(2)}) copy-start(f32[4,8,16,128]{3,2,1,0:T(8,128)} %param.12) | copy-start | bytes 786436
  0.7 12.5 %copy-start.5 = (s32[512,1]{0,1:T(1,128)S(1)}, s32[512,1]{0,1:T(1,128)}, u32[]{:S(2)}) copy-start(s32[512,1]{0,1:T(1,128)} %param.13) | copy-start | bytes 6148
  0.7 12.5 %copy-start.6 = (s32[512]{0:T(512)S(1)}, s32[512]{0:T(512)}, u32[]{:S(2)}) copy-start(s32[512]{0:T(512)} %param.15) | copy-start | bytes 6148
  0.7 12.5 %copy-start.7 = (s32[512]{0:T(512)S(1)}, s32[512]{0:T(512)}, u32[]{:S(2)}) copy-start(s32[512]{0:T(512)} %param.16) | copy-start | bytes 6148
  1.8 12.0 %collective-permute-start = (f32[224,128]{1,0:T(8,128)S(1)}, f32[224,128]{1,0:T(8,128)S(1)}, u32[]{:S(2)}, u32[]{:S(2)}) collective-permute-start(f32[224,128]{1,0:T(8,128)S(1)} %get-tuple-element.15), channel_id=1, source_target_pairs={{0,16},{16,0},{32,48},{48,32},{64,80},{80,64},{96,112},{112,96},{1... | collective-permute-start | bytes 344072 | tf_op jit(solution)/shard_map/ppermute | solution.py:401
  5.1 8.7 %collective-permute-start.1 = (f32[224,128]{1,0:T(8,128)S(1)}, f32[224,128]{1,0:T(8,128)S(1)}, u32[]{:S(2)}, u32[]{:S(2)}) collective-permute-start(f32[224,128]{1,0:T(8,128)S(1)} %get-tuple-element.16), channel_id=1, source_target_pairs={{16,32},{32,16},{48,64},{64,48},{80,96},{96,80},{17,33},{33,17},{4... | collective-permute-start | bytes 344072 | tf_op jit(solution)/shard_map/ppermute | solution.py:401
  7.1 6.8 %copy-start.4 = (f32[128,128]{1,0:T(8,128)S(1)}, f32[128,128]{1,0:T(8,128)}, u32[]{:S(2)}) copy-start(f32[128,128]{1,0:T(8,128)} %far.3) | copy-start | bytes 196612
  7.6 6.2 %collective-permute-start.2 = (f32[96,128]{1,0:T(8,128)S(1)}, f32[96,128]{1,0:T(8,128)S(1)}, u32[]{:S(2)}, u32[]{:S(2)}) collective-permute-start(f32[96,128]{1,0:T(8,128)S(1)} %get-tuple-element.17), channel_id=1, source_target_pairs={{0,1},{1,0},{2,3},{3,2},{4,5},{5,4},{6,7},{7,6},{8,9},{9,8},{10,11... | collective-permute-start | bytes 147464 | tf_op jit(solution)/shard_map/ppermute | solution.py:401
  10.1 3.7 %collective-permute-start.3 = (f32[96,128]{1,0:T(8,128)S(1)}, f32[96,128]{1,0:T(8,128)S(1)}, u32[]{:S(2)}, u32[]{:S(2)}) collective-permute-start(f32[96,128]{1,0:T(8,128)S(1)} %get-tuple-element.18), channel_id=1, source_target_pairs={{1,2},{2,1},{3,4},{4,3},{5,6},{6,5},{7,8},{8,7},{9,10},{10,9},{11,... | collective-permute-start | bytes 147464 | tf_op jit(solution)/shard_map/ppermute | solution.py:401
  10.8 3.0 %collective-permute-start.4 = (f32[24,128]{1,0:T(8,128)S(1)}, f32[24,128]{1,0:T(8,128)S(1)}, u32[]{:S(2)}, u32[]{:S(2)}) collective-permute-start(f32[24,128]{1,0:T(8,128)S(1)} %get-tuple-element.19), channel_id=1, source_target_pairs={{0,128},{128,0},{1,129},{129,1},{2,130},{130,2},{3,131},{131,3},{4... | collective-permute-start | bytes 36872 | tf_op jit(solution)/shard_map/ppermute | solution.py:401
  13.2 0.7 copy-start.8
  13.2 3.4 %copy-start = (bf16[512,64,128]{2,1,0:T(8,128)(2,1)S(1)}, bf16[512,64,128]{2,1,0:T(8,128)(2,1)}, u32[]{:S(2)}) copy-start(bf16[512,64,128]{2,1,0:T(8,128)(2,1)} %param.14) | copy-start | bytes 25165828
  14.5 4.6 %collective-permute-start.5 = (f32[8,128]{1,0:T(8,128)S(1)}, f32[8,128]{1,0:T(8,128)S(1)}, u32[]{:S(2)}, u32[]{:S(2)}) collective-permute-start(f32[8,128]{1,0:T(8,128)S(1)} %get-tuple-element.23.share), channel_id=1, source_target_pairs={{0,128},{128,0},{1,129},{129,1},{2,130},{130,2},{3,131},{131,3},{4... | collective-permute-start | bytes 12296 | tf_op jit(solution)/shard_map/ppermute | solution.py:401
  20.8 50.1 %all-to-all-start = ((f32[128,1,2176]{2,1,0:T(1,128)}), f32[128,1,2176]{2,1,0:T(1,128)S(1)}, u32[]{:S(2)}, u32[]{:S(2)}) async-start(f32[128,1,2176]{2,1,0:T(1,128)} %bitcast.10), calls=%async_computation | async-start | bytes 2228224 | tf_op jit(solution)/shard_map/all_to_all | solution.py:489

commit v5 on v4

--- a/solution.py
+++ b/solution.py
@@ -51,40 +51,42 @@
     return lax.rem(lax.axis_index(axis), 2) == 0
 
 
-def pack_x_kernel(rho, rest, wave, far, x_even, x_odd, landed):
-    index = even("gx")
-    copies = []
-    for order, (target, upper) in enumerate(((x_even, index), (x_odd, jnp.logical_not(index)))):
-        at = pl.multiple_of(jnp.where(upper, 480, 0), 32)
-        wave_at = pl.multiple_of(jnp.where(upper, 112, 0), 16)
-        moves = [(rho.at[pl.ds(at, 32)], target.at[0:32])]
-        for part in range(4):
-            here = target.at[32 * part + 32 : 32 * part + 64]
-            moves.append((rest.at[pl.ds(part * 512 + at, 32)], here))
-            here = target.at[16 * part + 160 : 16 * part + 176]
-            moves.append((wave.at[pl.ds(part * 128 + wave_at, 16)], here))
-        for k, (here, there) in enumerate(moves):
-            copies.append(pltpu.make_async_copy(here, there, landed.at[order, k]))
+def pack_y_kernel(rho, rest, wave, far, y_even, y_odd, low, high, wave_low, wave_high, landed):
+    moves = [
+        (rho.at[:, 0:8], low.at[0]), (rho.at[:, 24:32], high.at[0]),
+        (rest.at[:, :, 0:8], low.at[1:5]), (rest.at[:, :, 24:32], high.at[1:5]),
+    ]
+    for k, part in enumerate((0, 2)):
+        moves.append((wave.at[part, :, 0:8], wave_low.at[k]))
+        moves.append((wave.at[part, :, 8:16], wave_high.at[k]))
+    copies = [
+        pltpu.make_async_copy(here, there, landed.at[k]) for k, (here, there) in enumerate(moves)
+    ]
     for copy in copies:
         copy.start()
     for copy in copies:
         copy.wait()
-
-
-def pack_kernel(rho, rest, wave, y_even, y_odd, z_face):
+    upper = even("row")
+    lines = [(16 * part, 16, low[part, :, 0], high[part, :, 7]) for part in range(5)]
+    lines += [(80 + 8 * part, 8, wave_low[part, :, 0], wave_high[part, :, 7]) for part in range(2)]
+    for at, count, first, last in lines:
+        y_even[at : at + count] = jnp.where(upper, last, first)
+        y_odd[at : at + count] = jnp.where(upper, first, last)
+    y_even[96:104] = jnp.zeros((8, 128), F32)
+    y_odd[96:104] = jnp.zeros((8, 128), F32)
+
+
+def pack_kernel(rho, rest, wave, weights, after, x_odd, x_even, z_face):
+    index = even("gx")
+    for target, upper in ((x_even, index), (x_odd, jnp.logical_not(index))):
+        at = pl.multiple_of(jnp.where(upper, 480, 0), 32)
+        wave_at = pl.multiple_of(jnp.where(upper, 112, 0), 16)
+        inverse = 1.0 / rho[pl.ds(at, 32)]
+        for k in range(2):
+            target[32 * k : 32 * k + 32] = rest[pl.ds(512 * k + 512 + at, 32)] * inverse
+            target[64 + 16 * k : 80 + 16 * k] = wave[pl.ds(128 * k + wave_at, 16)]
     high = lax.axis_index("sec") == 0
-    index = even("row")
     eye = iota((128, 128), 0) == iota((128, 128), 1)
-
-    def pick(ref, start, count, width, upper):
-        return ref[pl.ds(start + jnp.where(upper, width - 1, 0), count, stride=width)]
-
-    for target, upper in ((y_even, index), (y_odd, jnp.logical_not(index))):
-        target[0:16] = pick(rho, 0, 16, 32, upper)
-        for part in range(4):
-            target[16 * part + 16 : 16 * part + 32] = pick(rest, part * 512, 16, 32, upper)
-        target[80:88] = pick(wave, 0, 8, 16, upper)
-        target[88:96] = pick(wave, 256, 8, 16, upper)
     blocks = [(rho, piece) for piece in range(4)] + [(rest, piece) for piece in range(16)]
     blocks += [(wave, 0), (wave, 3)]
     for lane, here in ((127, high), (0, jnp.logical_not(high))):
@@ -97,6 +99,18 @@
     z_face[22:24] = jnp.zeros((2, 128), F32)
 
 
+def late_kernel(rho, rest, wave, token, x_odd, x_even):
+    index = even("gx")
+    for target, upper in ((x_even, index), (x_odd, jnp.logical_not(index))):
+        at = pl.multiple_of(jnp.where(upper, 480, 0), 32)
+        wave_at = pl.multiple_of(jnp.where(upper, 112, 0), 16)
+        target[0:32] = rho[pl.ds(at, 32)]
+        for part in range(4):
+            target[32 * part + 32 : 32 * part + 64] = rest[pl.ds(part * 512 + at, 32)]
+        for k in range(2):
+            target[160 + 16 * k : 176 + 16 * k] = wave[pl.ds(128 * k + 256 + wave_at, 16)]
+
+
 def sides(x_even, x_odd, y_even, y_odd):
     x_index, y_index = even("gx"), even("row")
     return (
@@ -107,7 +121,7 @@
     )
 
 
-def slot_kernel(owner, counts, patch, weights, slots, valid, patches):
+def slot_kernel(owner, counts, patch, slots, valid, patches):
     below = iota((128, 128), 0) < iota((128, 128), 1)
     target = iota((128, 128), 0) * 16
     lane = iota((128, 128), 1)
@@ -131,7 +145,7 @@
 
 
 def payload_kernel(
-    rho, momentum, x_even, x_odd, y_even, y_odd, z_face, valid, weights,
+    rho, momentum, y_odd, y_even, x_odd, x_even, z_face, valid, weights,
     payload, speed, z_speed, y_speed,
 ):
     sec = lax.axis_index("sec")
@@ -143,10 +157,9 @@
     inverse = 1.0 / rho[...]
     for part in range(3):
         speed[part, 32:544] = momentum[part * 512 : part * 512 + 512] * inverse
+    for part in range(2):
         for at, face in ((0, x_low), (544, x_high)):
-            speed[part, at : at + 32] = (
-                face[32 * part + 32 : 32 * part + 64] / safe(face[0:32])
-            )
+            speed[part + 1, at : at + 32] = face[32 * part : 32 * part + 32]
     for part in range(2):
         edge = z_face[4 * part + 4 : 4 * part + 8] / safe(z_face[0:4])
         for piece in range(4):
@@ -248,48 +261,38 @@
         copy.wait()
 
 
-def wave_kernel(
-    tile_class, wave, x_even, x_odd, y_even, y_odd, z_face, samples, far, base, share
+def factors(level):
+    number = level[...].astype(F32)
+    return 0.1 + 0.3 * number, 1.0 + 0.25 * number
+
+
+def pressure_kernel(
+    level, wave, y_odd, y_even, x_odd, x_even, z_face, samples, far, base, share
 ):
     sec = lax.axis_index("sec")
     x_low, x_high, y_low, y_high = sides(x_even, x_odd, y_even, y_odd)
-    level = tile_class[0, 0].astype(F32)
-    mean_flow = 0.1 + 0.3 * level
-    stiffness = 1.0 + 0.25 * level
-    z_pressure = as_column(z_face[20:21])
+    mean_flow, stiffness = factors(level)
     z_speed = as_column(z_face[21:22])
     for x in range(8):
         def row(part, at):
-            start = part * 128 + at * 16
             if at < 0:
-                return x_low[160 + 16 * part : 176 + 16 * part]
+                return x_low[64 + 16 * part : 80 + 16 * part]
             if at > 7:
-                return x_high[160 + 16 * part : 176 + 16 * part]
-            return wave[start : start + 16]
-
-        now = [row(part, x) for part in range(4)]
-        along = [0.5 * (row(part, x + 1) - row(part, x - 1)) for part in range(4)]
-        across = [
-            0.5
-            * (
-                up(now[part], y_high[80 + 8 * k + x : 81 + 8 * k + x])
-                - down(now[part], y_low[80 + 8 * k + x : 81 + 8 * k + x])
-            )
-            for k, part in enumerate((0, 2))
-        ]
+                return x_high[64 + 16 * part : 80 + 16 * part]
+            return wave[part * 128 + at * 16 : part * 128 + at * 16 + 16]
+
         here = slice(x * 16, x * 16 + 16)
-        deep = [derive_z(now[0], z_pressure[here], sec), derive_z(now[3], z_speed[here], sec)]
-        divergence = along[1] + across[1] + deep[1]
-        base[here] = now[0] - WAVE_STEP * (mean_flow * along[0] + stiffness * divergence)
-        for part, gradient in ((1, along[0]), (2, across[0]), (3, deep[0])):
-            base[part * 128 + x * 16 : part * 128 + x * 16 + 16] = now[part] - WAVE_STEP * (
-                mean_flow * along[part] + gradient
-            )
+        along = [0.5 * (row(part, x + 1) - row(part, x - 1)) for part in range(2)]
+        side = wave[256 + x * 16 : 272 + x * 16]
+        across = 0.5 * (up(side, y_high[88 + x : 89 + x]) - down(side, y_low[88 + x : 89 + x]))
+        deep = derive_z(wave[384 + x * 16 : 400 + x * 16], z_speed[here], sec)
+        divergence = along[1] + across + deep
+        base[here] = wave[here] - WAVE_STEP * (mean_flow * along[0] + stiffness * divergence)
     index = samples[...]
     line, cell = index // 128, index % 128
     picks = (iota((128, 128), 0) == line).astype(F32)
     columns = lax.dot_general(
-        base[0:128], picks, (((0,), (0,)), ((), ())),
+        base[...], picks, (((0,), (0,)), ((), ())),
         precision=lax.Precision.HIGHEST, preferred_element_type=F32,
     )
     values = jnp.sum(
@@ -301,10 +304,33 @@
     )
 
 
-def les_kernel(rho, rest, x_even, x_odd, y_even, y_odd, z_face, out):
+def les_kernel(
+    level, rho, rest, wave, y_odd, y_even, x_odd, x_even, z_face, late_odd, late_even, out, base
+):
     sec = lax.axis_index("sec")
     x_low, x_high, y_low, y_high = sides(x_even, x_odd, y_even, y_odd)
-    lane = iota((32, 128), 1)
+    below, above, _, _ = sides(late_even, late_odd, y_even, y_odd)
+    mean_flow, _ = factors(level)
+    z_pressure = as_column(z_face[20:21])
+    for x in range(8):
+        def row(part, at):
+            if 0 <= at <= 7:
+                return wave[part * 128 + at * 16 : part * 128 + at * 16 + 16]
+            early, rest_of = (x_low, below) if at < 0 else (x_high, above)
+            if part < 2:
+                return early[64 + 16 * part : 80 + 16 * part]
+            return rest_of[128 + 16 * part : 144 + 16 * part]
+
+        now = row(0, x)
+        across = 0.5 * (up(now, y_high[80 + x : 81 + x]) - down(now, y_low[80 + x : 81 + x]))
+        deep = derive_z(now, z_pressure[x * 16 : x * 16 + 16], sec)
+        along = [0.5 * (row(part, x + 1) - row(part, x - 1)) for part in range(4)]
+        for part, gradient in ((1, along[0]), (2, across), (3, deep)):
+            start = part * 128 - 128 + x * 16
+            base[start : start + 16] = row(part, x) - WAVE_STEP * (
+                mean_flow * along[part] + gradient
+            )
+    x_low, x_high = below, above
     z_rho = safe(z_face[0:4])
     z_v = z_face[12:16] / z_rho
     y_low_v = y_low[32:48] / safe(y_low[0:16])
@@ -344,7 +370,7 @@
             out[start : start + 32] = now - LES_STEP * (along + across + deep)
 
 
-def finish_kernel(arrived, base, out, far):
+def finish_kernel(arrived, pressure, base, out, far):
     names = jnp.transpose(arrived[pl.ds(CAP * 3 // 2, 128, stride=ROWS)])
     place = iota((256, 128), 0)
     patch = (place % 128 * 2 + place // 128).astype(F32)
@@ -376,10 +402,10 @@
         jnp.where(half, pltpu.roll(even, 64, 1), odd),
         jnp.where(half, third[0:128], third[128:256]),
     ]
-    out[0:128] = base[0:128]
+    out[0:128] = pressure[...]
     for part in range(3):
-        here = slice(part * 128 + 128, part * 128 + 256)
-        out[here] = base[here] - WAVE_STEP * source[part]
+        here = slice(part * 128, part * 128 + 128)
+        out[part * 128 + 128 : part * 128 + 256] = base[here] - WAVE_STEP * source[part]
     shares = arrived[pl.ds(CAP * 3 // 2 + 1, 128, stride=ROWS)]
     far[...] = jnp.sum(shares, axis=0, keepdims=True)
 
@@ -419,49 +445,46 @@
     weights = block_weights.reshape(512 * 64, 128)
     hbm = pl.BlockSpec(memory_space=pltpu.HBM)
     vmem = pl.BlockSpec(memory_space=pltpu.VMEM)
-    smem = pl.BlockSpec(memory_space=pltpu.SMEM)
     pinned = lambda x: pltpu.with_memory_space_constraint(x, pltpu.HBM)
-    with jax.named_scope("pack_x"):
-        faces = call(
-            pack_x_kernel,
-            [((224, 128), F32)] * 2,
-            1 << 10, 1 << 20,
+    with jax.named_scope("pack_y"):
+        y_even, y_odd = call(
+            pack_y_kernel,
+            [((104, 128), F32)] * 2,
+            1 << 18, 1 << 20,
             in_specs=[hbm] * 4,
-            scratch_shapes=[pltpu.SemaphoreType.DMA((2, 9))],
-        )(pinned(rho), pinned(rest), pinned(wave), pinned(far_kernel))
-    x_even = exchange(faces[0], "gx", 0)
-    x_odd = exchange(faces[1], "gx", 1)
+            scratch_shapes=[pltpu.VMEM((5, 16, 8, 128), F32)] * 2
+            + [pltpu.VMEM((2, 8, 8, 128), F32)] * 2
+            + [pltpu.SemaphoreType.DMA((8,))],
+        )(pinned(les_density), pinned(les_rest), pinned(acoustic), pinned(far_kernel))
     with jax.named_scope("pack"):
-        faces = call(
+        x_odd, x_even, z_face = call(
             pack_kernel,
             [((96, 128), F32)] * 2 + [((24, 128), F32)],
             1 << 20, 2 << 20,
-        )(rho, rest, wave)
-    y_even = exchange(faces[0], "row", 0)
-    y_odd = exchange(faces[1], "row", 1)
-    z_face = exchange(faces[2], "sec", 0)
-    halos = [x_even, x_odd, y_even, y_odd, z_face]
+            in_specs=[vmem] * 3 + [hbm, vmem],
+        )(rho, rest, wave, pinned(weights), y_even)
+    halos = [
+        exchange(y_odd, "row", 1),
+        exchange(y_even, "row", 0),
+        exchange(x_odd, "gx", 1),
+        exchange(x_even, "gx", 0),
+        exchange(z_face, "sec", 0),
+    ]
     with jax.named_scope("slots"):
         slots, valid, patches = call(
             slot_kernel,
             [((CAP * 128, 512), BF16), ((512, 128), F32), ((512, 128), BF16)],
             1 << 22, 2 << 20,
-            in_specs=[vmem] * 3 + [hbm],
         )(
             block_owner.reshape(4, 128),
             block_counts.reshape(4, 128),
             block_patch.reshape(4, 128),
-            pinned(weights),
         )
-    with jax.named_scope("wave"):
-        base, share = call(
-            wave_kernel,
-            [((512, 128), F32), ((8, 128), F32)],
-            1 << 24, 2 << 20,
-            in_specs=[smem] + [vmem] * 8,
-        )(
-            tile_class.reshape(1, 1), wave, *halos, sample_index.reshape(1, 128), far_kernel
-        )
+    level = tile_class.reshape(1, 1)
+    with jax.named_scope("pressure"):
+        pressure, share = call(
+            pressure_kernel, [((128, 128), F32), ((8, 128), F32)], 1 << 24, 2 << 20,
+        )(level, wave, *halos, sample_index.reshape(1, 128), far_kernel)
     other = exchange(share, "sec", 0)
     with jax.named_scope("payload"):
         (payload,) = call(
@@ -489,12 +512,20 @@
     arrived = lax.all_to_all(
         send.reshape(128, 1, ROWS * 128), ("gx", "row"), split_axis=0, concat_axis=0, tiled=True
     )
+    with jax.named_scope("late"):
+        late_odd, late_even = call(
+            late_kernel, [((192, 128), F32)] * 2, 1 << 10, 1 << 19, in_specs=[vmem] * 3 + [hbm],
+        )(rho, rest, wave, pinned(send))
+    late_odd = exchange(late_odd, "gx", 1)
+    late_even = exchange(late_even, "gx", 0)
     with jax.named_scope("les"):
-        (les_next,) = call(les_kernel, [((2560, 128), F32)], 1 << 23, 4 << 20)(rho, rest, *halos)
+        les_next, base = call(
+            les_kernel, [((2560, 128), F32), ((384, 128), F32)], 1 << 23, 4 << 20
+        )(level, rho, rest, wave, *halos, late_odd, late_even)
     with jax.named_scope("finish"):
         wave_next, far_field = call(
             finish_kernel, [((512, 128), F32), ((1, 128), F32)], 1 << 28, 3 << 20,
-        )(arrived.reshape(128 * ROWS, 128), base)
+        )(arrived.reshape(128 * ROWS, 128), pressure, base)
     return (
         les_next.reshape(5, 16, 32, 128),
         wave_next.reshape(4, 8, 16, 128),

time: 72.5 us -> 70.7 us (0.975)
  waiting for transfers between devices: 30.1 us -> 26.6 us
  starting transfers between devices: 28.6 us -> 30.7 us
  local copies, waits for them, and re-layouts: 0.85 us -> 0.05 us
    ppermute x6 -> x8, starting transfers between devices: 11.3 us -> 19.9 us  [exchange(): return lax.ppermute(face, axis, pairs)]
    all_to_all x1, waiting for transfers between devices: 30.1 us -> 23 us  [per_device(): lax.all_to_all(send.reshape(128, 1, ROWS * 128), ('gx', 'row'), split_axi...]
    all_to_all x1, starting transfers between devices: 17.3 us -> 10.8 us  [per_device(): lax.all_to_all(send.reshape(128, 1, ROWS * 128), ('gx', 'row'), split_axi...]
    ppermute x6 -> x8, waiting for transfers between devices: 0.02 us -> 3.59 us  [exchange(): return lax.ppermute(face, axis, pairs)]
    unnamed x18, local copies, waits for them, and re-layouts: 0.85 us -> 0.05 us
    pallas_call x3 -> x4, Pallas kernels: 4.47 us -> 4.86 us  [the longest x1 2.79 us: per_device(): call(les_kernel, [((2560, 128), F32), ((384, 128), F32)], 1 << 23, 4 << 20)]
  transfers between devices with their start and end apart: 7 -> 9, of which waited for: 1 -> 3; matrix products, arithmetic and copies ran while one was open for 0% -> 0% of each run, Pallas kernels for 9% -> 9%
where the time goes in v5:
time: 70.7 us; the launch traced here: 70.4 us
  starting transfers between devices  30.7 us (43%)
  waiting for transfers between devices  26.6 us (38%)
  Pallas kernels  11.5 us (16%)
  between operations  1.51 us (2%)
    all_to_all x1, waiting for transfers between devices, per_device(): lax.all_to_all(send.reshape(128, 1, ROWS * 128), ('gx', 'row'), split_axi...  23 us
    ppermute x8, starting transfers between devices, exchange(): return lax.ppermute(face, axis, pairs)  19.9 us
    all_to_all x1, starting transfers between devices, per_device(): lax.all_to_all(send.reshape(128, 1, ROWS * 128), ('gx', 'row'), split_axi...  10.8 us
    ppermute x8, waiting for transfers between devices, exchange(): return lax.ppermute(face, axis, pairs)  3.59 us
    pallas_call x1, Pallas kernels, per_device(): call(les_kernel, [((2560, 128), F32), ((384, 128), F32)], 1 << 23, 4 << 20)  2.79 us
    pallas_call x1, Pallas kernels, per_device(): call(payload_kernel, [((512, 384), BF16)], 1 << 27, 16 << 20, 24, in_spec...  2.55 us
    pallas_call x1, Pallas kernels, per_device(): call(place_kernel, [((128 * ROWS, 128), F32)], 1 << 28, 3 << 20, out_spec...  1.7 us
  transfers between devices with their start and end apart: 9, of which 3 were waited for; matrix products, arithmetic and copies ran while one was open for 0% of the time, Pallas kernels for 9%

profile of v5, /device:TPU:1, one launch (start us, length us, event | category | flops | bytes accessed | tf_op | source)
XLA Modules:
  0.0 70.4 jit_solution(15427500563473824241)
XLA Ops:
  0.7 1.4 %pack_y.1 = (f32[104,128]{1,0:T(8,128)S(1)}, f32[104,128]{1,0:T(8,128)S(1)}) custom-call(f32[16,32,128]{2,1,0:T(8,128)} %rho.1, f32[4,16,32,128]{3,2,1,0:T(8,128)} %rest.1, f32[4,8,16,128]{3,2,1,0:T(8,128)} %wave.1, f32[128,128]{1,0:T(8,128)} %far.3), custom_call_target="tpu_custom_call" | custom-call | flops 262144 | bytes 1048576 | tf_op jit(solution)/shard_map/pack_y/pallas_call | solution.py:450
  2.0 0.7 collective-permute-start
  2.7 9.4 %collective-permute-start.1 = (f32[104,128]{1,0:T(8,128)S(1)}, f32[104,128]{1,0:T(8,128)S(1)}, u32[]{:S(2)}, u32[]{:S(2)}) collective-permute-start(f32[104,128]{1,0:T(8,128)S(1)} %get-tuple-element.20.after), channel_id=1, source_target_pairs={{0,1},{1,0},{2,3},{3,2},{4,5},{5,4},{6,7},{7,6},{8,9},{9,8},{10,11... | collective-permute-start | bytes 159752 | tf_op jit(solution)/shard_map/ppermute | solution.py:427
  12.1 0.0 copy-start.7
  12.1 0.0 copy-start.8
  12.1 0.0 copy-start.5
  12.1 0.0 copy-start
  12.1 0.5 pack.1
  12.6 4.5 %collective-permute-start.2 = (f32[96,128]{1,0:T(8,128)S(1)}, f32[96,128]{1,0:T(8,128)S(1)}, u32[]{:S(2)}, u32[]{:S(2)}) collective-permute-start(f32[96,128]{1,0:T(8,128)S(1)} %get-tuple-element.21), channel_id=1, source_target_pairs={{16,32},{32,16},{48,64},{64,48},{80,96},{96,80},{17,33},{33,17},{4... | collective-permute-start | bytes 147464 | tf_op jit(solution)/shard_map/ppermute | solution.py:427
  17.1 0.1 collective-permute-start.3
  17.2 0.8 %collective-permute-start.4 = (f32[24,128]{1,0:T(8,128)S(1)}, f32[24,128]{1,0:T(8,128)S(1)}, u32[]{:S(2)}, u32[]{:S(2)}) collective-permute-start(f32[24,128]{1,0:T(8,128)S(1)} %get-tuple-element.23), channel_id=1, source_target_pairs={{0,128},{128,0},{1,129},{129,1},{2,130},{130,2},{3,131},{131,3},{4... | collective-permute-start | bytes 36872 | tf_op jit(solution)/shard_map/ppermute | solution.py:427
  18.7 0.6 slots.1
  19.3 0.5 collective-permute-done.4.z_face
  19.9 0.7 pressure.1
  20.6 0.8 %collective-permute-start.5 = (f32[8,128]{1,0:T(8,128)S(1)}, f32[8,128]{1,0:T(8,128)S(1)}, u32[]{:S(2)}, u32[]{:S(2)}) collective-permute-start(f32[8,128]{1,0:T(8,128)S(1)} %get-tuple-element.27.share), channel_id=1, source_target_pairs={{0,128},{128,0},{1,129},{129,1},{2,130},{130,2},{3,131},{131,3},{4... | collective-permute-start | bytes 12296 | tf_op jit(solution)/shard_map/ppermute | solution.py:427
  21.3 2.5 %payload.1 = bf16[512,384]{1,0:T(8,128)(2,1)S(1)} custom-call(f32[512,128]{1,0:T(8,128)S(1)} %bitcast.23, f32[2048,128]{1,0:T(8,128)S(1)} %bitcast.19, f32[104,128]{1,0:T(8,128)S(1)} %collective-permute-done.y_odd, f32[104,128]{1,0:T(8,128)S(1)} %collective-permute-done.1.y_even, f32[96,128]{1,0:T(8,128)S(1)} %collective-permute-done.2.x_odd, ...), custom_call_target="tpu_custom_call" | custom-call | flops 134217728 | bytes 16777216 | tf_op jit(solution)/shard_map/payload/pallas_call | solution.py:490
  23.9 1.7 %place.1.token = f32[2176,128]{1,0:T(8,128)} custom-call(bf16[1280,512]{1,0:T(8,128)(2,1)S(1)} %get-tuple-element.24.slots, bf16[512,384]{1,0:T(8,128)(2,1)S(1)} %payload.1, bf16[512,128]{1,0:T(8,128)(2,1)S(1)} %get-tuple-element.26.patches, f32[8,128]{1,0:T(8,128)S(1)} %get-tuple-element.27.share, f32[8,128]{1,0:T(8,128)S(1)} %collective-permute-done.5.other), custom_call_target="tpu_custom_call" | custom-call | flops 268435456 | bytes 3145728 | tf_op jit(solution)/shard_map/place/pallas_call | solution.py:502
  25.6 10.8 %all-to-all-start = ((f32[128,1,2176]{2,1,0:T(1,128)}), f32[128,1,2176]{2,1,0:T(1,128)S(1)}, u32[]{:S(2)}, u32[]{:S(2)}) async-start(f32[128,1,2176]{2,1,0:T(1,128)} %bitcast.10), calls=%async_computation | async-start | bytes 2228224 | tf_op jit(solution)/shard_map/all_to_all | solution.py:512
  36.4 3.6 %collective-permute-start.6 = (f32[192,128]{1,0:T(8,128)S(1)}, f32[192,128]{1,0:T(8,128)S(1)}, u32[]{:S(2)}, u32[]{:S(2)}) collective-permute-start(f32[192,128]{1,0:T(8,128)S(1)} %get-tuple-element.28), channel_id=1, source_target_pairs={{16,32},{32,16},{48,64},{64,48},{80,96},{96,80},{17,33},{33,17},{4... | collective-permute-start | bytes 294920 | tf_op jit(solution)/shard_map/ppermute | solution.py:427
  40.1 0.1 collective-permute-start.7
  40.2 3.0 %collective-permute-done.6.late_odd = f32[192,128]{1,0:T(8,128)S(1)} collective-permute-done((f32[192,128]{1,0:T(8,128)S(1)}, f32[192,128]{1,0:T(8,128)S(1)}, u32[]{:S(2)}, u32[]{:S(2)}) %collective-permute-start.6) | collective-permute-done | bytes 98336 | tf_op jit(solution)/shard_map/ppermute | solution.py:427
  43.2 2.8 %les.1 = (f32[2560,128]{1,0:T(8,128)}, f32[384,128]{1,0:T(8,128)S(1)}) custom-call(s32[1,1]{1,0:T(1,128)} %bitcast.15.level, f32[512,128]{1,0:T(8,128)S(1)} %bitcast.25, f32[2048,128]{1,0:T(8,128)S(1)} %bitcast.21, f32[512,128]{1,0:T(8,128)S(1)} %bitcast.29, f32[104,128]{1,0:T(8,128)S(1)} %collective-permute-done.y_odd, ...), custom_call_target="tpu_custom_call" | custom-call | flops 8388608 | bytes 4194304 | tf_op jit(solution)/shard_map/les/pallas_call | solution.py:522
  46.0 23.0 %all-to-all-done = f32[128,1,2176]{2,1,0:T(1,128)S(1)} async-done(((f32[128,1,2176]{2,1,0:T(1,128)}), f32[128,1,2176]{2,1,0:T(1,128)S(1)}, u32[]{:S(2)}, u32[]{:S(2)}) %all-to-all-start) | async-done | bytes 1114144 | tf_op jit(solution)/shard_map/all_to_all | solution.py:512
  69.0 1.3 %finish.1 = (f32[512,128]{1,0:T(8,128)}, f32[1,128]{1,0:T(1,128)}) custom-call(f32[2176,128]{1,0:T(8,128)S(1)} %bitcast.30, f32[128,128]{1,0:T(8,128)S(1)} %get-tuple-element.31.pressure, f32[384,128]{1,0:T(8,128)S(1)} %get-tuple-element.32.base), custom_call_target="tpu_custom_call" | custom-call | flops 268435456 | bytes 3145728 | tf_op jit(solution)/shard_map/finish/pallas_call | solution.py:526
  (21 shorter events, 0.1 us)
Async XLA Ops:
  0.6 11.4 %copy-start.3 = (f32[4,8,16,128]{3,2,1,0:T(8,128)S(1)}, f32[4,8,16,128]{3,2,1,0:T(8,128)}, u32[]{:S(2)}) copy-start(f32[4,8,16,128]{3,2,1,0:T(8,128)} %wave.1) | copy-start | bytes 786436
  0.6 11.4 %copy-start.1 = (f32[4,16,32,128]{3,2,1,0:T(8,128)S(1)}, f32[4,16,32,128]{3,2,1,0:T(8,128)}, u32[]{:S(2)}) copy-start(f32[4,16,32,128]{3,2,1,0:T(8,128)} %rest.1) | copy-start | bytes 3145732
  0.7 11.4 %copy-start.2 = (f32[16,32,128]{2,1,0:T(8,128)S(1)}, f32[16,32,128]{2,1,0:T(8,128)}, u32[]{:S(2)}) copy-start(f32[16,32,128]{2,1,0:T(8,128)} %rho.1) | copy-start | bytes 786436
  2.0 17.8 %collective-permute-start = (f32[104,128]{1,0:T(8,128)S(1)}, f32[104,128]{1,0:T(8,128)S(1)}, u32[]{:S(2)}, u32[]{:S(2)}) collective-permute-start(f32[104,128]{1,0:T(8,128)S(1)} %get-tuple-element.19), channel_id=1, source_target_pairs={{1,2},{2,1},{3,4},{4,3},{5,6},{6,5},{7,8},{8,7},{9,10},{10,9},{11,... | collective-permute-start | bytes 159752 | tf_op jit(solution)/shard_map/ppermute | solution.py:427
  2.7 17.2 %collective-permute-start.1 = (f32[104,128]{1,0:T(8,128)S(1)}, f32[104,128]{1,0:T(8,128)S(1)}, u32[]{:S(2)}, u32[]{:S(2)}) collective-permute-start(f32[104,128]{1,0:T(8,128)S(1)} %get-tuple-element.20.after), channel_id=1, source_target_pairs={{0,1},{1,0},{2,3},{3,2},{4,5},{5,4},{6,7},{7,6},{8,9},{9,8},{10,11... | collective-permute-start | bytes 159752 | tf_op jit(solution)/shard_map/ppermute | solution.py:427
  12.1 6.6 %copy-start.6 = (s32[512,1]{0,1:T(1,128)S(1)}, s32[512,1]{0,1:T(1,128)}, u32[]{:S(2)}) copy-start(s32[512,1]{0,1:T(1,128)} %param.13) | copy-start | bytes 6148
  12.1 6.6 %copy-start.7 = (s32[512]{0:T(512)S(1)}, s32[512]{0:T(512)}, u32[]{:S(2)}) copy-start(s32[512]{0:T(512)} %param.15) | copy-start | bytes 6148
  12.1 6.6 %copy-start.8 = (s32[512]{0:T(512)S(1)}, s32[512]{0:T(512)}, u32[]{:S(2)}) copy-start(s32[512]{0:T(512)} %param.16) | copy-start | bytes 6148
  12.1 7.8 %copy-start.4 = (f32[128,128]{1,0:T(8,128)S(1)}, f32[128,128]{1,0:T(8,128)}, u32[]{:S(2)}) copy-start(f32[128,128]{1,0:T(8,128)} %far.3) | copy-start | bytes 196612
  12.1 7.8 %copy-start.5 = (s32[128]{0:T(128)S(1)}, s32[128]{0:T(128)}, u32[]{:S(2)}) copy-start(s32[128]{0:T(128)} %param.18) | copy-start | bytes 1540
  12.1 9.2 %copy-start = (bf16[512,64,128]{2,1,0:T(8,128)(2,1)S(1)}, bf16[512,64,128]{2,1,0:T(8,128)(2,1)}, u32[]{:S(2)}) copy-start(bf16[512,64,128]{2,1,0:T(8,128)(2,1)} %param.14) | copy-start | bytes 25165828
  12.6 7.2 %collective-permute-start.2 = (f32[96,128]{1,0:T(8,128)S(1)}, f32[96,128]{1,0:T(8,128)S(1)}, u32[]{:S(2)}, u32[]{:S(2)}) collective-permute-start(f32[96,128]{1,0:T(8,128)S(1)} %get-tuple-element.21), channel_id=1, source_target_pairs={{16,32},{32,16},{48,64},{64,48},{80,96},{96,80},{17,33},{33,17},{4... | collective-permute-start | bytes 147464 | tf_op jit(solution)/shard_map/ppermute | solution.py:427
  17.1 2.7 %collective-permute-start.3 = (f32[96,128]{1,0:T(8,128)S(1)}, f32[96,128]{1,0:T(8,128)S(1)}, u32[]{:S(2)}, u32[]{:S(2)}) collective-permute-start(f32[96,128]{1,0:T(8,128)S(1)} %get-tuple-element.22), channel_id=1, source_target_pairs={{0,16},{16,0},{32,48},{48,32},{64,80},{80,64},{96,112},{112,96},{1... | collective-permute-start | bytes 147464 | tf_op jit(solution)/shard_map/ppermute | solution.py:427
  17.2 2.6 %collective-permute-start.4 = (f32[24,128]{1,0:T(8,128)S(1)}, f32[24,128]{1,0:T(8,128)S(1)}, u32[]{:S(2)}, u32[]{:S(2)}) collective-permute-start(f32[24,128]{1,0:T(8,128)S(1)} %get-tuple-element.23), channel_id=1, source_target_pairs={{0,128},{128,0},{1,129},{129,1},{2,130},{130,2},{3,131},{131,3},{4... | collective-permute-start | bytes 36872 | tf_op jit(solution)/shard_map/ppermute | solution.py:427
  20.6 3.3 %collective-permute-start.5 = (f32[8,128]{1,0:T(8,128)S(1)}, f32[8,128]{1,0:T(8,128)S(1)}, u32[]{:S(2)}, u32[]{:S(2)}) collective-permute-start(f32[8,128]{1,0:T(8,128)S(1)} %get-tuple-element.27.share), channel_id=1, source_target_pairs={{0,128},{128,0},{1,129},{129,1},{2,130},{130,2},{3,131},{131,3},{4... | collective-permute-start | bytes 12296 | tf_op jit(solution)/shard_map/ppermute | solution.py:427
  25.6 43.4 %all-to-all-start = ((f32[128,1,2176]{2,1,0:T(1,128)}), f32[128,1,2176]{2,1,0:T(1,128)S(1)}, u32[]{:S(2)}, u32[]{:S(2)}) async-start(f32[128,1,2176]{2,1,0:T(1,128)} %bitcast.10), calls=%async_computation | async-start | bytes 2228224 | tf_op jit(solution)/shard_map/all_to_all | solution.py:512
  36.4 6.8 %collective-permute-start.6 = (f32[192,128]{1,0:T(8,128)S(1)}, f32[192,128]{1,0:T(8,128)S(1)}, u32[]{:S(2)}, u32[]{:S(2)}) collective-permute-start(f32[192,128]{1,0:T(8,128)S(1)} %get-tuple-element.28), channel_id=1, source_target_pairs={{16,32},{32,16},{48,64},{64,48},{80,96},{96,80},{17,33},{33,17},{4... | collective-permute-start | bytes 294920 | tf_op jit(solution)/shard_map/ppermute | solution.py:427
  40.1 3.2 %collective-permute-start.7 = (f32[192,128]{1,0:T(8,128)S(1)}, f32[192,128]{1,0:T(8,128)S(1)}, u32[]{:S(2)}, u32[]{:S(2)}) collective-permute-start(f32[192,128]{1,0:T(8,128)S(1)} %get-tuple-element.29), channel_id=1, source_target_pairs={{0,16},{16,0},{32,48},{48,32},{64,80},{80,64},{96,112},{112,96},{1... | collective-permute-start | bytes 294920 | tf_op jit(solution)/shard_map/ppermute | solution.py:427

commit v6 on v5

--- a/solution.py
+++ b/solution.py
@@ -96,7 +96,7 @@
                 z_face[line : line + 1] = edge_line(
                     ref[piece * 128 : piece * 128 + 128], lane, eye
                 )
-    z_face[22:24] = jnp.zeros((2, 128), F32)
+    z_face[22:100] = jnp.zeros((78, 128), F32)
 
 
 def late_kernel(rho, rest, wave, token, x_odd, x_even):
@@ -169,6 +169,7 @@
     half = iota((16, 128), 1) < 64
     keep = [(group // 4 == part).astype(F32).astype(BF16) for part in range(4)]
     column = iota((64, 48), 1) % 4
+    wide = iota((16, 256), 1) // 64 == iota((16, 256), 0) % 4
 
     for x in range(16):
         at = x * 32
@@ -209,14 +210,24 @@
                 ],
                 axis=1,
             )
-            product = lax.dot_general(
-                right, left, (((1,), (1,)), ((), ())), preferred_element_type=F32
-            )
-            merged = product[0:64]
-            for k in range(1, 4):
-                merged = jnp.where(column == k, product[k * 64 : k * 64 + 64], merged)
-            turned = jnp.transpose(jnp.concatenate([merged, merged], axis=0))
-            folded = [turned[c * 16 : c * 16 + 16] for c in range(3)]
+            if part == 1 or x % 2 == 1:
+                product = lax.dot_general(
+                    left, right, (((1,), (1,)), ((), ())), preferred_element_type=F32
+                )
+                folded = []
+                for c in range(3):
+                    picked = jnp.where(wide, product[c * 16 : c * 16 + 16], 0.0)
+                    both = picked[:, 0:128] + picked[:, 128:256]
+                    folded.append(both + pltpu.roll(both, 64, 1))
+            else:
+                product = lax.dot_general(
+                    right, left, (((1,), (1,)), ((), ())), preferred_element_type=F32
+                )
+                merged = product[0:64]
+                for k in range(1, 4):
+                    merged = jnp.where(column == k, product[k * 64 : k * 64 + 64], merged)
+                turned = jnp.transpose(jnp.concatenate([merged, merged], axis=0))
+                folded = [turned[c * 16 : c * 16 + 16] for c in range(3)]
             pair = jnp.where(half, folded[0], folded[1])
             pair_top = pair.astype(BF16)
             pair_rest = (pair - pair_top.astype(F32)).astype(BF16)
@@ -459,7 +470,7 @@
     with jax.named_scope("pack"):
         x_odd, x_even, z_face = call(
             pack_kernel,
-            [((96, 128), F32)] * 2 + [((24, 128), F32)],
+            [((96, 128), F32)] * 2 + [((100, 128), F32)],
             1 << 20, 2 << 20,
             in_specs=[vmem] * 3 + [hbm, vmem],
         )(rho, rest, wave, pinned(weights), y_even)

time: 70.7 us -> 70 us (0.990)
  no operation moved by 1% of the time
where the time goes in v6:
time: 70 us; the launch traced here: 69.7 us
  starting transfers between devices  30.6 us (44%)
  waiting for transfers between devices  26.3 us (38%)
  Pallas kernels  11.3 us (16%)
  between operations  1.51 us (2%)
    all_to_all x1, waiting for transfers between devices, per_device(): lax.all_to_all(send.reshape(128, 1, ROWS * 128), ('gx', 'row'), split_axi...  22.9 us
    ppermute x8, starting transfers between devices, exchange(): return lax.ppermute(face, axis, pairs)  20.2 us
    all_to_all x1, starting transfers between devices, per_device(): lax.all_to_all(send.reshape(128, 1, ROWS * 128), ('gx', 'row'), split_axi...  10.4 us
    ppermute x8, waiting for transfers between devices, exchange(): return lax.ppermute(face, axis, pairs)  3.45 us
    pallas_call x1, Pallas kernels, per_device(): call(les_kernel, [((2560, 128), F32), ((384, 128), F32)], 1 << 23, 4 << 20)  2.79 us
    pallas_call x1, Pallas kernels, per_device(): call(payload_kernel, [((512, 384), BF16)], 1 << 27, 16 << 20, 24, in_spec...  2.29 us
    pallas_call x1, Pallas kernels, per_device(): call(place_kernel, [((128 * ROWS, 128), F32)], 1 << 28, 3 << 20, out_spec...  1.69 us
  transfers between devices with their start and end apart: 9, of which 3 were waited for; matrix products, arithmetic and copies ran while one was open for 0% of the time, Pallas kernels for 9%

profile of v6, /device:TPU:1, one launch (start us, length us, event | category | flops | bytes accessed | tf_op | source)
XLA Modules:
  0.0 69.7 jit_solution(13094121692579028901)
XLA Ops:
  0.7 1.4 %pack_y.1 = (f32[104,128]{1,0:T(8,128)S(1)}, f32[104,128]{1,0:T(8,128)S(1)}) custom-call(f32[16,32,128]{2,1,0:T(8,128)} %rho.1, f32[4,16,32,128]{3,2,1,0:T(8,128)} %rest.1, f32[4,8,16,128]{3,2,1,0:T(8,128)} %wave.1, f32[128,128]{1,0:T(8,128)} %far.3), custom_call_target="tpu_custom_call" | custom-call | flops 262144 | bytes 1048576 | tf_op jit(solution)/shard_map/pack_y/pallas_call | solution.py:461
  2.0 0.7 collective-permute-start
  2.7 9.4 %collective-permute-start.1 = (f32[104,128]{1,0:T(8,128)S(1)}, f32[104,128]{1,0:T(8,128)S(1)}, u32[]{:S(2)}, u32[]{:S(2)}) collective-permute-start(f32[104,128]{1,0:T(8,128)S(1)} %get-tuple-element.20.after), channel_id=1, source_target_pairs={{0,1},{1,0},{2,3},{3,2},{4,5},{5,4},{6,7},{7,6},{8,9},{9,8},{10,11... | collective-permute-start | bytes 159752 | tf_op jit(solution)/shard_map/ppermute | solution.py:438
  12.1 0.0 copy-start.7
  12.1 0.0 copy-start.8
  12.1 0.0 copy-start.4
  12.1 0.0 copy-start.5
  12.1 0.5 pack.1
  12.6 0.8 %collective-permute-start.4 = (f32[100,128]{1,0:T(8,128)S(1)}, f32[100,128]{1,0:T(8,128)S(1)}, u32[]{:S(2)}, u32[]{:S(2)}) collective-permute-start(f32[100,128]{1,0:T(8,128)S(1)} %get-tuple-element.23), channel_id=1, source_target_pairs={{0,128},{128,0},{1,129},{129,1},{2,130},{130,2},{3,131},{131,3},{4... | collective-permute-start | bytes 153608 | tf_op jit(solution)/shard_map/ppermute | solution.py:438
  13.4 4.8 %collective-permute-start.2 = (f32[96,128]{1,0:T(8,128)S(1)}, f32[96,128]{1,0:T(8,128)S(1)}, u32[]{:S(2)}, u32[]{:S(2)}) collective-permute-start(f32[96,128]{1,0:T(8,128)S(1)} %get-tuple-element.21), channel_id=1, source_target_pairs={{16,32},{32,16},{48,64},{64,48},{80,96},{96,80},{17,33},{33,17},{4... | collective-permute-start | bytes 147464 | tf_op jit(solution)/shard_map/ppermute | solution.py:438
  18.2 0.1 collective-permute-start.3
  19.0 0.6 slots.1
  19.6 0.4 collective-permute-done.2.x_odd
  20.0 0.7 pressure.1
  20.7 0.8 %collective-permute-start.5 = (f32[8,128]{1,0:T(8,128)S(1)}, f32[8,128]{1,0:T(8,128)S(1)}, u32[]{:S(2)}, u32[]{:S(2)}) collective-permute-start(f32[8,128]{1,0:T(8,128)S(1)} %get-tuple-element.27.share), channel_id=1, source_target_pairs={{0,128},{128,0},{1,129},{129,1},{2,130},{130,2},{3,131},{131,3},{4... | collective-permute-start | bytes 12296 | tf_op jit(solution)/shard_map/ppermute | solution.py:438
  21.5 2.3 %payload.1 = bf16[512,384]{1,0:T(8,128)(2,1)S(1)} custom-call(f32[512,128]{1,0:T(8,128)S(1)} %bitcast.23, f32[2048,128]{1,0:T(8,128)S(1)} %bitcast.19, f32[104,128]{1,0:T(8,128)S(1)} %collective-permute-done.y_odd, f32[104,128]{1,0:T(8,128)S(1)} %collective-permute-done.1.y_even, f32[96,128]{1,0:T(8,128)S(1)} %collective-permute-done.2.x_odd, ...), custom_call_target="tpu_custom_call" | custom-call | flops 134217728 | bytes 16777216 | tf_op jit(solution)/shard_map/payload/pallas_call | solution.py:501
  23.8 1.7 %place.1.token = f32[2176,128]{1,0:T(8,128)} custom-call(bf16[1280,512]{1,0:T(8,128)(2,1)S(1)} %get-tuple-element.24.slots, bf16[512,384]{1,0:T(8,128)(2,1)S(1)} %payload.1, bf16[512,128]{1,0:T(8,128)(2,1)S(1)} %get-tuple-element.26.patches, f32[8,128]{1,0:T(8,128)S(1)} %get-tuple-element.27.share, f32[8,128]{1,0:T(8,128)S(1)} %collective-permute-done.5.other), custom_call_target="tpu_custom_call" | custom-call | flops 268435456 | bytes 3145728 | tf_op jit(solution)/shard_map/place/pallas_call | solution.py:513
  25.5 10.4 %all-to-all-start = ((f32[128,1,2176]{2,1,0:T(1,128)}), f32[128,1,2176]{2,1,0:T(1,128)S(1)}, u32[]{:S(2)}, u32[]{:S(2)}) async-start(f32[128,1,2176]{2,1,0:T(1,128)} %bitcast.10), calls=%async_computation | async-start | bytes 2228224 | tf_op jit(solution)/shard_map/all_to_all | solution.py:523
  35.9 3.6 %collective-permute-start.6 = (f32[192,128]{1,0:T(8,128)S(1)}, f32[192,128]{1,0:T(8,128)S(1)}, u32[]{:S(2)}, u32[]{:S(2)}) collective-permute-start(f32[192,128]{1,0:T(8,128)S(1)} %get-tuple-element.28), channel_id=1, source_target_pairs={{16,32},{32,16},{48,64},{64,48},{80,96},{96,80},{17,33},{33,17},{4... | collective-permute-start | bytes 294920 | tf_op jit(solution)/shard_map/ppermute | solution.py:438
  39.5 0.1 collective-permute-start.7
  39.6 3.0 %collective-permute-done.6.late_odd = f32[192,128]{1,0:T(8,128)S(1)} collective-permute-done((f32[192,128]{1,0:T(8,128)S(1)}, f32[192,128]{1,0:T(8,128)S(1)}, u32[]{:S(2)}, u32[]{:S(2)}) %collective-permute-start.6) | collective-permute-done | bytes 98336 | tf_op jit(solution)/shard_map/ppermute | solution.py:438
  42.7 2.8 %les.1 = (f32[2560,128]{1,0:T(8,128)}, f32[384,128]{1,0:T(8,128)S(1)}) custom-call(s32[1,1]{1,0:T(1,128)} %bitcast.15.level, f32[512,128]{1,0:T(8,128)S(1)} %bitcast.25, f32[2048,128]{1,0:T(8,128)S(1)} %bitcast.21, f32[512,128]{1,0:T(8,128)S(1)} %bitcast.29, f32[104,128]{1,0:T(8,128)S(1)} %collective-permute-done.y_odd, ...), custom_call_target="tpu_custom_call" | custom-call | flops 8388608 | bytes 4194304 | tf_op jit(solution)/shard_map/les/pallas_call | solution.py:533
  45.5 22.9 %all-to-all-done = f32[128,1,2176]{2,1,0:T(1,128)S(1)} async-done(((f32[128,1,2176]{2,1,0:T(1,128)}), f32[128,1,2176]{2,1,0:T(1,128)S(1)}, u32[]{:S(2)}, u32[]{:S(2)}) %all-to-all-start) | async-done | bytes 1114144 | tf_op jit(solution)/shard_map/all_to_all | solution.py:523
  68.3 1.3 %finish.1 = (f32[512,128]{1,0:T(8,128)}, f32[1,128]{1,0:T(1,128)}) custom-call(f32[2176,128]{1,0:T(8,128)S(1)} %bitcast.30, f32[128,128]{1,0:T(8,128)S(1)} %get-tuple-element.31.pressure, f32[384,128]{1,0:T(8,128)S(1)} %get-tuple-element.32.base), custom_call_target="tpu_custom_call" | custom-call | flops 268435456 | bytes 3145728 | tf_op jit(solution)/shard_map/finish/pallas_call | solution.py:537
  (21 shorter events, 0.1 us)
Async XLA Ops:
  0.6 11.4 %copy-start.3 = (f32[4,8,16,128]{3,2,1,0:T(8,128)S(1)}, f32[4,8,16,128]{3,2,1,0:T(8,128)}, u32[]{:S(2)}) copy-start(f32[4,8,16,128]{3,2,1,0:T(8,128)} %wave.1) | copy-start | bytes 786436
  0.6 11.4 %copy-start.1 = (f32[4,16,32,128]{3,2,1,0:T(8,128)S(1)}, f32[4,16,32,128]{3,2,1,0:T(8,128)}, u32[]{:S(2)}) copy-start(f32[4,16,32,128]{3,2,1,0:T(8,128)} %rest.1) | copy-start | bytes 3145732
  0.7 11.4 %copy-start.2 = (f32[16,32,128]{2,1,0:T(8,128)S(1)}, f32[16,32,128]{2,1,0:T(8,128)}, u32[]{:S(2)}) copy-start(f32[16,32,128]{2,1,0:T(8,128)} %rho.1) | copy-start | bytes 786436
  2.0 18.0 %collective-permute-start = (f32[104,128]{1,0:T(8,128)S(1)}, f32[104,128]{1,0:T(8,128)S(1)}, u32[]{:S(2)}, u32[]{:S(2)}) collective-permute-start(f32[104,128]{1,0:T(8,128)S(1)} %get-tuple-element.19), channel_id=1, source_target_pairs={{1,2},{2,1},{3,4},{4,3},{5,6},{6,5},{7,8},{8,7},{9,10},{10,9},{11,... | collective-permute-start | bytes 159752 | tf_op jit(solution)/shard_map/ppermute | solution.py:438
  2.7 17.3 %collective-permute-start.1 = (f32[104,128]{1,0:T(8,128)S(1)}, f32[104,128]{1,0:T(8,128)S(1)}, u32[]{:S(2)}, u32[]{:S(2)}) collective-permute-start(f32[104,128]{1,0:T(8,128)S(1)} %get-tuple-element.20.after), channel_id=1, source_target_pairs={{0,1},{1,0},{2,3},{3,2},{4,5},{5,4},{6,7},{7,6},{8,9},{9,8},{10,11... | collective-permute-start | bytes 159752 | tf_op jit(solution)/shard_map/ppermute | solution.py:438
  12.1 6.9 %copy-start.6 = (s32[512,1]{0,1:T(1,128)S(1)}, s32[512,1]{0,1:T(1,128)}, u32[]{:S(2)}) copy-start(s32[512,1]{0,1:T(1,128)} %param.13) | copy-start | bytes 6148
  12.1 6.9 %copy-start.7 = (s32[512]{0:T(512)S(1)}, s32[512]{0:T(512)}, u32[]{:S(2)}) copy-start(s32[512]{0:T(512)} %param.15) | copy-start | bytes 6148
  12.1 6.9 %copy-start.8 = (s32[512]{0:T(512)S(1)}, s32[512]{0:T(512)}, u32[]{:S(2)}) copy-start(s32[512]{0:T(512)} %param.16) | copy-start | bytes 6148
  12.1 7.9 %copy-start.4 = (f32[128,128]{1,0:T(8,128)S(1)}, f32[128,128]{1,0:T(8,128)}, u32[]{:S(2)}) copy-start(f32[128,128]{1,0:T(8,128)} %far.3) | copy-start | bytes 196612
  12.1 7.9 %copy-start.5 = (s32[128]{0:T(128)S(1)}, s32[128]{0:T(128)}, u32[]{:S(2)}) copy-start(s32[128]{0:T(128)} %param.18) | copy-start | bytes 1540
  12.1 9.3 %copy-start = (bf16[512,64,128]{2,1,0:T(8,128)(2,1)S(1)}, bf16[512,64,128]{2,1,0:T(8,128)(2,1)}, u32[]{:S(2)}) copy-start(bf16[512,64,128]{2,1,0:T(8,128)(2,1)} %param.14) | copy-start | bytes 25165828
  12.6 7.4 %collective-permute-start.4 = (f32[100,128]{1,0:T(8,128)S(1)}, f32[100,128]{1,0:T(8,128)S(1)}, u32[]{:S(2)}, u32[]{:S(2)}) collective-permute-start(f32[100,128]{1,0:T(8,128)S(1)} %get-tuple-element.23), channel_id=1, source_target_pairs={{0,128},{128,0},{1,129},{129,1},{2,130},{130,2},{3,131},{131,3},{4... | collective-permute-start | bytes 153608 | tf_op jit(solution)/shard_map/ppermute | solution.py:438
  13.4 6.5 %collective-permute-start.2 = (f32[96,128]{1,0:T(8,128)S(1)}, f32[96,128]{1,0:T(8,128)S(1)}, u32[]{:S(2)}, u32[]{:S(2)}) collective-permute-start(f32[96,128]{1,0:T(8,128)S(1)} %get-tuple-element.21), channel_id=1, source_target_pairs={{16,32},{32,16},{48,64},{64,48},{80,96},{96,80},{17,33},{33,17},{4... | collective-permute-start | bytes 147464 | tf_op jit(solution)/shard_map/ppermute | solution.py:438
  18.2 1.8 %collective-permute-start.3 = (f32[96,128]{1,0:T(8,128)S(1)}, f32[96,128]{1,0:T(8,128)S(1)}, u32[]{:S(2)}, u32[]{:S(2)}) collective-permute-start(f32[96,128]{1,0:T(8,128)S(1)} %get-tuple-element.22), channel_id=1, source_target_pairs={{0,16},{16,0},{32,48},{48,32},{64,80},{80,64},{96,112},{112,96},{1... | collective-permute-start | bytes 147464 | tf_op jit(solution)/shard_map/ppermute | solution.py:438
  20.7 3.1 %collective-permute-start.5 = (f32[8,128]{1,0:T(8,128)S(1)}, f32[8,128]{1,0:T(8,128)S(1)}, u32[]{:S(2)}, u32[]{:S(2)}) collective-permute-start(f32[8,128]{1,0:T(8,128)S(1)} %get-tuple-element.27.share), channel_id=1, source_target_pairs={{0,128},{128,0},{1,129},{129,1},{2,130},{130,2},{3,131},{131,3},{4... | collective-permute-start | bytes 12296 | tf_op jit(solution)/shard_map/ppermute | solution.py:438
  25.5 42.9 %all-to-all-start = ((f32[128,1,2176]{2,1,0:T(1,128)}), f32[128,1,2176]{2,1,0:T(1,128)S(1)}, u32[]{:S(2)}, u32[]{:S(2)}) async-start(f32[128,1,2176]{2,1,0:T(1,128)} %bitcast.10), calls=%async_computation | async-start | bytes 2228224 | tf_op jit(solution)/shard_map/all_to_all | solution.py:523
  35.9 6.8 %collective-permute-start.6 = (f32[192,128]{1,0:T(8,128)S(1)}, f32[192,128]{1,0:T(8,128)S(1)}, u32[]{:S(2)}, u32[]{:S(2)}) collective-permute-start(f32[192,128]{1,0:T(8,128)S(1)} %get-tuple-element.28), channel_id=1, source_target_pairs={{16,32},{32,16},{48,64},{64,48},{80,96},{96,80},{17,33},{33,17},{4... | collective-permute-start | bytes 294920 | tf_op jit(solution)/shard_map/ppermute | solution.py:438
  39.5 3.2 %collective-permute-start.7 = (f32[192,128]{1,0:T(8,128)S(1)}, f32[192,128]{1,0:T(8,128)S(1)}, u32[]{:S(2)}, u32[]{:S(2)}) collective-permute-start(f32[192,128]{1,0:T(8,128)S(1)} %get-tuple-element.29), channel_id=1, source_target_pairs={{0,16},{16,0},{32,48},{48,32},{64,80},{80,64},{96,112},{112,96},{1... | collective-permute-start | bytes 294920 | tf_op jit(solution)/shard_map/ppermute | solution.py:438
